TPU v7x, 512 devices: a whole 4x4x16 slice. The times are simulated.
512 devices in a mesh: stream: 32 (over z, x_hi), span: 16 (over y, x_lo, core).
Axes of the slice: x: 4 (x_hi: 2, x_lo: 2; x = x_hi * 2 + x_lo), y: 4, z: 16, core: 2. Of those that a mesh axis runs over, the one named last changes fastest.
Arguments:
- checkpoint: float32 [19, 128, 128, 128], P(None, 'stream', 'span'), may hold values from 0.5 to 1.5
- porosity: float32 [128, 128, 128], P('stream', 'span'), may hold values from 0 to 1
- deposit_weight: float32 [128, 128, 128], P('stream', 'span'), may hold values from -24 to 24
- solid_mask: int32 [128, 128, 128], P('stream', 'span'), may hold values 0 or 1
- surface_mask: int32 [128, 128, 128], P('stream', 'span'), may hold values 0 or 1
Outputs:
- adjoint_state: float32 [19, 128, 128, 128], P(None, 'stream', 'span')
- shape_sensitivity: float32 [128, 128, 128], P('stream', 'span')
All inputs are finite; a program needn't handle non-finite values. No bound on the sum of `solid_mask` or of `surface_mask` on one device may be relied on, other than what follows from the above.
Results may differ from a plain program's by a relative error of at most 0.0003.
Values sent between devices are 32-bit elements; how exact they have to be, the bound alone decides.
No kernel may reach another device: no remote copies, remote signals or barrier semaphores. Data moves between devices by JAX's collectives and lax.ppermute only.
A program may use at most 64 MiB of HBM per device.

v0:
```python
import jax
import jax.numpy as jnp
import numpy as np
from jax import lax
from jax.sharding import PartitionSpec as P

ITERS = 2


VELOCITY = np.array(
    [
        [0, 0, 0],
        [1, 0, 0],
        [-1, 0, 0],
        [0, 1, 0],
        [0, -1, 0],
        [0, 0, 1],
        [0, 0, -1],
        [1, 1, 0],
        [-1, -1, 0],
        [1, -1, 0],
        [-1, 1, 0],
        [1, 0, 1],
        [-1, 0, -1],
        [1, 0, -1],
        [-1, 0, 1],
        [0, 1, 1],
        [0, -1, -1],
        [0, 1, -1],
        [0, -1, 1],
    ]
)
WEIGHTS = np.array([1.0 / 3.0] + [1.0 / 18.0] * 6 + [1.0 / 36.0] * 12)
RELAX_RATE = 0.9
GHOST_DENSITY = 18.0
INFLOW_SPEED = 0.08
GHOST_STATE = (
    WEIGHTS
    * GHOST_DENSITY
    * (
        1.0
        + 3.0 * VELOCITY[:, 0] * INFLOW_SPEED
        + 4.5 * (VELOCITY[:, 0] * INFLOW_SPEED) ** 2
        - 1.5 * INFLOW_SPEED**2
    )
)


def extended_2(block, sides, width):
    for axis, dim in sides:
        count = lax.axis_size(axis)
        forward = [(i, i + 1) for i in range(count - 1)]
        forward.append((count - 1, 0))
        backward = [(target, source) for source, target in forward]
        low = lax.ppermute(
            lax.slice_in_dim(block, block.shape[dim] - width, None, axis=dim), axis, forward
        )
        high = lax.ppermute(lax.slice_in_dim(block, 0, width, axis=dim), axis, backward)
        block = jnp.concatenate([low, block, high], axis=dim)
    return block


def moments(field):
    velocity = jnp.asarray(VELOCITY, field.dtype)
    density = jnp.sum(field, axis=0)
    momentum = jnp.tensordot(velocity.T, field, axes=1, precision=lax.Precision.HIGHEST)
    return (density, momentum)


def collide(field, blend):
    velocity = jnp.asarray(VELOCITY, field.dtype)
    density, momentum = moments(field)
    speed = momentum / density
    along = jnp.tensordot(velocity, speed, axes=1, precision=lax.Precision.HIGHEST)
    square = jnp.sum(speed * speed, axis=0)
    weights = jnp.asarray(WEIGHTS, field.dtype).reshape(19, 1, 1, 1)
    equil = weights * density * (1.0 + 3.0 * along + 4.5 * along * along - 1.5 * square)
    relaxed = field - RELAX_RATE * (field - equil)
    tail = field[1:].reshape((9, 2) + field.shape[1:])[:, ::-1].reshape((18,) + field.shape[1:])
    bounced = jnp.concatenate([field[:1], tail], axis=0)
    return relaxed + blend * (bounced - relaxed)


def pull(extended, sign, outside):
    count, width, height, depth = extended.shape
    zplane = jnp.broadcast_to(outside.reshape(count, 1, 1, 1), (count, width, height, 1))
    padded = jnp.concatenate([zplane, extended, zplane], axis=3)
    sizex, sizey, sizez = (width - 2, height - 2, depth)
    pieces = []
    for popul in range(19):
        offx = 1 - sign * int(VELOCITY[popul, 0])
        offy = 1 - sign * int(VELOCITY[popul, 1])
        offz = 1 - sign * int(VELOCITY[popul, 2])
        pieces.append(padded[popul, offx : offx + sizex, offy : offy + sizey, offz : offz + sizez])
    return jnp.stack(pieces, axis=0)


def fill_ends(extended, outside):
    count = lax.axis_size("stream")
    place = lax.axis_index("stream")
    width = extended.shape[1]
    rows = lax.broadcasted_iota(jnp.int32, (1, width, 1, 1), 1)
    edge = (rows == 0) & (place == 0) | (rows == width - 1) & (place == count - 1)
    return jnp.where(edge, outside.reshape(19, 1, 1, 1), extended)


def extend(field, outside):
    extended = extended_2(field, (("stream", 1), ("span", 2)), 1)
    return fill_ends(extended, outside)


def measure_of(field, deposit_weight):
    density, momentum = moments(field)
    return jnp.sum(deposit_weight * jnp.sum(momentum * momentum, axis=0) / (2.0 * density))


def shards(checkpoint, porosity, deposit_weight, solid_mask, surface_mask):
    blend = jnp.where(
        solid_mask == 1,
        jnp.ones_like(porosity),
        jnp.where(surface_mask == 1, porosity, jnp.zeros_like(porosity)),
    )
    design = (solid_mask == 0) & (surface_mask == 1)
    ghost = jnp.asarray(GHOST_STATE, jnp.float32)
    nothing = jnp.zeros((19,), jnp.float32)
    states = []
    field = checkpoint
    for repeat in range(ITERS):
        states.append(field)
        field = pull(extend(collide(field, blend), ghost), 1, ghost)
    adjoint = jax.grad(measure_of)(field, deposit_weight)
    sensitivity = jnp.zeros_like(porosity)
    for repeat in range(ITERS - 1, -1, -1):
        after_collide = pull(extend(adjoint, nothing), -1, nothing)
        value, backward = jax.vjp(collide, states[repeat], blend)
        adjoint, blend_part = backward(after_collide)
        sensitivity = sensitivity + blend_part
    shape_sensitivity = jnp.where(design, sensitivity, jnp.zeros_like(sensitivity))
    return (adjoint, shape_sensitivity)


def solution(mesh):
    placed = (
        P(None, "stream", "span", None),
        P("stream", "span", None),
        P("stream", "span", None),
        P("stream", "span", None),
        P("stream", "span", None),
    )
    return jax.shard_map(
        shards,
        mesh=mesh,
        in_specs=placed,
        out_specs=(P(None, "stream", "span", None), P("stream", "span", None)),
        check_vma=False,
    )
```

profile of v0, /device:TPU:27, one launch (start us, length us, event | category | flops | bytes accessed | tf_op | source)
XLA Modules:
  0.0 108.6 jit_solution(4051091569592651908)
XLA Ops:
  0.7 0.8 slice.329
  1.5 1.0 reduce_sum.334
  2.5 0.5 multiply_reduce_fusion.6
  3.0 0.5 fusion.67
  3.7 0.2 multiply_add_fusion.1
  3.9 3.8 %collective-permute-start = (f32[19,1,8,128]{3,2,1,0:T(8,128)S(1)}, f32[19,1,8,128]{3,2,1,0:T(8,128)S(1)}, u32[]{:S(2)}, u32[]{:S(2)}) collective-permute-start(f32[19,1,8,128]{3,2,1,0:T(8,128)S(1)} %get-tuple-element.56), channel_id=1, source_target_pairs={{0,16},{16,32},{32,48},{48,64},{64,80},{80,96},{96,112},{112,128},... | collective-permute-start | bytes 233480 | tf_op jit(solution)/shard_map/ppermute | solution.py:55
  7.7 10.9 %collective-permute-start.1 = (f32[19,1,8,128]{3,2,1,0:T(8,128)S(1)}, f32[19,1,8,128]{3,2,1,0:T(8,128)S(1)}, u32[]{:S(2)}, u32[]{:S(2)}) collective-permute-start(f32[19,1,8,128]{3,2,1,0:T(8,128)S(1)} %get-tuple-element.57), channel_id=1, source_target_pairs={{16,0},{32,16},{48,32},{64,48},{80,64},{96,80},{112,96},{128,112},... | collective-permute-start | bytes 233480 | tf_op jit(solution)/shard_map/ppermute | solution.py:58
  18.5 1.4 %collective-permute-done.1 = f32[19,1,8,128]{3,2,1,0:T(8,128)S(1)} collective-permute-done((f32[19,1,8,128]{3,2,1,0:T(8,128)S(1)}, f32[19,1,8,128]{3,2,1,0:T(8,128)S(1)}, u32[]{:S(2)}, u32[]{:S(2)}) %collective-permute-start.1) | collective-permute-done | bytes 77856 | tf_op jit(solution)/shard_map/ppermute | solution.py:58
  20.0 4.1 %collective-permute-start.2 = (f32[19,6,1,128]{3,2,1,0:T(1,128)S(1)}, f32[19,6,1,128]{3,2,1,0:T(1,128)S(1)}, u32[]{:S(2)}, u32[]{:S(2)}) collective-permute-start(f32[19,6,1,128]{3,2,1,0:T(1,128)S(1)} %get-tuple-element.46), channel_id=1, source_target_pairs={{0,1},{1,2},{2,3},{3,4},{4,5},{5,6},{6,7},{7,8},{8,9},{9,10},{10,1... | collective-permute-start | bytes 175112 | tf_op jit(solution)/shard_map/ppermute | solution.py:55
  24.1 1.9 %collective-permute-start.3 = (f32[19,6,1,128]{3,2,1,0:T(1,128)S(1)}, f32[19,6,1,128]{3,2,1,0:T(1,128)S(1)}, u32[]{:S(2)}, u32[]{:S(2)}) collective-permute-start(f32[19,6,1,128]{3,2,1,0:T(1,128)S(1)} %get-tuple-element.47), channel_id=1, source_target_pairs={{1,0},{2,1},{3,2},{4,3},{5,4},{6,5},{7,6},{8,7},{9,8},{10,9},{11,1... | collective-permute-start | bytes 175112 | tf_op jit(solution)/shard_map/ppermute | solution.py:58
  26.1 5.7 %collective-permute-done.3 = f32[19,6,1,128]{3,2,1,0:T(1,128)S(1)} collective-permute-done((f32[19,6,1,128]{3,2,1,0:T(1,128)S(1)}, f32[19,6,1,128]{3,2,1,0:T(1,128)S(1)}, u32[]{:S(2)}, u32[]{:S(2)}) %collective-permute-start.3) | collective-permute-done | bytes 58400 | tf_op jit(solution)/shard_map/ppermute | solution.py:58
  31.8 0.2 maximum_select_fusion
  33.5 0.6 multiply_reduce_fusion.4
  34.1 0.6 fusion.42
  34.7 0.2 multiply_add_fusion
  34.9 1.9 %collective-permute-start.4 = (f32[19,1,8,128]{3,2,1,0:T(8,128)S(1)}, f32[19,1,8,128]{3,2,1,0:T(8,128)S(1)}, u32[]{:S(2)}, u32[]{:S(2)}) collective-permute-start(f32[19,1,8,128]{3,2,1,0:T(8,128)S(1)} %get-tuple-element.54), channel_id=1, source_target_pairs={{0,16},{16,32},{32,48},{48,64},{64,80},{80,96},{96,112},{112,128},... | collective-permute-start | bytes 233480 | tf_op jit(solution)/shard_map/ppermute | solution.py:55
  36.8 7.0 %collective-permute-start.5 = (f32[19,1,8,128]{3,2,1,0:T(8,128)S(1)}, f32[19,1,8,128]{3,2,1,0:T(8,128)S(1)}, u32[]{:S(2)}, u32[]{:S(2)}) collective-permute-start(f32[19,1,8,128]{3,2,1,0:T(8,128)S(1)} %get-tuple-element.55), channel_id=1, source_target_pairs={{16,0},{32,16},{48,32},{64,48},{80,64},{96,80},{112,96},{128,112},... | collective-permute-start | bytes 233480 | tf_op jit(solution)/shard_map/ppermute | solution.py:58
  43.8 1.4 %collective-permute-done.5 = f32[19,1,8,128]{3,2,1,0:T(8,128)S(1)} collective-permute-done((f32[19,1,8,128]{3,2,1,0:T(8,128)S(1)}, f32[19,1,8,128]{3,2,1,0:T(8,128)S(1)}, u32[]{:S(2)}, u32[]{:S(2)}) %collective-permute-start.5) | collective-permute-done | bytes 77856 | tf_op jit(solution)/shard_map/ppermute | solution.py:58
  45.3 3.3 %collective-permute-start.6 = (f32[19,6,1,128]{3,2,1,0:T(1,128)S(1)}, f32[19,6,1,128]{3,2,1,0:T(1,128)S(1)}, u32[]{:S(2)}, u32[]{:S(2)}) collective-permute-start(f32[19,6,1,128]{3,2,1,0:T(1,128)S(1)} %get-tuple-element.44), channel_id=1, source_target_pairs={{0,1},{1,2},{2,3},{3,4},{4,5},{5,6},{6,7},{7,8},{8,9},{9,10},{10,1... | collective-permute-start | bytes 175112 | tf_op jit(solution)/shard_map/ppermute | solution.py:55
  48.7 1.9 %collective-permute-start.7 = (f32[19,6,1,128]{3,2,1,0:T(1,128)S(1)}, f32[19,6,1,128]{3,2,1,0:T(1,128)S(1)}, u32[]{:S(2)}, u32[]{:S(2)}) collective-permute-start(f32[19,6,1,128]{3,2,1,0:T(1,128)S(1)} %get-tuple-element.45), channel_id=1, source_target_pairs={{1,0},{2,1},{3,2},{4,3},{5,4},{6,5},{7,6},{8,7},{9,8},{10,9},{11,1... | collective-permute-start | bytes 175112 | tf_op jit(solution)/shard_map/ppermute | solution.py:58
  50.6 5.7 %collective-permute-done.7 = f32[19,6,1,128]{3,2,1,0:T(1,128)S(1)} collective-permute-done((f32[19,6,1,128]{3,2,1,0:T(1,128)S(1)}, f32[19,6,1,128]{3,2,1,0:T(1,128)S(1)}, u32[]{:S(2)}, u32[]{:S(2)}) %collective-permute-start.7) | collective-permute-done | bytes 58400 | tf_op jit(solution)/shard_map/ppermute | solution.py:58
  56.3 0.2 maximum_select_fusion.1
  57.4 0.6 multiply_reduce_fusion.5
  58.2 0.5 fusion.40
  58.8 1.9 %collective-permute-start.8 = (f32[19,1,8,128]{3,2,1,0:T(8,128)S(1)}, f32[19,1,8,128]{3,2,1,0:T(8,128)S(1)}, u32[]{:S(2)}, u32[]{:S(2)}) collective-permute-start(f32[19,1,8,128]{3,2,1,0:T(8,128)S(1)} %get-tuple-element.52), channel_id=1, source_target_pairs={{0,16},{16,32},{32,48},{48,64},{64,80},{80,96},{96,112},{112,128},... | collective-permute-start | bytes 233480 | tf_op jit(solution)/shard_map/ppermute | solution.py:55
  60.7 7.0 %collective-permute-start.9 = (f32[19,1,8,128]{3,2,1,0:T(8,128)S(1)}, f32[19,1,8,128]{3,2,1,0:T(8,128)S(1)}, u32[]{:S(2)}, u32[]{:S(2)}) collective-permute-start(f32[19,1,8,128]{3,2,1,0:T(8,128)S(1)} %get-tuple-element.53), channel_id=1, source_target_pairs={{16,0},{32,16},{48,32},{64,48},{80,64},{96,80},{112,96},{128,112},... | collective-permute-start | bytes 233480 | tf_op jit(solution)/shard_map/ppermute | solution.py:58
  67.7 0.6 fusion.68
  68.3 0.9 collective-permute-done.9
  69.2 3.3 %collective-permute-start.10 = (f32[19,6,1,128]{3,2,1,0:T(1,128)S(1)}, f32[19,6,1,128]{3,2,1,0:T(1,128)S(1)}, u32[]{:S(2)}, u32[]{:S(2)}) collective-permute-start(f32[19,6,1,128]{3,2,1,0:T(1,128)S(1)} %get-tuple-element.42), channel_id=1, source_target_pairs={{0,1},{1,2},{2,3},{3,4},{4,5},{5,6},{6,7},{7,8},{8,9},{9,10},{10,1... | collective-permute-start | bytes 175112 | tf_op jit(solution)/shard_map/ppermute | solution.py:55
  72.6 1.9 %collective-permute-start.11 = (f32[19,6,1,128]{3,2,1,0:T(1,128)S(1)}, f32[19,6,1,128]{3,2,1,0:T(1,128)S(1)}, u32[]{:S(2)}, u32[]{:S(2)}) collective-permute-start(f32[19,6,1,128]{3,2,1,0:T(1,128)S(1)} %get-tuple-element.43), channel_id=1, source_target_pairs={{1,0},{2,1},{3,2},{4,3},{5,4},{6,5},{7,6},{8,7},{9,8},{10,9},{11,1... | collective-permute-start | bytes 175112 | tf_op jit(solution)/shard_map/ppermute | solution.py:58
  74.5 5.7 %collective-permute-done.11 = f32[19,6,1,128]{3,2,1,0:T(1,128)S(1)} collective-permute-done((f32[19,6,1,128]{3,2,1,0:T(1,128)S(1)}, f32[19,6,1,128]{3,2,1,0:T(1,128)S(1)}, u32[]{:S(2)}, u32[]{:S(2)}) %collective-permute-start.11) | collective-permute-done | bytes 58400 | tf_op jit(solution)/shard_map/ppermute | solution.py:58
  80.2 0.2 maximum_select_fusion.2
  81.3 0.3 fusion.29
  81.7 0.5 fusion.39
  82.3 0.6 fusion.37
  82.8 0.2 fusion.31
  83.1 1.9 %collective-permute-start.12 = (f32[19,1,8,128]{3,2,1,0:T(8,128)S(1)}, f32[19,1,8,128]{3,2,1,0:T(8,128)S(1)}, u32[]{:S(2)}, u32[]{:S(2)}) collective-permute-start(f32[19,1,8,128]{3,2,1,0:T(8,128)S(1)} %get-tuple-element.50), channel_id=1, source_target_pairs={{0,16},{16,32},{32,48},{48,64},{64,80},{80,96},{96,112},{112,128},... | collective-permute-start | bytes 233480 | tf_op jit(solution)/shard_map/ppermute | solution.py:55
  85.0 7.0 %collective-permute-start.13 = (f32[19,1,8,128]{3,2,1,0:T(8,128)S(1)}, f32[19,1,8,128]{3,2,1,0:T(8,128)S(1)}, u32[]{:S(2)}, u32[]{:S(2)}) collective-permute-start(f32[19,1,8,128]{3,2,1,0:T(8,128)S(1)} %get-tuple-element.51), channel_id=1, source_target_pairs={{16,0},{32,16},{48,32},{64,48},{80,64},{96,80},{112,96},{128,112},... | collective-permute-start | bytes 233480 | tf_op jit(solution)/shard_map/ppermute | solution.py:58
  92.0 1.4 %collective-permute-done.13 = f32[19,1,8,128]{3,2,1,0:T(8,128)S(1)} collective-permute-done((f32[19,1,8,128]{3,2,1,0:T(8,128)S(1)}, f32[19,1,8,128]{3,2,1,0:T(8,128)S(1)}, u32[]{:S(2)}, u32[]{:S(2)}) %collective-permute-start.13) | collective-permute-done | bytes 77856 | tf_op jit(solution)/shard_map/ppermute | solution.py:58
  93.5 3.3 %collective-permute-start.14 = (f32[19,6,1,128]{3,2,1,0:T(1,128)S(1)}, f32[19,6,1,128]{3,2,1,0:T(1,128)S(1)}, u32[]{:S(2)}, u32[]{:S(2)}) collective-permute-start(f32[19,6,1,128]{3,2,1,0:T(1,128)S(1)} %get-tuple-element.40), channel_id=1, source_target_pairs={{0,1},{1,2},{2,3},{3,4},{4,5},{5,6},{6,7},{7,8},{8,9},{9,10},{10,1... | collective-permute-start | bytes 175112 | tf_op jit(solution)/shard_map/ppermute | solution.py:55
  96.8 1.9 %collective-permute-start.15 = (f32[19,6,1,128]{3,2,1,0:T(1,128)S(1)}, f32[19,6,1,128]{3,2,1,0:T(1,128)S(1)}, u32[]{:S(2)}, u32[]{:S(2)}) collective-permute-start(f32[19,6,1,128]{3,2,1,0:T(1,128)S(1)} %get-tuple-element.41), channel_id=1, source_target_pairs={{1,0},{2,1},{3,2},{4,3},{5,4},{6,5},{7,6},{8,7},{9,8},{10,9},{11,1... | collective-permute-start | bytes 175112 | tf_op jit(solution)/shard_map/ppermute | solution.py:58
  98.8 5.7 %collective-permute-done.15 = f32[19,6,1,128]{3,2,1,0:T(1,128)S(1)} collective-permute-done((f32[19,6,1,128]{3,2,1,0:T(1,128)S(1)}, f32[19,6,1,128]{3,2,1,0:T(1,128)S(1)}, u32[]{:S(2)}, u32[]{:S(2)}) %collective-permute-start.15) | collective-permute-done | bytes 58400 | tf_op jit(solution)/shard_map/ppermute | solution.py:58
  104.5 0.2 maximum_select_fusion.3
  105.6 0.3 multiply_reduce_fusion
  106.0 0.5 multiply_reduce_fusion.3
  106.5 0.6 fusion.35
  107.1 0.6 add_select_fusion
  107.7 0.9 fusion.30
  (142 shorter events, 4.7 us)
Async XLA Ops:
  0.6 1.9 %copy-start.1 = (f32[19,3,1,1]{0,1,3,2:T(4,128)S(1)}, f32[19,3,1,1]{0,1,3,2:T(4,128)}, u32[]{:S(2)}) copy-start(f32[19,3,1,1]{0,1,3,2:T(4,128)} %constant.64) | copy-start | bytes 688
  0.6 1.8 %copy-start = (f32[19,4,8,128]{3,2,1,0:T(8,128)S(1)}, f32[19,4,8,128]{3,2,1,0:T(8,128)}, u32[]{:S(2)}) copy-start(f32[19,4,8,128]{3,2,1,0:T(8,128)} %param.19) | copy-start | bytes 933892
  0.7 2.9 %slice-start = ((f32[19,4,8,128]{3,2,1,0:T(8,128)}), f32[18,4,8,128]{3,2,1,0:T(8,128)S(1)}, s32[]{:S(2)}) async-start(f32[19,4,8,128]{3,2,1,0:T(8,128)} %param.19), calls=%async_computation | async-start | bytes 589824 | tf_op jit(solution)/shard_map/slice | solution.py:79
  1.4 2.2 %copy-start.3 = (s32[4,8,128]{2,1,0:T(8,128)S(1)}, s32[4,8,128]{2,1,0:T(8,128)}, u32[]{:S(2)}) copy-start(s32[4,8,128]{2,1,0:T(8,128)} %param.22) | copy-start | bytes 49156
  1.4 2.2 %copy-start.4 = (f32[4,8,128]{2,1,0:T(8,128)S(1)}, f32[4,8,128]{2,1,0:T(8,128)}, u32[]{:S(2)}) copy-start(f32[4,8,128]{2,1,0:T(8,128)} %param.20) | copy-start | bytes 49156
  1.4 2.2 %copy-start.5 = (s32[4,8,128]{2,1,0:T(8,128)S(1)}, s32[4,8,128]{2,1,0:T(8,128)}, u32[]{:S(2)}) copy-start(s32[4,8,128]{2,1,0:T(8,128)} %param.23) | copy-start | bytes 49156
  2.5 1.2 %copy-start.6 = (f32[19]{0:T(128)S(1)}, f32[19]{0:T(128)}, u32[]{:S(2)}) copy-start(f32[19]{0:T(128)} %constant.46.clone) | copy-start | bytes 232
  3.7 28.1 %copy-start.7 = (f32[19]{0:T(128)S(1)}, f32[19]{0:T(128)}, u32[]{:S(2)}) copy-start(f32[19]{0:T(128)} %constant.15.clone) | copy-start | bytes 232
  3.9 14.6 %collective-permute-start = (f32[19,1,8,128]{3,2,1,0:T(8,128)S(1)}, f32[19,1,8,128]{3,2,1,0:T(8,128)S(1)}, u32[]{:S(2)}, u32[]{:S(2)}) collective-permute-start(f32[19,1,8,128]{3,2,1,0:T(8,128)S(1)} %get-tuple-element.56), channel_id=1, source_target_pairs={{0,16},{16,32},{32,48},{48,64},{64,80},{80,96},{96,112},{112,128},... | collective-permute-start | bytes 233480 | tf_op jit(solution)/shard_map/ppermute | solution.py:55
  7.7 12.3 %collective-permute-start.1 = (f32[19,1,8,128]{3,2,1,0:T(8,128)S(1)}, f32[19,1,8,128]{3,2,1,0:T(8,128)S(1)}, u32[]{:S(2)}, u32[]{:S(2)}) collective-permute-start(f32[19,1,8,128]{3,2,1,0:T(8,128)S(1)} %get-tuple-element.57), channel_id=1, source_target_pairs={{16,0},{32,16},{48,32},{64,48},{80,64},{96,80},{112,96},{128,112},... | collective-permute-start | bytes 233480 | tf_op jit(solution)/shard_map/ppermute | solution.py:58
  20.0 6.1 %collective-permute-start.2 = (f32[19,6,1,128]{3,2,1,0:T(1,128)S(1)}, f32[19,6,1,128]{3,2,1,0:T(1,128)S(1)}, u32[]{:S(2)}, u32[]{:S(2)}) collective-permute-start(f32[19,6,1,128]{3,2,1,0:T(1,128)S(1)} %get-tuple-element.46), channel_id=1, source_target_pairs={{0,1},{1,2},{2,3},{3,4},{4,5},{5,6},{6,7},{7,8},{8,9},{9,10},{10,1... | collective-permute-start | bytes 175112 | tf_op jit(solution)/shard_map/ppermute | solution.py:55
  24.1 7.6 %collective-permute-start.3 = (f32[19,6,1,128]{3,2,1,0:T(1,128)S(1)}, f32[19,6,1,128]{3,2,1,0:T(1,128)S(1)}, u32[]{:S(2)}, u32[]{:S(2)}) collective-permute-start(f32[19,6,1,128]{3,2,1,0:T(1,128)S(1)} %get-tuple-element.47), channel_id=1, source_target_pairs={{1,0},{2,1},{3,2},{4,3},{5,4},{6,5},{7,6},{8,7},{9,8},{10,9},{11,1... | collective-permute-start | bytes 175112 | tf_op jit(solution)/shard_map/ppermute | solution.py:58
  34.9 9.0 %collective-permute-start.4 = (f32[19,1,8,128]{3,2,1,0:T(8,128)S(1)}, f32[19,1,8,128]{3,2,1,0:T(8,128)S(1)}, u32[]{:S(2)}, u32[]{:S(2)}) collective-permute-start(f32[19,1,8,128]{3,2,1,0:T(8,128)S(1)} %get-tuple-element.54), channel_id=1, source_target_pairs={{0,16},{16,32},{32,48},{48,64},{64,80},{80,96},{96,112},{112,128},... | collective-permute-start | bytes 233480 | tf_op jit(solution)/shard_map/ppermute | solution.py:55
  36.8 8.4 %collective-permute-start.5 = (f32[19,1,8,128]{3,2,1,0:T(8,128)S(1)}, f32[19,1,8,128]{3,2,1,0:T(8,128)S(1)}, u32[]{:S(2)}, u32[]{:S(2)}) collective-permute-start(f32[19,1,8,128]{3,2,1,0:T(8,128)S(1)} %get-tuple-element.55), channel_id=1, source_target_pairs={{16,0},{32,16},{48,32},{64,48},{80,64},{96,80},{112,96},{128,112},... | collective-permute-start | bytes 233480 | tf_op jit(solution)/shard_map/ppermute | solution.py:58
  45.3 5.3 %collective-permute-start.6 = (f32[19,6,1,128]{3,2,1,0:T(1,128)S(1)}, f32[19,6,1,128]{3,2,1,0:T(1,128)S(1)}, u32[]{:S(2)}, u32[]{:S(2)}) collective-permute-start(f32[19,6,1,128]{3,2,1,0:T(1,128)S(1)} %get-tuple-element.44), channel_id=1, source_target_pairs={{0,1},{1,2},{2,3},{3,4},{4,5},{5,6},{6,7},{7,8},{8,9},{9,10},{10,1... | collective-permute-start | bytes 175112 | tf_op jit(solution)/shard_map/ppermute | solution.py:55
  48.7 7.6 %collective-permute-start.7 = (f32[19,6,1,128]{3,2,1,0:T(1,128)S(1)}, f32[19,6,1,128]{3,2,1,0:T(1,128)S(1)}, u32[]{:S(2)}, u32[]{:S(2)}) collective-permute-start(f32[19,6,1,128]{3,2,1,0:T(1,128)S(1)} %get-tuple-element.45), channel_id=1, source_target_pairs={{1,0},{2,1},{3,2},{4,3},{5,4},{6,5},{7,6},{8,7},{9,8},{10,9},{11,1... | collective-permute-start | bytes 175112 | tf_op jit(solution)/shard_map/ppermute | solution.py:58
  57.3 0.7 copy-start.2
  58.8 9.5 %collective-permute-start.8 = (f32[19,1,8,128]{3,2,1,0:T(8,128)S(1)}, f32[19,1,8,128]{3,2,1,0:T(8,128)S(1)}, u32[]{:S(2)}, u32[]{:S(2)}) collective-permute-start(f32[19,1,8,128]{3,2,1,0:T(8,128)S(1)} %get-tuple-element.52), channel_id=1, source_target_pairs={{0,16},{16,32},{32,48},{48,64},{64,80},{80,96},{96,112},{112,128},... | collective-permute-start | bytes 233480 | tf_op jit(solution)/shard_map/ppermute | solution.py:55
  60.7 8.4 %collective-permute-start.9 = (f32[19,1,8,128]{3,2,1,0:T(8,128)S(1)}, f32[19,1,8,128]{3,2,1,0:T(8,128)S(1)}, u32[]{:S(2)}, u32[]{:S(2)}) collective-permute-start(f32[19,1,8,128]{3,2,1,0:T(8,128)S(1)} %get-tuple-element.53), channel_id=1, source_target_pairs={{16,0},{32,16},{48,32},{64,48},{80,64},{96,80},{112,96},{128,112},... | collective-permute-start | bytes 233480 | tf_op jit(solution)/shard_map/ppermute | solution.py:58
  69.2 5.3 %collective-permute-start.10 = (f32[19,6,1,128]{3,2,1,0:T(1,128)S(1)}, f32[19,6,1,128]{3,2,1,0:T(1,128)S(1)}, u32[]{:S(2)}, u32[]{:S(2)}) collective-permute-start(f32[19,6,1,128]{3,2,1,0:T(1,128)S(1)} %get-tuple-element.42), channel_id=1, source_target_pairs={{0,1},{1,2},{2,3},{3,4},{4,5},{5,6},{6,7},{7,8},{8,9},{9,10},{10,1... | collective-permute-start | bytes 175112 | tf_op jit(solution)/shard_map/ppermute | solution.py:55
  72.6 7.6 %collective-permute-start.11 = (f32[19,6,1,128]{3,2,1,0:T(1,128)S(1)}, f32[19,6,1,128]{3,2,1,0:T(1,128)S(1)}, u32[]{:S(2)}, u32[]{:S(2)}) collective-permute-start(f32[19,6,1,128]{3,2,1,0:T(1,128)S(1)} %get-tuple-element.43), channel_id=1, source_target_pairs={{1,0},{2,1},{3,2},{4,3},{5,4},{6,5},{7,6},{8,7},{9,8},{10,9},{11,1... | collective-permute-start | bytes 175112 | tf_op jit(solution)/shard_map/ppermute | solution.py:58
  81.7 1.1 %copy-start.8 = (pred[19]{0:T(512)(128)(4,1)S(1)}, pred[19]{0:T(512)(128)(4,1)}, u32[]{:S(2)}) copy-start(pred[19]{0:T(512)(128)(4,1)} %constant.17.clone.1) | copy-start | bytes 61
  83.1 8.9 %collective-permute-start.12 = (f32[19,1,8,128]{3,2,1,0:T(8,128)S(1)}, f32[19,1,8,128]{3,2,1,0:T(8,128)S(1)}, u32[]{:S(2)}, u32[]{:S(2)}) collective-permute-start(f32[19,1,8,128]{3,2,1,0:T(8,128)S(1)} %get-tuple-element.50), channel_id=1, source_target_pairs={{0,16},{16,32},{32,48},{48,64},{64,80},{80,96},{96,112},{112,128},... | collective-permute-start | bytes 233480 | tf_op jit(solution)/shard_map/ppermute | solution.py:55
  85.0 8.4 %collective-permute-start.13 = (f32[19,1,8,128]{3,2,1,0:T(8,128)S(1)}, f32[19,1,8,128]{3,2,1,0:T(8,128)S(1)}, u32[]{:S(2)}, u32[]{:S(2)}) collective-permute-start(f32[19,1,8,128]{3,2,1,0:T(8,128)S(1)} %get-tuple-element.51), channel_id=1, source_target_pairs={{16,0},{32,16},{48,32},{64,48},{80,64},{96,80},{112,96},{128,112},... | collective-permute-start | bytes 233480 | tf_op jit(solution)/shard_map/ppermute | solution.py:58
  93.5 5.3 %collective-permute-start.14 = (f32[19,6,1,128]{3,2,1,0:T(1,128)S(1)}, f32[19,6,1,128]{3,2,1,0:T(1,128)S(1)}, u32[]{:S(2)}, u32[]{:S(2)}) collective-permute-start(f32[19,6,1,128]{3,2,1,0:T(1,128)S(1)} %get-tuple-element.40), channel_id=1, source_target_pairs={{0,1},{1,2},{2,3},{3,4},{4,5},{5,6},{6,7},{7,8},{8,9},{9,10},{10,1... | collective-permute-start | bytes 175112 | tf_op jit(solution)/shard_map/ppermute | solution.py:55
  96.8 7.6 %collective-permute-start.15 = (f32[19,6,1,128]{3,2,1,0:T(1,128)S(1)}, f32[19,6,1,128]{3,2,1,0:T(1,128)S(1)}, u32[]{:S(2)}, u32[]{:S(2)}) collective-permute-start(f32[19,6,1,128]{3,2,1,0:T(1,128)S(1)} %get-tuple-element.41), channel_id=1, source_target_pairs={{1,0},{2,1},{3,2},{4,3},{5,4},{6,5},{7,6},{8,7},{9,8},{10,9},{11,1... | collective-permute-start | bytes 175112 | tf_op jit(solution)/shard_map/ppermute | solution.py:58
where the time goes:
time: 109 us
  starting transfers between devices  63.2 us (58%)
  waiting for transfers between devices  27.8 us (26%)
  other arithmetic  7.15 us (7%)
  matrix products  5.93 us (5%)
  local copies, waits for them, and re-layouts  2.91 us (3%)
  between operations  1.6 us (1%)
    ppermute x8, starting transfers between devices, extended_2(): lax.ppermute(lax.slice_in_dim(block, 0, width, axis=dim), axis, backward)  39.6 us
    ppermute x8, waiting for transfers between devices, extended_2(): lax.ppermute(lax.slice_in_dim(block, 0, width, axis=dim), axis, backward)  27.8 us
    ppermute x8, starting transfers between devices, extended_2(): lax.ppermute(lax.slice_in_dim(block, block.shape[dim] - width, None, axis...  23.7 us
    dot_general x6, matrix products, moments(): jnp.tensordot(velocity.T, field, axes=1, precision=lax.Precision.HIGHEST)  3.24 us
    dot_general x5, matrix products, collide(): jnp.tensordot(velocity, speed, axes=1, precision=lax.Precision.HIGHEST)  2.69 us
  transfers between devices with their start and end apart: 16, of which 8 were waited for; matrix products, arithmetic and copies ran while one was open for 1% of the time, Pallas kernels for 0%

commit v1 on v0

v1 whole, which is shorter than its diff:
```python
import functools

import jax
import jax.numpy as jnp
import numpy as np
from jax import lax
from jax.experimental import pallas as pl
from jax.experimental.pallas import tpu as pltpu
from jax.sharding import PartitionSpec as P

VELOCITY = np.array(
    [
        [0, 0, 0],
        [1, 0, 0],
        [-1, 0, 0],
        [0, 1, 0],
        [0, -1, 0],
        [0, 0, 1],
        [0, 0, -1],
        [1, 1, 0],
        [-1, -1, 0],
        [1, -1, 0],
        [-1, 1, 0],
        [1, 0, 1],
        [-1, 0, -1],
        [1, 0, -1],
        [-1, 0, 1],
        [0, 1, 1],
        [0, -1, -1],
        [0, 1, -1],
        [0, -1, 1],
    ]
)
WEIGHTS = np.array([1.0 / 3.0] + [1.0 / 18.0] * 6 + [1.0 / 36.0] * 12)
GHOST_DENSITY = 18.0
INFLOW_SPEED = 0.08
GHOST_STATE = (
    WEIGHTS
    * GHOST_DENSITY
    * (
        1.0
        + 3.0 * VELOCITY[:, 0] * INFLOW_SPEED
        + 4.5 * (VELOCITY[:, 0] * INFLOW_SPEED) ** 2
        - 1.5 * INFLOW_SPEED**2
    )
)
GHOST = [float(value) for value in GHOST_STATE]
VEL = [tuple(int(part) for part in row) for row in VELOCITY]
CX = [row[0] for row in VEL]
UP = [p for p in range(19) if CX[p] == 1]
DOWN = [p for p in range(19) if CX[p] == -1]
FLAT = [p for p in range(19) if CX[p] == 0]
BLEND, WEIGHT = 19, 20
NEAR, NEAR_FLAT, NEAR_BLEND, NEAR_WEIGHT = 0, 5, 14, 15
FAR, FAR_NEXT, FAR_PART, FAR_WEIGHT, LAYERS = 16, 21, 26, 30, 31


def sublane(tile):
    return lax.broadcasted_iota(jnp.int32, tile.shape, len(tile.shape) - 2)


def lane(tile):
    return lax.broadcasted_iota(jnp.int32, tile.shape, len(tile.shape) - 1)


def shift_z(tile, step, fill):
    if step == 0:
        return tile
    rolled = pltpu.roll(tile, step % 128, 1)
    return jnp.where(lane(tile) == (0 if step == 1 else 127), fill, rolled)


def shift_y(pair, step):
    if step == 0:
        return pair
    own, side = (pltpu.roll(tile, step % 8, 0) for tile in pair)
    edge = sublane(own) == (0 if step == 1 else 7)
    return (jnp.where(edge, side, own), jnp.where(edge, own, side))


def shift_pair(pair, stepy, stepz, fill):
    return tuple(shift_z(tile, stepz, fill) for tile in shift_y(pair, stepy))


def pairs_of(f):
    sums = [f[2 * i + 1] + f[2 * i + 2] for i in range(9)]
    diffs = [f[2 * i + 1] - f[2 * i + 2] for i in range(9)]
    return sums, diffs


def along_axes(v):
    return (
        v[0] + v[3] + v[4] + v[5] + v[6],
        v[1] + v[3] - v[4] + v[7] + v[8],
        v[2] + v[5] - v[6] + v[7] - v[8],
    )


def dots(u):
    x, y, z = u
    return [x, y, z, x + y, x - y, x + z, x - z, y + z, y - z]


def flow(f0, sums, diffs):
    density = f0 + sum(sums[1:], sums[0])
    inverse = 1.0 / density
    u = [m * inverse for m in along_axes(diffs)]
    square = u[0] * u[0] + u[1] * u[1] + u[2] * u[2]
    return density, u, square


def collide(f, b):
    sums, diffs = pairs_of(f)
    density, u, square = flow(f[0], sums, diffs)
    keep = 1.0 - b
    j = 0.1 * keep
    alpha, beta = 0.5 * (j + b), 0.5 * (j - b)
    scaled = (0.9 * keep) * density
    rest = scaled * (1.0 - 1.5 * square)
    flux = dots([scaled * part for part in u])
    out = [(j + b) * f[0] + (1.0 / 3.0) * rest]
    rest_axis, rest_diag = rest * (1.0 / 18.0), rest * (1.0 / 36.0)
    for i, along in enumerate(dots(u)):
        w = 1.0 / 18.0 if i < 3 else 1.0 / 36.0
        even = alpha * sums[i] + (rest_axis if i < 3 else rest_diag) + flux[i] * along * (4.5 * w)
        odd = beta * diffs[i] + flux[i] * (3.0 * w)
        out += [even + odd, even - odd]
    return out


def adjoint_collide(f, b, h, wanted, blend_part):
    fsums, fdiffs = pairs_of(f)
    density, u, square = flow(f[0], fsums, fdiffs)
    s, d = pairs_of(h)
    axis = (s[0] + s[1] + s[2]) * (1.0 / 18.0)
    h0 = h[0] * (1.0 / 3.0) + axis + sum(s[4:], s[3]) * (1.0 / 36.0)
    w = [1.0 / 18.0] * 3 + [1.0 / 36.0] * 6
    h1 = along_axes([d[i] * w[i] for i in range(9)])
    t = [s[i] * w[i] for i in range(9)]
    xx = t[0] + t[3] + t[4] + t[5] + t[6]
    yy = t[1] + t[3] + t[4] + t[7] + t[8]
    zz = t[2] + t[5] + t[6] + t[7] + t[8]
    xy, xz, yz = t[3] - t[4], t[5] - t[6], t[7] - t[8]
    v = (
        xx * u[0] + xy * u[1] + xz * u[2],
        xy * u[0] + yy * u[1] + yz * u[2],
        xz * u[0] + yz * u[1] + zz * u[2],
    )
    quad = u[0] * v[0] + u[1] * v[1] + u[2] * v[2]
    keep = 1.0 - b
    j, k = 0.1 * keep, 0.9 * keep
    alpha, beta = 0.5 * (j + b), 0.5 * (j - b)
    base = k * (h0 * (1.0 + 1.5 * square) - 4.5 * quad)
    push = dots([k * (3.0 * h1[i] + 9.0 * v[i] - 3.0 * u[i] * h0) for i in range(3)])
    out = {}
    if 0 in wanted:
        out[0] = (j + b) * h[0] + base
    for i in range(9):
        first, second = 2 * i + 1, 2 * i + 2
        if first in wanted or second in wanted:
            even = alpha * s[i] + base
            odd = beta * d[i] + push[i]
            if first in wanted:
                out[first] = even + odd
            if second in wanted:
                out[second] = even - odd
    part = None
    if blend_part:
        equil = h0 * (1.0 - 1.5 * square) + 4.5 * quad
        equil = equil + 3.0 * (u[0] * h1[0] + u[1] * h1[1] + u[2] * h1[2])
        evens = sum((s[i] * fsums[i] for i in range(1, 9)), s[0] * fsums[0])
        odds = sum((d[i] * fdiffs[i] for i in range(1, 9)), d[0] * fdiffs[0])
        part = 0.9 * h[0] * f[0] + 0.45 * evens - 0.55 * odds - 0.9 * density * equil
    return out, part


def moment_sums(values):
    density = functools.reduce(lambda a, b: a + b, values.values())
    momentum = []
    for k in range(3):
        total = None
        for p, value in values.items():
            if VEL[p][k] == 1:
                total = value if total is None else total + value
        for p, value in values.items():
            if VEL[p][k] == -1:
                total = -value if total is None else total - value
        momentum.append(total)
    return [density] + momentum


def start_kernel(f_ref, porosity_ref, weight_ref, solid_ref, surface_ref, own_ref, half_ref):
    core = lax.rem(lax.axis_index("span"), 2)
    for x in range(4):
        porosity = porosity_ref[x]
        blend = jnp.where(
            solid_ref[x] == 1, 1.0, jnp.where(surface_ref[x] == 1, porosity, 0.0)
        )
        out = collide([f_ref[p, x] for p in range(19)], blend)
        for p in range(19):
            own_ref[p, x] = out[p]
        own_ref[BLEND, x] = blend
        own_ref[WEIGHT, x] = weight_ref[x]
    for layer in range(21):
        for pair in range(2):
            first, second = own_ref[layer, 2 * pair], own_ref[layer, 2 * pair + 1]
            low = (sublane(first) < 4) == (core == 0)
            half_ref[layer, pair] = jnp.where(low, first, pltpu.roll(second, 4, 0))


def inner_kernel(own_ref, both_ref, half_ref, side_ref, state_ref, next_ref, up_ref, down_ref):
    core = lax.rem(lax.axis_index("span"), 2)
    for layer in range(21):
        for pair in range(2):
            came = half_ref[layer, pair]
            low = (sublane(came) < 4) == (core == 0)
            for x, tile in ((2 * pair, came), (2 * pair + 1, pltpu.roll(came, 4, 0))):
                side_ref[layer, x] = jnp.where(low, both_ref[1 - core, layer, x], tile)

    for x in (1, 2):
        f = []
        for p in range(19):
            cx, cy, cz = VEL[p]
            f.append(shift_pair((own_ref[p, x - cx], side_ref[p, x - cx]), cy, cz, GHOST[p]))
        for t in range(2):
            blend = (own_ref, side_ref)[t][BLEND, x]
            tiles = [f[p][t] for p in range(19)]
            out = collide(tiles, blend)
            for p in range(19):
                state_ref[p, x - 1, t] = tiles[p]
                next_ref[p, x - 1, t] = out[p]

    for ref, near, far, inward in ((up_ref, 3, 2, UP), (down_ref, 0, 1, DOWN)):
        for t, block in ((0, own_ref), (1, side_ref)):
            for i, p in enumerate(inward):
                ref[NEAR + i, t] = block[p, near]
                ref[FAR + i, t] = block[p, far]
                ref[FAR_NEXT + i, t] = next_ref[p, far - 1, t]
            for i, p in enumerate(FLAT):
                ref[NEAR_FLAT + i, t] = block[p, near]
            ref[NEAR_BLEND, t] = block[BLEND, near]
            ref[NEAR_WEIGHT, t] = block[WEIGHT, near]
            ref[FAR_WEIGHT, t] = block[WEIGHT, far]
        came = {}
        for p in inward + FLAT:
            cx, cy, cz = VEL[p]
            at = far - cx - 1
            came[p] = shift_pair((next_ref[p, at, 0], next_ref[p, at, 1]), cy, cz, GHOST[p])
        for t in range(2):
            for i, part in enumerate(moment_sums({p: came[p][t] for p in came})):
                ref[FAR_PART + i, t] = part


def last_kernel(
    f_ref, solid_ref, surface_ref, own_ref, side_ref, state_ref, next_ref, up_ref, down_ref,
    low_ref, high_ref, adjoint_ref, sensitivity_ref, c1_ref, s1_ref, a1_ref, field_ref,
):
    place = lax.axis_index("stream")
    first = place == 0
    last = place == lax.axis_size("stream") - 1

    def outside(x):
        return first if x < 0 else last if x > 3 else None

    def masked(x, value, fill):
        flag = outside(x)
        return value if flag is None else jnp.where(flag, fill, value)

    def message(x):
        return (low_ref, UP) if x < 0 else (high_ref, DOWN)

    def c0(p, x):
        if 0 <= x <= 3:
            return (own_ref[p, x], side_ref[p, x])
        ref, inward = message(x)
        if x in (-1, 4):
            at = NEAR + inward.index(p) if p in inward else NEAR_FLAT + FLAT.index(p)
        else:
            at = FAR + inward.index(p)
        return tuple(masked(x, ref[at, t], GHOST[p]) for t in range(2))

    def layer_of(x, which, near_at, far_at=None):
        if 0 <= x <= 3:
            return (own_ref[which, x], side_ref[which, x])
        ref, _ = message(x)
        at = near_at if x in (-1, 4) else far_at
        return (ref[at, 0], ref[at, 1])

    for x in (1, 2):
        for p in range(19):
            for t in range(2):
                s1_ref[p, x + 1, t] = state_ref[p, x - 1, t]
                c1_ref[p, x + 2, t] = next_ref[p, x - 1, t]
    for x in (-2, 5):
        ref, inward = message(x)
        for i, p in enumerate(inward):
            for t in range(2):
                c1_ref[p, x + 2, t] = masked(x, ref[FAR_NEXT + i, t], GHOST[p])
    for x in (-1, 0, 3, 4):
        f = []
        for p in range(19):
            cx, cy, cz = VEL[p]
            f.append(shift_pair(c0(p, x - cx), cy, cz, GHOST[p]))
        blend = layer_of(x, BLEND, NEAR_BLEND)
        for t in range(2):
            tiles = [f[p][t] for p in range(19)]
            out = collide(tiles, blend[t])
            for p in range(19):
                s1_ref[p, x + 1, t] = tiles[p]
                c1_ref[p, x + 2, t] = masked(x, out[p], GHOST[p])

    for x in range(-2, 6):
        parts, pops = None, list(range(19))
        if x in (-2, 2):
            parts = low_ref if x == -2 else up_ref
            pops = DOWN
        if x in (1, 5):
            parts = high_ref if x == 5 else down_ref
            pops = UP
        came = {}
        for p in pops:
            cx, cy, cz = VEL[p]
            at = x - cx + 2
            came[p] = shift_pair((c1_ref[p, at, 0], c1_ref[p, at, 1]), cy, cz, GHOST[p])
        weight = layer_of(x, WEIGHT, NEAR_WEIGHT, FAR_WEIGHT)
        for t in range(2):
            total = moment_sums({p: came[p][t] for p in came})
            if parts is not None:
                total = [total[i] + parts[FAR_PART + i, t] for i in range(4)]
            inverse = 1.0 / total[0]
            u = [total[i] * inverse for i in range(1, 4)]
            kinetic = 0.5 * (u[0] * u[0] + u[1] * u[1] + u[2] * u[2])
            for i, value in enumerate(u + [kinetic]):
                field_ref[i, x + 2, t] = masked(x, weight[t] * value, 0.0)

    def cotangent(p, x):
        cx, cy, cz = VEL[p]
        pair = []
        for t in range(2):
            value = -field_ref[3, x + cx + 2, t]
            for k in range(3):
                if VEL[p][k] == 1:
                    value = value + field_ref[k, x + cx + 2, t]
                if VEL[p][k] == -1:
                    value = value - field_ref[k, x + cx + 2, t]
            pair.append(value)
        return shift_pair(tuple(pair), -cy, -cz, 0.0)

    parts = {}
    for x in range(-1, 5):
        h = [cotangent(p, x) for p in range(19)]
        blend = layer_of(x, BLEND, NEAR_BLEND)
        for t in range(2):
            wanted = set(range(19) if 0 <= x <= 3 else DOWN if x < 0 else UP)
            if t == 1:
                wanted = {p for p in wanted if VEL[p][1] != 0}
            out, part = adjoint_collide(
                [s1_ref[p, x + 1, t] for p in range(19)],
                blend[t],
                [h[p][t] for p in range(19)],
                wanted,
                t == 0 and 0 <= x <= 3,
            )
            for p, value in out.items():
                a1_ref[p, x + 1, t] = masked(x, value, 0.0)
            if part is not None:
                parts[x] = part
    for x in range(4):
        sensitivity_ref[x] = parts[x]

    for x in range(4):
        h = []
        for p in range(19):
            cx, cy, cz = VEL[p]
            at = x + cx + 1
            tile = a1_ref[p, at, 0]
            if cy:
                tile = shift_y((tile, a1_ref[p, at, 1]), -cy)[0]
            h.append(shift_z(tile, -cz, 0.0))
        out, part = adjoint_collide(
            [f_ref[p, x] for p in range(19)], own_ref[BLEND, x], h, set(range(19)), True
        )
        for p in range(19):
            adjoint_ref[p, x] = out[p]
        design = (solid_ref[x] == 0) & (surface_ref[x] == 1)
        sensitivity_ref[x] = jnp.where(design, sensitivity_ref[x] + part, 0.0)


def call(kernel, inputs, shapes, scratch=()):
    vmem = pl.BlockSpec(memory_space=pltpu.VMEM)
    return pl.pallas_call(
        kernel,
        out_shape=[jax.ShapeDtypeStruct(shape, jnp.float32) for shape in shapes],
        in_specs=[vmem] * len(inputs),
        out_specs=[vmem] * len(shapes),
        scratch_shapes=[pltpu.VMEM(shape, jnp.float32) for shape in scratch],
        compiler_params=pltpu.CompilerParams(vmem_limit_bytes=24 * 1024 * 1024),
    )(*inputs)


def shards(checkpoint, porosity, deposit_weight, solid_mask, surface_mask):
    stream, span = lax.axis_size("stream"), lax.axis_size("span")
    tile = (8, 128)
    block, half = (21, 4) + tile, (21, 2) + tile
    own, mine = call(
        start_kernel,
        (checkpoint, porosity, deposit_weight, solid_mask, surface_mask),
        [block, half],
    )
    cores = [[i, i + 1] for i in range(0, span, 2)]
    chips = [(i, (i + 1) % span) for i in range(1, span, 2)]
    came = lax.ppermute(mine, "span", chips + [(b, a) for a, b in chips])
    both = lax.all_gather(own, "span", axis_index_groups=cores)
    rows = (19, 2, 2) + tile
    message = (LAYERS, 2) + tile
    side, state, following, up, down = call(
        inner_kernel, (own, both, came), [block, rows, rows, message, message]
    )
    low = lax.ppermute(up, "stream", [(i, (i + 1) % stream) for i in range(stream)])
    high = lax.ppermute(down, "stream", [((i + 1) % stream, i) for i in range(stream)])
    adjoint, sensitivity = call(
        last_kernel,
        (
            checkpoint, solid_mask, surface_mask, own, side, state, following, up, down,
            low, high,
        ),
        [(19, 4) + tile, (4,) + tile],
        [(19, 8, 2) + tile, (19, 6, 2) + tile, (19, 6, 2) + tile, (4, 8, 2) + tile],
    )
    return (adjoint, sensitivity)


def solution(mesh):
    placed = (
        P(None, "stream", "span", None),
        P("stream", "span", None),
        P("stream", "span", None),
        P("stream", "span", None),
        P("stream", "span", None),
    )
    return jax.shard_map(
        shards,
        mesh=mesh,
        in_specs=placed,
        out_specs=(P(None, "stream", "span", None), P("stream", "span", None)),
        check_vma=False,
    )
```

time: 109 us -> 37.1 us (0.34)
  the two profiles are of different devices: /device:TPU:27 before, /device:TPU:24 now
where the time goes in v1:
time: 37.1 us; the launch traced here: 36.6 us
  starting transfers between devices  18.8 us (51%)
  waiting for transfers between devices  8.67 us (23%)
  local copies, waits for them, and re-layouts  3.84 us (10%)
  blocking collectives  2.42 us (7%)
  Pallas kernels  2.23 us (6%)
  between operations  0.69 us (2%)
    ppermute x1, starting transfers between devices, shards(): lax.ppermute(down, 'stream', [((i + 1) % stream, i) for i in range(stream)])  10.9 us
    ppermute x1, starting transfers between devices, shards(): lax.ppermute(up, 'stream', [(i, (i + 1) % stream) for i in range(stream)])  4.89 us
    ppermute x1, waiting for transfers between devices, shards(): lax.ppermute(up, 'stream', [(i, (i + 1) % stream) for i in range(stream)])  4.03 us
    unnamed x16, local copies, waits for them, and re-layouts  3.84 us
    ppermute x1, waiting for transfers between devices, shards(): came = lax.ppermute(mine, 'span', chips + [(b, a) for a, b in chips])  3.35 us
    ppermute x1, starting transfers between devices, shards(): came = lax.ppermute(mine, 'span', chips + [(b, a) for a, b in chips])  3.02 us
    all_gather x1, blocking collectives, shards(): both = lax.all_gather(own, 'span', axis_index_groups=cores)  2.42 us
    pallas_call x3, Pallas kernels, call(): pl.pallas_call(kernel, out_shape=[jax.ShapeDtypeStruct(shape, jnp.float32...  2.23 us
  transfers between devices with their start and end apart: 3, of which 3 were waited for; matrix products, arithmetic and copies ran while one was open for 0% of the time, Pallas kernels for 0%

profile of v1, /device:TPU:24, one launch (start us, length us, event | category | flops | bytes accessed | tf_op | source)
XLA Modules:
  0.0 36.6 jit_solution(2268065841233761985)
XLA Ops:
  0.6 0.0 copy-start
  0.6 1.0 %copy-done = f32[19,4,8,128]{3,2,1,0:T(8,128)S(1)} copy-done((f32[19,4,8,128]{3,2,1,0:T(8,128)S(1)}, f32[19,4,8,128]{3,2,1,0:T(8,128)}, u32[]{:S(2)}) %copy-start) | copy-done | bytes 311320
  1.6 0.0 copy-start.2
  1.6 0.7 %copy-done.2 = s32[4,8,128]{2,1,0:T(8,128)S(1)} copy-done((s32[4,8,128]{2,1,0:T(8,128)S(1)}, s32[4,8,128]{2,1,0:T(8,128)}, u32[]{:S(2)}) %copy-start.2) | copy-done | bytes 16408
  2.3 0.0 copy-start.4
  2.3 0.7 %copy-done.4 = s32[4,8,128]{2,1,0:T(8,128)S(1)} copy-done((s32[4,8,128]{2,1,0:T(8,128)S(1)}, s32[4,8,128]{2,1,0:T(8,128)}, u32[]{:S(2)}) %copy-start.4) | copy-done | bytes 16408
  3.0 0.0 copy-start.6
  3.0 0.7 %copy-done.6 = f32[4,8,128]{2,1,0:T(8,128)S(1)} copy-done((f32[4,8,128]{2,1,0:T(8,128)S(1)}, f32[4,8,128]{2,1,0:T(8,128)}, u32[]{:S(2)}) %copy-start.6) | copy-done | bytes 16408
  3.8 0.0 copy-start.7
  3.8 0.7 %copy-done.7 = f32[4,8,128]{2,1,0:T(8,128)S(1)} copy-done((f32[4,8,128]{2,1,0:T(8,128)S(1)}, f32[4,8,128]{2,1,0:T(8,128)}, u32[]{:S(2)}) %copy-start.7) | copy-done | bytes 16408
  4.5 0.1 shard_map.68
  4.6 3.0 %collective-permute-start = (f32[21,2,8,128]{3,2,1,0:T(8,128)S(1)}, f32[21,2,8,128]{3,2,1,0:T(8,128)S(1)}, u32[]{:S(2)}, u32[]{:S(2)}) collective-permute-start(f32[21,2,8,128]{3,2,1,0:T(8,128)S(1)} %get-tuple-element.10), channel_id=1, source_target_pairs={{1,2},{3,4},{5,6},{7,8},{9,10},{11,12},{13,14},{15,0},{2,1},{4,3},... | collective-permute-start | bytes 516104 | tf_op jit(solution)/shard_map/ppermute | solution.py:412
  7.6 2.4 %all-gather = f32[42,4,8,128]{3,2,1,0:T(8,128)S(1)} all-gather(f32[21,4,8,128]{3,2,1,0:T(8,128)S(1)} %get-tuple-element.9.own_ref), channel_id=2, replica_groups={{0,1},{2,3},{4,5},{6,7},{8,9},{10,11},{12,13},{14,15},{16,17},{18,19},{..., dimensions={0}, use_global_device_ids=true | all-gather | bytes 1032192 | tf_op jit(solution)/shard_map/all_gather | solution.py:413
  10.1 3.4 %collective-permute-done.half_ref = f32[21,2,8,128]{3,2,1,0:T(8,128)S(1)} collective-permute-done((f32[21,2,8,128]{3,2,1,0:T(8,128)S(1)}, f32[21,2,8,128]{3,2,1,0:T(8,128)S(1)}, u32[]{:S(2)}, u32[]{:S(2)}) %collective-permute-start) | collective-permute-done | bytes 172064 | tf_op jit(solution)/shard_map/ppermute | solution.py:412
  13.4 0.0 copy-start.1
  13.4 0.0 copy-start.3
  13.4 0.0 copy-start.5
  13.4 0.3 shard_map.69
  13.7 4.9 %collective-permute-start.1 = (f32[31,2,8,128]{3,2,1,0:T(8,128)S(1)}, f32[31,2,8,128]{3,2,1,0:T(8,128)S(1)}, u32[]{:S(2)}, u32[]{:S(2)}) collective-permute-start(f32[31,2,8,128]{3,2,1,0:T(8,128)S(1)} %get-tuple-element.14.up_ref), channel_id=1, source_target_pairs={{0,16},{16,32},{32,48},{48,64},{64,80},{80,96},{96,112},{112,128},... | collective-permute-start | bytes 761864 | tf_op jit(solution)/shard_map/ppermute | solution.py:419
  18.6 10.9 %collective-permute-start.2 = (f32[31,2,8,128]{3,2,1,0:T(8,128)S(1)}, f32[31,2,8,128]{3,2,1,0:T(8,128)S(1)}, u32[]{:S(2)}, u32[]{:S(2)}) collective-permute-start(f32[31,2,8,128]{3,2,1,0:T(8,128)S(1)} %get-tuple-element.15.down_ref), channel_id=1, source_target_pairs={{16,0},{32,16},{48,32},{64,48},{80,64},{96,80},{112,96},{128,112},... | collective-permute-start | bytes 761864 | tf_op jit(solution)/shard_map/ppermute | solution.py:420
  29.5 4.0 %collective-permute-done.1.low_ref = f32[31,2,8,128]{3,2,1,0:T(8,128)S(1)} collective-permute-done((f32[31,2,8,128]{3,2,1,0:T(8,128)S(1)}, f32[31,2,8,128]{3,2,1,0:T(8,128)S(1)}, u32[]{:S(2)}, u32[]{:S(2)}) %collective-permute-start.1) | collective-permute-done | bytes 253984 | tf_op jit(solution)/shard_map/ppermute | solution.py:419
  33.5 1.3 %collective-permute-done.2.high_ref = f32[31,2,8,128]{3,2,1,0:T(8,128)S(1)} collective-permute-done((f32[31,2,8,128]{3,2,1,0:T(8,128)S(1)}, f32[31,2,8,128]{3,2,1,0:T(8,128)S(1)}, u32[]{:S(2)}, u32[]{:S(2)}) %collective-permute-start.2) | collective-permute-done | bytes 253984 | tf_op jit(solution)/shard_map/ppermute | solution.py:420
  34.8 0.0 copy-done.1
  34.8 0.0 copy-done.3
  34.8 0.0 copy-done.5
  34.8 1.8 %shard_map.70 = (f32[19,4,8,128]{3,2,1,0:T(8,128)}, f32[4,8,128]{2,1,0:T(8,128)}) custom-call(f32[19,4,8,128]{3,2,1,0:T(8,128)S(1)} %copy-done.1, s32[4,8,128]{2,1,0:T(8,128)S(1)} %copy-done.3, s32[4,8,128]{2,1,0:T(8,128)S(1)} %copy-done.5, f32[21,4,8,128]{3,2,1,0:T(8,128)S(1)} %get-tuple-element.9.own_ref, ...), custom_call_target="tpu_custom_call" | custom-call | tf_op jit(solution)/shard_map/pallas_call | solution.py:391
Async XLA Ops:
  0.6 1.0 %copy-start = (f32[19,4,8,128]{3,2,1,0:T(8,128)S(1)}, f32[19,4,8,128]{3,2,1,0:T(8,128)}, u32[]{:S(2)}) copy-start(f32[19,4,8,128]{3,2,1,0:T(8,128)} %f_ref.3) | copy-start | bytes 933892
  1.6 0.7 %copy-start.2 = (s32[4,8,128]{2,1,0:T(8,128)S(1)}, s32[4,8,128]{2,1,0:T(8,128)}, u32[]{:S(2)}) copy-start(s32[4,8,128]{2,1,0:T(8,128)} %solid_ref.3) | copy-start | bytes 49156
  2.3 0.7 %copy-start.4 = (s32[4,8,128]{2,1,0:T(8,128)S(1)}, s32[4,8,128]{2,1,0:T(8,128)}, u32[]{:S(2)}) copy-start(s32[4,8,128]{2,1,0:T(8,128)} %surface_ref.3) | copy-start | bytes 49156
  3.0 0.7 %copy-start.6 = (f32[4,8,128]{2,1,0:T(8,128)S(1)}, f32[4,8,128]{2,1,0:T(8,128)}, u32[]{:S(2)}) copy-start(f32[4,8,128]{2,1,0:T(8,128)} %porosity_ref.1) | copy-start | bytes 49156
  3.8 0.7 %copy-start.7 = (f32[4,8,128]{2,1,0:T(8,128)S(1)}, f32[4,8,128]{2,1,0:T(8,128)}, u32[]{:S(2)}) copy-start(f32[4,8,128]{2,1,0:T(8,128)} %weight_ref.1) | copy-start | bytes 49156
  4.6 8.8 %collective-permute-start = (f32[21,2,8,128]{3,2,1,0:T(8,128)S(1)}, f32[21,2,8,128]{3,2,1,0:T(8,128)S(1)}, u32[]{:S(2)}, u32[]{:S(2)}) collective-permute-start(f32[21,2,8,128]{3,2,1,0:T(8,128)S(1)} %get-tuple-element.10), channel_id=1, source_target_pairs={{1,2},{3,4},{5,6},{7,8},{9,10},{11,12},{13,14},{15,0},{2,1},{4,3},... | collective-permute-start | bytes 516104 | tf_op jit(solution)/shard_map/ppermute | solution.py:412
  13.4 21.4 %copy-start.1 = (f32[19,4,8,128]{3,2,1,0:T(8,128)S(1)}, f32[19,4,8,128]{3,2,1,0:T(8,128)}, u32[]{:S(2)}) copy-start(f32[19,4,8,128]{3,2,1,0:T(8,128)} %f_ref.3) | copy-start | bytes 933892
  13.4 21.4 %copy-start.3 = (s32[4,8,128]{2,1,0:T(8,128)S(1)}, s32[4,8,128]{2,1,0:T(8,128)}, u32[]{:S(2)}) copy-start(s32[4,8,128]{2,1,0:T(8,128)} %solid_ref.3) | copy-start | bytes 49156
  13.4 21.4 %copy-start.5 = (s32[4,8,128]{2,1,0:T(8,128)S(1)}, s32[4,8,128]{2,1,0:T(8,128)}, u32[]{:S(2)}) copy-start(s32[4,8,128]{2,1,0:T(8,128)} %surface_ref.3) | copy-start | bytes 49156
  13.7 19.8 %collective-permute-start.1 = (f32[31,2,8,128]{3,2,1,0:T(8,128)S(1)}, f32[31,2,8,128]{3,2,1,0:T(8,128)S(1)}, u32[]{:S(2)}, u32[]{:S(2)}) collective-permute-start(f32[31,2,8,128]{3,2,1,0:T(8,128)S(1)} %get-tuple-element.14.up_ref), channel_id=1, source_target_pairs={{0,16},{16,32},{32,48},{48,64},{64,80},{80,96},{96,112},{112,128},... | collective-permute-start | bytes 761864 | tf_op jit(solution)/shard_map/ppermute | solution.py:419
  18.6 16.2 %collective-permute-start.2 = (f32[31,2,8,128]{3,2,1,0:T(8,128)S(1)}, f32[31,2,8,128]{3,2,1,0:T(8,128)S(1)}, u32[]{:S(2)}, u32[]{:S(2)}) collective-permute-start(f32[31,2,8,128]{3,2,1,0:T(8,128)S(1)} %get-tuple-element.15.down_ref), channel_id=1, source_target_pairs={{16,0},{32,16},{48,32},{64,48},{80,64},{96,80},{112,96},{128,112},... | collective-permute-start | bytes 761864 | tf_op jit(solution)/shard_map/ppermute | solution.py:420

commit v2 on v1

v2 whole, which is shorter than its diff:
```python
import functools

import jax
import jax.numpy as jnp
import numpy as np
from jax import lax
from jax.experimental import pallas as pl
from jax.experimental.pallas import tpu as pltpu
from jax.sharding import PartitionSpec as P

VELOCITY = np.array(
    [
        [0, 0, 0],
        [1, 0, 0],
        [-1, 0, 0],
        [0, 1, 0],
        [0, -1, 0],
        [0, 0, 1],
        [0, 0, -1],
        [1, 1, 0],
        [-1, -1, 0],
        [1, -1, 0],
        [-1, 1, 0],
        [1, 0, 1],
        [-1, 0, -1],
        [1, 0, -1],
        [-1, 0, 1],
        [0, 1, 1],
        [0, -1, -1],
        [0, 1, -1],
        [0, -1, 1],
    ]
)
WEIGHTS = np.array([1.0 / 3.0] + [1.0 / 18.0] * 6 + [1.0 / 36.0] * 12)
GHOST_DENSITY = 18.0
INFLOW_SPEED = 0.08
GHOST_STATE = (
    WEIGHTS
    * GHOST_DENSITY
    * (
        1.0
        + 3.0 * VELOCITY[:, 0] * INFLOW_SPEED
        + 4.5 * (VELOCITY[:, 0] * INFLOW_SPEED) ** 2
        - 1.5 * INFLOW_SPEED**2
    )
)
GHOST = [float(value) for value in GHOST_STATE]
VEL = [tuple(int(part) for part in row) for row in VELOCITY]
CX = [row[0] for row in VEL]
UP = [p for p in range(19) if CX[p] == 1]
DOWN = [p for p in range(19) if CX[p] == -1]
FLAT = [p for p in range(19) if CX[p] == 0]
OPP = [0] + [p + 1 if p % 2 else p - 1 for p in range(1, 19)]
BLEND, WEIGHT = 19, 20
STATE, MOMENTS, NEAR_BLEND, WIDE = 0, 5, 9, 10
SUM_FAR, SUM_NEAR, SUM_OWN, WEIGHT_FAR, WEIGHT_NEAR, LAYERS = 10, 14, 18, 21, 22, 23
TILES = LAYERS + WIDE + (LAYERS - WIDE + 1) // 2


def sublane(tile):
    return lax.broadcasted_iota(jnp.int32, tile.shape, len(tile.shape) - 2)


def lane(tile):
    return lax.broadcasted_iota(jnp.int32, tile.shape, len(tile.shape) - 1)


def shift_z(tile, step, fill):
    if step == 0:
        return tile
    rolled = pltpu.roll(tile, step % 128, 1)
    return jnp.where(lane(tile) == (0 if step == 1 else 127), fill, rolled)


def shift_y(pair, step):
    if step == 0:
        return pair
    own, side = (pltpu.roll(tile, step % 8, 0) for tile in pair)
    edge = sublane(own) == (0 if step == 1 else 7)
    return (jnp.where(edge, side, own), jnp.where(edge, own, side))


def shift_pair(pair, stepy, stepz, fill):
    return tuple(shift_z(tile, stepz, fill) for tile in shift_y(pair, stepy))


def pairs_of(f):
    sums = [f[2 * i + 1] + f[2 * i + 2] for i in range(9)]
    diffs = [f[2 * i + 1] - f[2 * i + 2] for i in range(9)]
    return sums, diffs


def along_axes(v):
    return (
        v[0] + v[3] + v[4] + v[5] + v[6],
        v[1] + v[3] - v[4] + v[7] + v[8],
        v[2] + v[5] - v[6] + v[7] - v[8],
    )


def dots(u):
    x, y, z = u
    return [x, y, z, x + y, x - y, x + z, x - z, y + z, y - z]


def flow(f0, sums, diffs):
    density = f0 + sum(sums[1:], sums[0])
    inverse = 1.0 / density
    u = [m * inverse for m in along_axes(diffs)]
    square = u[0] * u[0] + u[1] * u[1] + u[2] * u[2]
    return density, u, square


def collide(f, b):
    sums, diffs = pairs_of(f)
    density, u, square = flow(f[0], sums, diffs)
    keep = 1.0 - b
    j = 0.1 * keep
    alpha, beta = 0.5 * (j + b), 0.5 * (j - b)
    scaled = (0.9 * keep) * density
    rest = scaled * (1.0 - 1.5 * square)
    flux = dots([scaled * part for part in u])
    out = [(j + b) * f[0] + (1.0 / 3.0) * rest]
    rest_axis, rest_diag = rest * (1.0 / 18.0), rest * (1.0 / 36.0)
    for i, along in enumerate(dots(u)):
        w = 1.0 / 18.0 if i < 3 else 1.0 / 36.0
        even = alpha * sums[i] + (rest_axis if i < 3 else rest_diag) + flux[i] * along * (4.5 * w)
        odd = beta * diffs[i] + flux[i] * (3.0 * w)
        out += [even + odd, even - odd]
    return out


def adjoint_values(u, square, b, h, wanted):
    s, d = pairs_of(h)
    w = [1.0 / 18.0] * 3 + [1.0 / 36.0] * 6
    t = [s[i] * w[i] for i in range(9)]
    h0 = h[0] * (1.0 / 3.0) + sum(t[1:], t[0])
    h1 = along_axes([d[i] * w[i] for i in range(9)])
    xx = t[0] + t[3] + t[4] + t[5] + t[6]
    yy = t[1] + t[3] + t[4] + t[7] + t[8]
    zz = t[2] + t[5] + t[6] + t[7] + t[8]
    xy, xz, yz = t[3] - t[4], t[5] - t[6], t[7] - t[8]
    v = (
        xx * u[0] + xy * u[1] + xz * u[2],
        xy * u[0] + yy * u[1] + yz * u[2],
        xz * u[0] + yz * u[1] + zz * u[2],
    )
    quad = u[0] * v[0] + u[1] * v[1] + u[2] * v[2]
    keep = 1.0 - b
    j, k = 0.1 * keep, 0.9 * keep
    alpha, beta = 0.5 * (j + b), 0.5 * (j - b)
    base = k * (h0 * (1.0 + 1.5 * square) - 4.5 * quad)
    push = dots([k * (3.0 * h1[i] + 9.0 * v[i] - 3.0 * u[i] * h0) for i in range(3)])
    out = {}
    if 0 in wanted:
        out[0] = (j + b) * h[0] + base
    for i in range(9):
        first, second = 2 * i + 1, 2 * i + 2
        if first in wanted or second in wanted:
            even = alpha * s[i] + base
            odd = beta * d[i] + push[i]
            if first in wanted:
                out[first] = even + odd
            if second in wanted:
                out[second] = even - odd
    return out, s, d, h0, h1, quad


def adjoint_collide(f, b, h, wanted, blend_part):
    fsums, fdiffs = pairs_of(f)
    density, u, square = flow(f[0], fsums, fdiffs)
    out, s, d, h0, h1, quad = adjoint_values(u, square, b, h, wanted)
    part = None
    if blend_part:
        equil = h0 * (1.0 - 1.5 * square) + 4.5 * quad
        equil = equil + 3.0 * (u[0] * h1[0] + u[1] * h1[1] + u[2] * h1[2])
        evens = sum((s[i] * fsums[i] for i in range(1, 9)), s[0] * fsums[0])
        odds = sum((d[i] * fdiffs[i] for i in range(1, 9)), d[0] * fdiffs[0])
        part = 0.9 * h[0] * f[0] + 0.45 * evens - 0.55 * odds - 0.9 * density * equil
    return out, part


def moment_sums(values):
    density = functools.reduce(lambda a, b: a + b, values.values())
    momentum = []
    for k in range(3):
        total = None
        for p, value in values.items():
            if VEL[p][k] == 1:
                total = value if total is None else total + value
        for p, value in values.items():
            if VEL[p][k] == -1:
                total = -value if total is None else total - value
        momentum.append(total)
    return [density] + momentum


def add(*totals):
    return [functools.reduce(lambda a, b: a + b, parts) for parts in zip(*totals)]


def put_message(ref, layers):
    for i, pair in enumerate(layers):
        ref[i] = pair[0]
    for i in range(WIDE):
        ref[LAYERS + i] = layers[i][1]
    for i in range(WIDE, LAYERS, 2):
        tile = layers[i][1]
        if i + 1 < LAYERS:
            at = sublane(tile)
            tile = jnp.where((at < 2) | (at > 5), tile, pltpu.roll(layers[i + 1][1], 4, 0))
        ref[LAYERS + WIDE + (i - WIDE) // 2] = tile


def get_message(ref, i):
    if i < WIDE:
        return (ref[i], ref[LAYERS + i])
    tile = ref[LAYERS + WIDE + (i - WIDE) // 2]
    return (ref[i], pltpu.roll(tile, 4, 0) if (i - WIDE) % 2 else tile)


def start_kernel(
    f_hbm, porosity_hbm, weight_hbm, solid_hbm, surface_hbm, own_ref, half_ref,
    f_ref, porosity_ref, weight_ref, solid_ref, surface_ref, sems,
):
    copies = [
        pltpu.make_async_copy(source, target, sems.at[i])
        for i, (source, target) in enumerate(
            (
                (solid_hbm, solid_ref),
                (surface_hbm, surface_ref),
                (porosity_hbm, porosity_ref),
                (weight_hbm, weight_ref),
                (f_hbm, f_ref),
            )
        )
    ]
    for copy in copies:
        copy.start()
    for copy in copies:
        copy.wait()
    core = lax.rem(lax.axis_index("span"), 2)
    for x in range(4):
        porosity = porosity_ref[x]
        blend = jnp.where(
            solid_ref[x] == 1, 1.0, jnp.where(surface_ref[x] == 1, porosity, 0.0)
        )
        out = collide([f_ref[p, x] for p in range(19)], blend)
        for p in range(19):
            own_ref[p, x] = out[p]
        own_ref[BLEND, x] = blend
        own_ref[WEIGHT, x] = weight_ref[x]
    for layer in range(21):
        for pair in range(2):
            first, second = own_ref[layer, 2 * pair], own_ref[layer, 2 * pair + 1]
            low = (sublane(first) < 4) == (core == 0)
            half_ref[layer, pair] = jnp.where(low, first, pltpu.roll(second, 4, 0))


def inner_kernel(own_ref, both_ref, half_ref, side_ref, state_ref, next_ref, up_ref, down_ref):
    core = lax.rem(lax.axis_index("span"), 2)
    for layer in range(21):
        for pair in range(2):
            came = half_ref[layer, pair]
            low = (sublane(came) < 4) == (core == 0)
            for x, tile in ((2 * pair, came), (2 * pair + 1, pltpu.roll(came, 4, 0))):
                side_ref[layer, x] = jnp.where(low, both_ref[1 - core, layer, x], tile)

    def c0(p, x):
        return (own_ref[p, x], side_ref[p, x])

    def moved(p, pair):
        return shift_pair(pair, VEL[p][1], VEL[p][2], GHOST[p])

    for x in (1, 2):
        f = [moved(p, c0(p, x - CX[p])) for p in range(19)]
        blend = c0(BLEND, x)
        for t in range(2):
            tiles = [f[p][t] for p in range(19)]
            out = collide(tiles, blend[t])
            for p in range(19):
                state_ref[p, x - 1, t] = tiles[p]
                next_ref[p, x - 1, t] = out[p]

    def c1(p, x):
        return (next_ref[p, x - 1, 0], next_ref[p, x - 1, 1])

    for ref, near, far, inward, outward in (
        (up_ref, 3, 2, UP, DOWN),
        (down_ref, 0, 1, DOWN, UP),
    ):
        step = far - near
        enter = [moved(p, c0(p, near)) for p in inward]
        known = {p: moved(p, c0(p, near if p in FLAT else far)) for p in inward + FLAT}
        blend = c0(BLEND, near)
        j = [0.1 * (1.0 - part) for part in blend]
        layers = [None] * LAYERS
        layers[STATE : STATE + 5] = enter
        halves = [moment_sums({p: known[p][t] for p in known}) for t in range(2)]
        layers[MOMENTS : MOMENTS + 4] = list(zip(*halves))
        layers[NEAR_BLEND] = blend
        came = {p: moved(p, c1(p, far + step)) for p in inward}
        came.update({p: moved(p, c1(p, far)) for p in FLAT})
        for p in outward:
            came[p] = moved(p, tuple(blend[t] * known[OPP[p]][t] for t in range(2)))
        halves = [moment_sums({p: came[p][t] for p in came}) for t in range(2)]
        layers[SUM_FAR : SUM_FAR + 4] = list(zip(*halves))
        came = {p: moved(p, c1(p, far)) for p in inward}
        for p in FLAT:
            came[p] = moved(
                p,
                tuple(j[t] * known[p][t] + blend[t] * known[OPP[p]][t] for t in range(2)),
            )
        halves = [moment_sums({p: came[p][t] for p in came}) for t in range(2)]
        layers[SUM_NEAR : SUM_NEAR + 4] = list(zip(*halves))
        came = {p: moved(p, tuple(j[t] * known[p][t] for t in range(2))) for p in inward}
        halves = [moment_sums({p: came[p][t] for p in came}) for t in range(2)]
        halves = [[half[0], half[2], half[3]] for half in halves]
        layers[SUM_OWN : SUM_OWN + 3] = list(zip(*halves))
        layers[WEIGHT_FAR] = c0(WEIGHT, far)
        layers[WEIGHT_NEAR] = c0(WEIGHT, near)
        put_message(ref, layers)


def last_kernel(
    f_ref, solid_ref, surface_ref, own_ref, side_ref, state_ref, next_ref, low_ref, high_ref,
    adjoint_ref, sensitivity_ref, s1_ref, c1_ref, sum_ref, flow_ref, a1_ref, field_ref,
):
    place = lax.axis_index("stream")
    at_start = place == 0
    at_end = place == lax.axis_size("stream") - 1
    ends = (
        (low_ref, at_start, 0, -1, UP, DOWN),
        (high_ref, at_end, 3, 1, DOWN, UP),
    )

    def moved(p, pair, fill=None):
        return shift_pair(pair, VEL[p][1], VEL[p][2], GHOST[p] if fill is None else fill)

    def c0(p, x):
        return (own_ref[p, x], side_ref[p, x])

    for x in (1, 2):
        for p in range(19):
            for t in range(2):
                s1_ref[p, x, t] = state_ref[p, x - 1, t]
                c1_ref[p, x, t] = next_ref[p, x - 1, t]
    for ref, end, x, out, inward, outward in ends:
        f = {p: moved(p, c0(p, x if p in FLAT else x - out)) for p in FLAT + outward}
        for i, p in enumerate(inward):
            f[p] = tuple(
                jnp.where(end, GHOST[p], part) for part in get_message(ref, STATE + i)
            )
        blend = c0(BLEND, x)
        for t in range(2):
            tiles = [f[p][t] for p in range(19)]
            after = collide(tiles, blend[t])
            for p in range(19):
                s1_ref[p, x, t] = tiles[p]
                c1_ref[p, x, t] = after[p]

    def c1(p, x):
        return (c1_ref[p, x, 0], c1_ref[p, x, 1])

    def save_field(x, t, total, weight, end=None):
        inverse = 1.0 / total[0]
        u = [total[i] * inverse for i in range(1, 4)]
        kinetic = 0.5 * (u[0] * u[0] + u[1] * u[1] + u[2] * u[2])
        for i, value in enumerate(u + [kinetic]):
            value = weight * value
            field_ref[i, x + 2, t] = value if end is None else jnp.where(end, 0.0, value)

    for side, (ref, end, x, out, inward, outward) in enumerate(ends):
        sent = [get_message(ref, i) for i in range(LAYERS)]
        blend = sent[NEAR_BLEND]
        leaving = {p: moved(p, c0(p, x)) for p in outward}
        to_far, to_near, to_own = {}, {}, {}
        for t in range(2):
            total = add(
                moment_sums({p: leaving[p][t] for p in outward}),
                [sent[MOMENTS + i][t] for i in range(4)],
            )
            density = total[0]
            inverse = 1.0 / density
            u = [part * inverse for part in total[1:]]
            square = u[0] * u[0] + u[1] * u[1] + u[2] * u[2]
            for i, value in enumerate(u + [square]):
                flow_ref[side, i, t] = value
            keep = 1.0 - blend[t]
            scaled = (0.9 * keep) * density
            rest = scaled * (1.0 - 1.5 * square)
            along = dots(u)
            for p in range(19):
                value = float(WEIGHTS[p]) * rest
                if p:
                    cu = along[(p - 1) // 2]
                    flux = scaled * cu
                    value = value + flux * cu * float(4.5 * WEIGHTS[p])
                    value = value + flux * float((3.0 if p % 2 else -3.0) * WEIGHTS[p])
                if p in outward:
                    to_far.setdefault(p, []).append(value + 0.1 * keep * leaving[p][t])
                elif p in inward:
                    to_own.setdefault(p, []).append(value + blend[t] * leaving[OPP[p]][t])
                else:
                    to_near.setdefault(p, []).append(value)
        to_far = {p: moved(p, tuple(pair), 0.0) for p, pair in to_far.items()}
        to_near = {p: moved(p, tuple(pair), 0.0) for p, pair in to_near.items()}
        to_own = {p: moved(p, tuple(pair), 0.0) for p, pair in to_own.items()}
        back = {p: moved(p, c1(p, x)) for p in outward}
        for t in range(2):
            total = add(
                moment_sums({p: to_far[p][t] for p in to_far}),
                [sent[SUM_FAR + i][t] for i in range(4)],
            )
            save_field(x + 2 * out, t, total, sent[WEIGHT_FAR][t], end)
            near = dict(to_near)
            near.update(back)
            total = add(
                moment_sums({p: near[p][t] for p in near}),
                [sent[SUM_NEAR + i][t] for i in range(4)],
            )
            save_field(x + out, t, total, sent[WEIGHT_NEAR][t], end)
            own = moment_sums({p: to_own[p][t] for p in to_own})
            ready = [sent[SUM_OWN + i][t] for i in range(3)]
            own = add(own, [ready[0], -out * ready[0], ready[1], ready[2]])
            ghost = moment_sums({p: GHOST[p] for p in inward})
            for i in range(4):
                sum_ref[side, i, t] = jnp.where(end, ghost[i], own[i])

    for x in range(4):
        pops, given = list(range(19)), None
        if x == 0:
            pops, given = FLAT + DOWN, 0
        if x == 3:
            pops, given = FLAT + UP, 1
        came = {p: moved(p, c1(p, x - CX[p])) for p in pops}
        weight = c0(WEIGHT, x)
        for t in range(2):
            total = moment_sums({p: came[p][t] for p in came})
            if given is not None:
                total = add(total, [sum_ref[given, i, t] for i in range(4)])
            save_field(x, t, total, weight[t])

    def cotangent(p, x):
        pair = []
        for t in range(2):
            value = -field_ref[3, x + CX[p] + 2, t]
            for k in range(3):
                if VEL[p][k] == 1:
                    value = value + field_ref[k, x + CX[p] + 2, t]
                if VEL[p][k] == -1:
                    value = value - field_ref[k, x + CX[p] + 2, t]
            pair.append(value)
        return shift_pair(tuple(pair), -VEL[p][1], -VEL[p][2], 0.0)

    for x in range(4):
        h = [cotangent(p, x) for p in range(19)]
        blend = c0(BLEND, x)
        for t in range(2):
            wanted = [p for p in range(19) if t == 0 or VEL[p][1] != 0]
            out, part = adjoint_collide(
                [s1_ref[p, x, t] for p in range(19)],
                blend[t],
                [h[p][t] for p in range(19)],
                wanted,
                t == 0,
            )
            for p, value in out.items():
                a1_ref[p, x + 1, t] = value
            if part is not None:
                sensitivity_ref[x] = part
    for side, (ref, end, x, out, inward, outward) in enumerate(ends):
        h = [cotangent(p, x + out) for p in range(19)]
        blend = get_message(ref, NEAR_BLEND)
        for t in range(2):
            u = [flow_ref[side, i, t] for i in range(3)]
            wanted = [p for p in outward if t == 0 or VEL[p][1] != 0]
            got = adjoint_values(
                u, flow_ref[side, 3, t], blend[t], [h[p][t] for p in range(19)], wanted
            )[0]
            for p, value in got.items():
                a1_ref[p, x + out + 1, t] = jnp.where(end, 0.0, value)

    for x in range(4):
        h = []
        for p in range(19):
            at = x + CX[p] + 1
            tile = a1_ref[p, at, 0]
            if VEL[p][1]:
                tile = shift_y((tile, a1_ref[p, at, 1]), -VEL[p][1])[0]
            h.append(shift_z(tile, -VEL[p][2], 0.0))
        out, part = adjoint_collide(
            [f_ref[p, x] for p in range(19)], own_ref[BLEND, x], h, list(range(19)), True
        )
        for p in range(19):
            adjoint_ref[p, x] = out[p]
        design = (solid_ref[x] == 0) & (surface_ref[x] == 1)
        sensitivity_ref[x] = jnp.where(design, sensitivity_ref[x] + part, 0.0)


def call(kernel, inputs, shapes, scratch=(), space=pltpu.VMEM):
    return pl.pallas_call(
        kernel,
        out_shape=[jax.ShapeDtypeStruct(shape, jnp.float32) for shape in shapes],
        in_specs=[pl.BlockSpec(memory_space=space)] * len(inputs),
        out_specs=[pl.BlockSpec(memory_space=pltpu.VMEM)] * len(shapes),
        scratch_shapes=scratch,
        compiler_params=pltpu.CompilerParams(vmem_limit_bytes=24 * 1024 * 1024),
    )(*inputs)


def shards(checkpoint, porosity, deposit_weight, solid_mask, surface_mask):
    stream, span = lax.axis_size("stream"), lax.axis_size("span")
    tile = (8, 128)
    block, half = (21, 4) + tile, (21, 2) + tile
    inputs = (checkpoint, porosity, deposit_weight, solid_mask, surface_mask)
    own, mine = call(
        start_kernel,
        inputs,
        [block, half],
        [pltpu.VMEM(value.shape, value.dtype) for value in inputs]
        + [pltpu.SemaphoreType.DMA((5,))],
        pltpu.HBM,
    )
    cores = [[i, i + 1] for i in range(0, span, 2)]
    chips = [(i, (i + 1) % span) for i in range(1, span, 2)]
    came = lax.ppermute(mine, "span", chips + [(b, a) for a, b in chips])
    both = lax.all_gather(own, "span", axis_index_groups=cores)
    rows = (19, 2, 2) + tile
    message = (TILES,) + tile
    side, state, following, up, down = call(
        inner_kernel, (own, both, came), [block, rows, rows, message, message]
    )
    low = lax.ppermute(up, "stream", [(i, i + 1) for i in range(stream - 1)])
    high = lax.ppermute(down, "stream", [(i + 1, i) for i in range(stream - 1)])
    scratch = [(19, 4, 2), (19, 4, 2), (2, 4, 2), (2, 4, 2), (19, 6, 2), (4, 8, 2)]
    adjoint, sensitivity = call(
        last_kernel,
        (checkpoint, solid_mask, surface_mask, own, side, state, following, low, high),
        [(19, 4) + tile, (4,) + tile],
        [pltpu.VMEM(shape + tile, jnp.float32) for shape in scratch],
    )
    return (adjoint, sensitivity)


def solution(mesh):
    placed = (
        P(None, "stream", "span", None),
        P("stream", "span", None),
        P("stream", "span", None),
        P("stream", "span", None),
        P("stream", "span", None),
    )
    return jax.shard_map(
        shards,
        mesh=mesh,
        in_specs=placed,
        out_specs=(P(None, "stream", "span", None), P("stream", "span", None)),
        check_vma=False,
    )
```

time: 37.1 us -> 33.9 us (0.914)
  the two profiles are of different devices: /device:TPU:24 before, /device:TPU:238 now
where the time goes in v2:
time: 33.9 us; the launch traced here: 33.4 us
  waiting for transfers between devices  12.8 us (38%)
  starting transfers between devices  9.98 us (29%)
  local copies, waits for them, and re-layouts  3.84 us (11%)
  blocking collectives  3.61 us (11%)
  Pallas kernels  2.44 us (7%)
  between operations  0.69 us (2%)
    ppermute x1, waiting for transfers between devices, shards(): high = lax.ppermute(down, 'stream', [(i + 1, i) for i in range(stream - 1)])  7.72 us
    ppermute x1, starting transfers between devices, shards(): low = lax.ppermute(up, 'stream', [(i, i + 1) for i in range(stream - 1)])  5.88 us
    unnamed x16, local copies, waits for them, and re-layouts  3.84 us
    all_gather x1, blocking collectives, shards(): both = lax.all_gather(own, 'span', axis_index_groups=cores)  3.61 us
    ppermute x1, waiting for transfers between devices, shards(): came = lax.ppermute(mine, 'span', chips + [(b, a) for a, b in chips])  2.67 us
    pallas_call x3, Pallas kernels, call(): pl.pallas_call(kernel, out_shape=[jax.ShapeDtypeStruct(shape, jnp.float32...  2.44 us
    ppermute x1, waiting for transfers between devices, shards(): low = lax.ppermute(up, 'stream', [(i, i + 1) for i in range(stream - 1)])  2.42 us
    ppermute x1, starting transfers between devices, shards(): came = lax.ppermute(mine, 'span', chips + [(b, a) for a, b in chips])  2.18 us
  transfers between devices with their start and end apart: 3, of which 3 were waited for; matrix products, arithmetic and copies ran while one was open for 0% of the time, Pallas kernels for 0%

profile of v2, /device:TPU:238, one launch (start us, length us, event | category | flops | bytes accessed | tf_op | source)
XLA Modules:
  0.0 33.4 jit_solution(13486186979662866149)
XLA Ops:
  0.6 0.0 copy-start
  0.6 1.0 %copy-done = f32[19,4,8,128]{3,2,1,0:T(8,128)S(1)} copy-done((f32[19,4,8,128]{3,2,1,0:T(8,128)S(1)}, f32[19,4,8,128]{3,2,1,0:T(8,128)}, u32[]{:S(2)}) %copy-start) | copy-done | bytes 311320
  1.6 0.0 copy-start.2
  1.6 0.7 %copy-done.2 = s32[4,8,128]{2,1,0:T(8,128)S(1)} copy-done((s32[4,8,128]{2,1,0:T(8,128)S(1)}, s32[4,8,128]{2,1,0:T(8,128)}, u32[]{:S(2)}) %copy-start.2) | copy-done | bytes 16408
  2.3 0.0 copy-start.4
  2.3 0.7 %copy-done.4 = s32[4,8,128]{2,1,0:T(8,128)S(1)} copy-done((s32[4,8,128]{2,1,0:T(8,128)S(1)}, s32[4,8,128]{2,1,0:T(8,128)}, u32[]{:S(2)}) %copy-start.4) | copy-done | bytes 16408
  3.0 0.0 copy-start.6
  3.0 0.7 %copy-done.6 = f32[4,8,128]{2,1,0:T(8,128)S(1)} copy-done((f32[4,8,128]{2,1,0:T(8,128)S(1)}, f32[4,8,128]{2,1,0:T(8,128)}, u32[]{:S(2)}) %copy-start.6) | copy-done | bytes 16408
  3.8 0.0 copy-start.7
  3.8 0.7 %copy-done.7 = f32[4,8,128]{2,1,0:T(8,128)S(1)} copy-done((f32[4,8,128]{2,1,0:T(8,128)S(1)}, f32[4,8,128]{2,1,0:T(8,128)}, u32[]{:S(2)}) %copy-start.7) | copy-done | bytes 16408
  4.5 0.3 shard_map.68
  4.8 2.2 %collective-permute-start = (f32[21,2,8,128]{3,2,1,0:T(8,128)S(1)}, f32[21,2,8,128]{3,2,1,0:T(8,128)S(1)}, u32[]{:S(2)}, u32[]{:S(2)}) collective-permute-start(f32[21,2,8,128]{3,2,1,0:T(8,128)S(1)} %get-tuple-element.10), channel_id=1, source_target_pairs={{1,2},{3,4},{5,6},{7,8},{9,10},{11,12},{13,14},{15,0},{2,1},{4,3},... | collective-permute-start | bytes 516104 | tf_op jit(solution)/shard_map/ppermute | solution.py:527
  7.0 3.6 %all-gather = f32[42,4,8,128]{3,2,1,0:T(8,128)S(1)} all-gather(f32[21,4,8,128]{3,2,1,0:T(8,128)S(1)} %get-tuple-element.9.own_ref), channel_id=2, replica_groups={{0,1},{2,3},{4,5},{6,7},{8,9},{10,11},{12,13},{14,15},{16,17},{18,19},{..., dimensions={0}, use_global_device_ids=true | all-gather | bytes 1032192 | tf_op jit(solution)/shard_map/all_gather | solution.py:528
  10.6 2.7 %collective-permute-done.half_ref = f32[21,2,8,128]{3,2,1,0:T(8,128)S(1)} collective-permute-done((f32[21,2,8,128]{3,2,1,0:T(8,128)S(1)}, f32[21,2,8,128]{3,2,1,0:T(8,128)S(1)}, u32[]{:S(2)}, u32[]{:S(2)}) %collective-permute-start) | collective-permute-done | bytes 172064 | tf_op jit(solution)/shard_map/ppermute | solution.py:527
  13.3 0.0 copy-start.1
  13.3 0.0 copy-start.3
  13.3 0.0 copy-start.5
  13.3 0.4 %shard_map.69 = (f32[21,4,8,128]{3,2,1,0:T(8,128)S(1)}, f32[19,2,2,8,128]{4,3,2,1,0:T(8,128)S(1)}, f32[19,2,2,8,128]{4,3,2,1,0:T(8,128)S(1)}, f32[40,8,128]{2,1,0:T(8,128)S(1)}, f32[40,8,128]{2,1,0:T(8,128)S(1)}) custom-call(f32[21,4,8,128]{3,2,1,0:T(8,128)S(1)} %get-tuple-element.9.own_ref, f32[2,21,4,8,128]{4,3,2,1,0:T(8,128)S(1)} %bitcast.1, ...), custom_call_target="tpu_custom_call" | custom-call | tf_op jit(solution)/shard_map/pallas_call | solution.py:502
  13.6 5.9 %collective-permute-start.1 = (f32[40,8,128]{2,1,0:T(8,128)S(1)}, f32[40,8,128]{2,1,0:T(8,128)S(1)}, u32[]{:S(2)}, u32[]{:S(2)}) collective-permute-start(f32[40,8,128]{2,1,0:T(8,128)S(1)} %get-tuple-element.14), channel_id=1, source_target_pairs={{0,16},{16,32},{32,48},{48,64},{64,80},{80,96},{96,112},{112,128},... | collective-permute-start | bytes 491528 | tf_op jit(solution)/shard_map/ppermute | solution.py:534
  19.5 1.9 %collective-permute-start.2 = (f32[40,8,128]{2,1,0:T(8,128)S(1)}, f32[40,8,128]{2,1,0:T(8,128)S(1)}, u32[]{:S(2)}, u32[]{:S(2)}) collective-permute-start(f32[40,8,128]{2,1,0:T(8,128)S(1)} %get-tuple-element.15), channel_id=1, source_target_pairs={{16,0},{32,16},{48,32},{64,48},{80,64},{96,80},{112,96},{128,112},... | collective-permute-start | bytes 491528 | tf_op jit(solution)/shard_map/ppermute | solution.py:535
  21.5 2.4 %collective-permute-done.1.low_ref = f32[40,8,128]{2,1,0:T(8,128)S(1)} collective-permute-done((f32[40,8,128]{2,1,0:T(8,128)S(1)}, f32[40,8,128]{2,1,0:T(8,128)S(1)}, u32[]{:S(2)}, u32[]{:S(2)}) %collective-permute-start.1) | collective-permute-done | bytes 163872 | tf_op jit(solution)/shard_map/ppermute | solution.py:534
  23.9 7.7 %collective-permute-done.2.high_ref = f32[40,8,128]{2,1,0:T(8,128)S(1)} collective-permute-done((f32[40,8,128]{2,1,0:T(8,128)S(1)}, f32[40,8,128]{2,1,0:T(8,128)S(1)}, u32[]{:S(2)}, u32[]{:S(2)}) %collective-permute-start.2) | collective-permute-done | bytes 163872 | tf_op jit(solution)/shard_map/ppermute | solution.py:535
  31.6 0.0 copy-done.1
  31.6 0.0 copy-done.3
  31.6 0.0 copy-done.5
  31.6 1.8 %shard_map.70 = (f32[19,4,8,128]{3,2,1,0:T(8,128)}, f32[4,8,128]{2,1,0:T(8,128)}) custom-call(f32[19,4,8,128]{3,2,1,0:T(8,128)S(1)} %copy-done.1, s32[4,8,128]{2,1,0:T(8,128)S(1)} %copy-done.3, s32[4,8,128]{2,1,0:T(8,128)S(1)} %copy-done.5, f32[21,4,8,128]{3,2,1,0:T(8,128)S(1)} %get-tuple-element.9.own_ref, ...), custom_call_target="tpu_custom_call" | custom-call | tf_op jit(solution)/shard_map/pallas_call | solution.py:502
Async XLA Ops:
  0.6 1.0 %copy-start = (f32[19,4,8,128]{3,2,1,0:T(8,128)S(1)}, f32[19,4,8,128]{3,2,1,0:T(8,128)}, u32[]{:S(2)}) copy-start(f32[19,4,8,128]{3,2,1,0:T(8,128)} %f_ref.1) | copy-start | bytes 933892
  1.6 0.7 %copy-start.2 = (s32[4,8,128]{2,1,0:T(8,128)S(1)}, s32[4,8,128]{2,1,0:T(8,128)}, u32[]{:S(2)}) copy-start(s32[4,8,128]{2,1,0:T(8,128)} %solid_ref.1) | copy-start | bytes 49156
  2.3 0.7 %copy-start.4 = (s32[4,8,128]{2,1,0:T(8,128)S(1)}, s32[4,8,128]{2,1,0:T(8,128)}, u32[]{:S(2)}) copy-start(s32[4,8,128]{2,1,0:T(8,128)} %surface_ref.1) | copy-start | bytes 49156
  3.0 0.7 %copy-start.6 = (f32[4,8,128]{2,1,0:T(8,128)S(1)}, f32[4,8,128]{2,1,0:T(8,128)}, u32[]{:S(2)}) copy-start(f32[4,8,128]{2,1,0:T(8,128)} %porosity_hbm.1) | copy-start | bytes 49156
  3.8 0.7 %copy-start.7 = (f32[4,8,128]{2,1,0:T(8,128)S(1)}, f32[4,8,128]{2,1,0:T(8,128)}, u32[]{:S(2)}) copy-start(f32[4,8,128]{2,1,0:T(8,128)} %weight_hbm.1) | copy-start | bytes 49156
  4.8 8.5 %collective-permute-start = (f32[21,2,8,128]{3,2,1,0:T(8,128)S(1)}, f32[21,2,8,128]{3,2,1,0:T(8,128)S(1)}, u32[]{:S(2)}, u32[]{:S(2)}) collective-permute-start(f32[21,2,8,128]{3,2,1,0:T(8,128)S(1)} %get-tuple-element.10), channel_id=1, source_target_pairs={{1,2},{3,4},{5,6},{7,8},{9,10},{11,12},{13,14},{15,0},{2,1},{4,3},... | collective-permute-start | bytes 516104 | tf_op jit(solution)/shard_map/ppermute | solution.py:527
  13.3 18.3 %copy-start.1 = (f32[19,4,8,128]{3,2,1,0:T(8,128)S(1)}, f32[19,4,8,128]{3,2,1,0:T(8,128)}, u32[]{:S(2)}) copy-start(f32[19,4,8,128]{3,2,1,0:T(8,128)} %f_ref.1) | copy-start | bytes 933892
  13.3 18.3 %copy-start.3 = (s32[4,8,128]{2,1,0:T(8,128)S(1)}, s32[4,8,128]{2,1,0:T(8,128)}, u32[]{:S(2)}) copy-start(s32[4,8,128]{2,1,0:T(8,128)} %solid_ref.1) | copy-start | bytes 49156
  13.3 18.3 %copy-start.5 = (s32[4,8,128]{2,1,0:T(8,128)S(1)}, s32[4,8,128]{2,1,0:T(8,128)}, u32[]{:S(2)}) copy-start(s32[4,8,128]{2,1,0:T(8,128)} %surface_ref.1) | copy-start | bytes 49156
  13.6 10.2 %collective-permute-start.1 = (f32[40,8,128]{2,1,0:T(8,128)S(1)}, f32[40,8,128]{2,1,0:T(8,128)S(1)}, u32[]{:S(2)}, u32[]{:S(2)}) collective-permute-start(f32[40,8,128]{2,1,0:T(8,128)S(1)} %get-tuple-element.14), channel_id=1, source_target_pairs={{0,16},{16,32},{32,48},{48,64},{64,80},{80,96},{96,112},{112,128},... | collective-permute-start | bytes 491528 | tf_op jit(solution)/shard_map/ppermute | solution.py:534
  19.5 12.1 %collective-permute-start.2 = (f32[40,8,128]{2,1,0:T(8,128)S(1)}, f32[40,8,128]{2,1,0:T(8,128)S(1)}, u32[]{:S(2)}, u32[]{:S(2)}) collective-permute-start(f32[40,8,128]{2,1,0:T(8,128)S(1)} %get-tuple-element.15), channel_id=1, source_target_pairs={{16,0},{32,16},{48,32},{64,48},{80,64},{96,80},{112,96},{128,112},... | collective-permute-start | bytes 491528 | tf_op jit(solution)/shard_map/ppermute | solution.py:535

commit v3 on v2

--- a/solution.py
+++ b/solution.py
@@ -513,7 +513,10 @@
     stream, span = lax.axis_size("stream"), lax.axis_size("span")
     tile = (8, 128)
     block, half = (21, 4) + tile, (21, 2) + tile
-    inputs = (checkpoint, porosity, deposit_weight, solid_mask, surface_mask)
+    inputs = tuple(
+        pltpu.with_memory_space_constraint(value, pltpu.HBM)
+        for value in (checkpoint, porosity, deposit_weight, solid_mask, surface_mask)
+    )
     own, mine = call(
         start_kernel,
         inputs,

time: 33.9 us -> 30.7 us (0.906)
  local copies, waits for them, and re-layouts: 3.84 us -> 0.01 us
  Pallas kernels: 2.44 us -> 3.34 us
    unnamed x16 -> x6, local copies, waits for them, and re-layouts: 3.84 us -> 0.01 us
    pallas_call x3, Pallas kernels: 2.44 us -> 3.34 us  [call(): pl.pallas_call(kernel, out_shape=[jax.ShapeDtypeStruct(shape, jnp.float32...]
where the time goes in v3:
time: 30.7 us; the launch traced here: 30.4 us
  waiting for transfers between devices  12.8 us (42%)
  starting transfers between devices  9.98 us (33%)
  blocking collectives  3.61 us (12%)
  Pallas kernels  3.34 us (11%)
  between operations  0.68 us (2%)
    ppermute x1, waiting for transfers between devices, shards(): high = lax.ppermute(down, 'stream', [(i + 1, i) for i in range(stream - 1)])  7.72 us
    ppermute x1, starting transfers between devices, shards(): low = lax.ppermute(up, 'stream', [(i, i + 1) for i in range(stream - 1)])  5.88 us
    all_gather x1, blocking collectives, shards(): both = lax.all_gather(own, 'span', axis_index_groups=cores)  3.61 us
    pallas_call x3, Pallas kernels, call(): pl.pallas_call(kernel, out_shape=[jax.ShapeDtypeStruct(shape, jnp.float32...  3.34 us
    ppermute x1, waiting for transfers between devices, shards(): came = lax.ppermute(mine, 'span', chips + [(b, a) for a, b in chips])  2.67 us
    ppermute x1, waiting for transfers between devices, shards(): low = lax.ppermute(up, 'stream', [(i, i + 1) for i in range(stream - 1)])  2.42 us
    ppermute x1, starting transfers between devices, shards(): came = lax.ppermute(mine, 'span', chips + [(b, a) for a, b in chips])  2.18 us
    ppermute x1, starting transfers between devices, shards(): high = lax.ppermute(down, 'stream', [(i + 1, i) for i in range(stream - 1)])  1.92 us
  transfers between devices with their start and end apart: 3, of which 3 were waited for; matrix products, arithmetic and copies ran while one was open for 0% of the time, Pallas kernels for 0%

profile of v3, /device:TPU:238, one launch (start us, length us, event | category | flops | bytes accessed | tf_op | source)
XLA Modules:
  0.0 30.4 jit_solution(15321061686126554713)
XLA Ops:
  0.6 1.2 %shard_map.68 = (f32[21,4,8,128]{3,2,1,0:T(8,128)S(1)}, f32[21,2,8,128]{3,2,1,0:T(8,128)S(1)}) custom-call(f32[19,4,8,128]{3,2,1,0:T(8,128)} %f_ref.1, f32[4,8,128]{2,1,0:T(8,128)} %porosity_hbm.1, f32[4,8,128]{2,1,0:T(8,128)} %weight_hbm.1, s32[4,8,128]{2,1,0:T(8,128)} %solid_ref.1, s32[4,8,128]{2,1,0:T(8,128)} %surface_ref.1), custom_call_target="tpu_custom_call" | custom-call | tf_op jit(solution)/shard_map/pallas_call | solution.py:502
  1.9 2.2 %collective-permute-start = (f32[21,2,8,128]{3,2,1,0:T(8,128)S(1)}, f32[21,2,8,128]{3,2,1,0:T(8,128)S(1)}, u32[]{:S(2)}, u32[]{:S(2)}) collective-permute-start(f32[21,2,8,128]{3,2,1,0:T(8,128)S(1)} %get-tuple-element.10), channel_id=1, source_target_pairs={{1,2},{3,4},{5,6},{7,8},{9,10},{11,12},{13,14},{15,0},{2,1},{4,3},... | collective-permute-start | bytes 516104 | tf_op jit(solution)/shard_map/ppermute | solution.py:530
  4.0 3.6 %all-gather = f32[42,4,8,128]{3,2,1,0:T(8,128)S(1)} all-gather(f32[21,4,8,128]{3,2,1,0:T(8,128)S(1)} %get-tuple-element.9.own_ref), channel_id=2, replica_groups={{0,1},{2,3},{4,5},{6,7},{8,9},{10,11},{12,13},{14,15},{16,17},{18,19},{..., dimensions={0}, use_global_device_ids=true | all-gather | bytes 1032192 | tf_op jit(solution)/shard_map/all_gather | solution.py:531
  7.7 2.7 %collective-permute-done.half_ref = f32[21,2,8,128]{3,2,1,0:T(8,128)S(1)} collective-permute-done((f32[21,2,8,128]{3,2,1,0:T(8,128)S(1)}, f32[21,2,8,128]{3,2,1,0:T(8,128)S(1)}, u32[]{:S(2)}, u32[]{:S(2)}) %collective-permute-start) | collective-permute-done | bytes 172064 | tf_op jit(solution)/shard_map/ppermute | solution.py:530
  10.3 0.0 copy-start
  10.3 0.0 copy-start.1
  10.3 0.0 copy-start.2
  10.3 0.4 %shard_map.69 = (f32[21,4,8,128]{3,2,1,0:T(8,128)S(1)}, f32[19,2,2,8,128]{4,3,2,1,0:T(8,128)S(1)}, f32[19,2,2,8,128]{4,3,2,1,0:T(8,128)S(1)}, f32[40,8,128]{2,1,0:T(8,128)S(1)}, f32[40,8,128]{2,1,0:T(8,128)S(1)}) custom-call(f32[21,4,8,128]{3,2,1,0:T(8,128)S(1)} %get-tuple-element.9.own_ref, f32[2,21,4,8,128]{4,3,2,1,0:T(8,128)S(1)} %bitcast.1, ...), custom_call_target="tpu_custom_call" | custom-call | tf_op jit(solution)/shard_map/pallas_call | solution.py:502
  10.7 5.9 %collective-permute-start.1 = (f32[40,8,128]{2,1,0:T(8,128)S(1)}, f32[40,8,128]{2,1,0:T(8,128)S(1)}, u32[]{:S(2)}, u32[]{:S(2)}) collective-permute-start(f32[40,8,128]{2,1,0:T(8,128)S(1)} %get-tuple-element.14), channel_id=1, source_target_pairs={{0,16},{16,32},{32,48},{48,64},{64,80},{80,96},{96,112},{112,128},... | collective-permute-start | bytes 491528 | tf_op jit(solution)/shard_map/ppermute | solution.py:537
  16.6 1.9 %collective-permute-start.2 = (f32[40,8,128]{2,1,0:T(8,128)S(1)}, f32[40,8,128]{2,1,0:T(8,128)S(1)}, u32[]{:S(2)}, u32[]{:S(2)}) collective-permute-start(f32[40,8,128]{2,1,0:T(8,128)S(1)} %get-tuple-element.15), channel_id=1, source_target_pairs={{16,0},{32,16},{48,32},{64,48},{80,64},{96,80},{112,96},{128,112},... | collective-permute-start | bytes 491528 | tf_op jit(solution)/shard_map/ppermute | solution.py:538
  18.5 2.4 %collective-permute-done.1.low_ref = f32[40,8,128]{2,1,0:T(8,128)S(1)} collective-permute-done((f32[40,8,128]{2,1,0:T(8,128)S(1)}, f32[40,8,128]{2,1,0:T(8,128)S(1)}, u32[]{:S(2)}, u32[]{:S(2)}) %collective-permute-start.1) | collective-permute-done | bytes 163872 | tf_op jit(solution)/shard_map/ppermute | solution.py:537
  20.9 7.7 %collective-permute-done.2.high_ref = f32[40,8,128]{2,1,0:T(8,128)S(1)} collective-permute-done((f32[40,8,128]{2,1,0:T(8,128)S(1)}, f32[40,8,128]{2,1,0:T(8,128)S(1)}, u32[]{:S(2)}, u32[]{:S(2)}) %collective-permute-start.2) | collective-permute-done | bytes 163872 | tf_op jit(solution)/shard_map/ppermute | solution.py:538
  28.6 0.0 copy-done
  28.6 0.0 copy-done.1
  28.6 0.0 copy-done.2
  28.6 1.8 %shard_map.70 = (f32[19,4,8,128]{3,2,1,0:T(8,128)}, f32[4,8,128]{2,1,0:T(8,128)}) custom-call(f32[19,4,8,128]{3,2,1,0:T(8,128)S(1)} %copy-done, s32[4,8,128]{2,1,0:T(8,128)S(1)} %copy-done.1, s32[4,8,128]{2,1,0:T(8,128)S(1)} %copy-done.2, f32[21,4,8,128]{3,2,1,0:T(8,128)S(1)} %get-tuple-element.9.own_ref, f32[21,4,8,128]{3,2,1,0:T(8,128)S(1)} %get-tuple-element.11.side_ref, ...), custom_call_target="tpu_custom_call" | custom-call | tf_op jit(solution)/shard_map/pallas_call | solution.py:502
Async XLA Ops:
  1.9 8.5 %collective-permute-start = (f32[21,2,8,128]{3,2,1,0:T(8,128)S(1)}, f32[21,2,8,128]{3,2,1,0:T(8,128)S(1)}, u32[]{:S(2)}, u32[]{:S(2)}) collective-permute-start(f32[21,2,8,128]{3,2,1,0:T(8,128)S(1)} %get-tuple-element.10), channel_id=1, source_target_pairs={{1,2},{3,4},{5,6},{7,8},{9,10},{11,12},{13,14},{15,0},{2,1},{4,3},... | collective-permute-start | bytes 516104 | tf_op jit(solution)/shard_map/ppermute | solution.py:530
  10.3 18.3 %copy-start = (f32[19,4,8,128]{3,2,1,0:T(8,128)S(1)}, f32[19,4,8,128]{3,2,1,0:T(8,128)}, u32[]{:S(2)}) copy-start(f32[19,4,8,128]{3,2,1,0:T(8,128)} %f_ref.1) | copy-start | bytes 933892
  10.3 18.3 %copy-start.1 = (s32[4,8,128]{2,1,0:T(8,128)S(1)}, s32[4,8,128]{2,1,0:T(8,128)}, u32[]{:S(2)}) copy-start(s32[4,8,128]{2,1,0:T(8,128)} %solid_ref.1) | copy-start | bytes 49156
  10.3 18.3 %copy-start.2 = (s32[4,8,128]{2,1,0:T(8,128)S(1)}, s32[4,8,128]{2,1,0:T(8,128)}, u32[]{:S(2)}) copy-start(s32[4,8,128]{2,1,0:T(8,128)} %surface_ref.1) | copy-start | bytes 49156
  10.7 10.2 %collective-permute-start.1 = (f32[40,8,128]{2,1,0:T(8,128)S(1)}, f32[40,8,128]{2,1,0:T(8,128)S(1)}, u32[]{:S(2)}, u32[]{:S(2)}) collective-permute-start(f32[40,8,128]{2,1,0:T(8,128)S(1)} %get-tuple-element.14), channel_id=1, source_target_pairs={{0,16},{16,32},{32,48},{48,64},{64,80},{80,96},{96,112},{112,128},... | collective-permute-start | bytes 491528 | tf_op jit(solution)/shard_map/ppermute | solution.py:537
  16.6 12.1 %collective-permute-start.2 = (f32[40,8,128]{2,1,0:T(8,128)S(1)}, f32[40,8,128]{2,1,0:T(8,128)S(1)}, u32[]{:S(2)}, u32[]{:S(2)}) collective-permute-start(f32[40,8,128]{2,1,0:T(8,128)S(1)} %get-tuple-element.15), channel_id=1, source_target_pairs={{16,0},{32,16},{48,32},{64,48},{80,64},{96,80},{112,96},{128,112},... | collective-permute-start | bytes 491528 | tf_op jit(solution)/shard_map/ppermute | solution.py:538

commit v4 on v3

--- a/solution.py
+++ b/solution.py
@@ -50,8 +50,13 @@
 UP = [p for p in range(19) if CX[p] == 1]
 DOWN = [p for p in range(19) if CX[p] == -1]
 FLAT = [p for p in range(19) if CX[p] == 0]
+LEFT = [p for p in range(19) if VEL[p][1] == -1]
+RIGHT = [p for p in range(19) if VEL[p][1] == 1]
+ALONG = [p for p in range(19) if VEL[p][1] == 0]
 OPP = [0] + [p + 1 if p % 2 else p - 1 for p in range(1, 19)]
 BLEND, WEIGHT = 19, 20
+SPAN_WIDE = 15
+SPAN_TILES = 2 * SPAN_WIDE + 6
 STATE, MOMENTS, NEAR_BLEND, WIDE = 0, 5, 9, 10
 SUM_FAR, SUM_NEAR, SUM_OWN, WEIGHT_FAR, WEIGHT_NEAR, LAYERS = 10, 14, 18, 21, 22, 23
 TILES = LAYERS + WIDE + (LAYERS - WIDE + 1) // 2
@@ -212,11 +217,20 @@
         ref[LAYERS + WIDE + (i - WIDE) // 2] = tile
 
 
-def get_message(ref, i):
+def get_message(read, i):
     if i < WIDE:
-        return (ref[i], ref[LAYERS + i])
-    tile = ref[LAYERS + WIDE + (i - WIDE) // 2]
-    return (ref[i], pltpu.roll(tile, 4, 0) if (i - WIDE) % 2 else tile)
+        return (read(i), read(LAYERS + i))
+    tile = read(LAYERS + WIDE + (i - WIDE) // 2)
+    return (read(i), pltpu.roll(tile, 4, 0) if (i - WIDE) % 2 else tile)
+
+
+def wide_layers(core):
+    towards = [jnp.where(core == 0, a, b) for a, b in zip(LEFT, RIGHT)]
+    return towards + ALONG + [BLEND]
+
+
+def narrow_layers(core):
+    return [jnp.where(core == 0, b, a) for a, b in zip(LEFT, RIGHT)] + [WEIGHT]
 
 
 def start_kernel(
@@ -250,21 +264,36 @@
             own_ref[p, x] = out[p]
         own_ref[BLEND, x] = blend
         own_ref[WEIGHT, x] = weight_ref[x]
-    for layer in range(21):
+    at = sublane(own_ref[0, 0])
+    low = (at < 4) == (core == 0)
+    for i, layer in enumerate(wide_layers(core)):
         for pair in range(2):
             first, second = own_ref[layer, 2 * pair], own_ref[layer, 2 * pair + 1]
-            low = (sublane(first) < 4) == (core == 0)
-            half_ref[layer, pair] = jnp.where(low, first, pltpu.roll(second, 4, 0))
-
-
-def inner_kernel(own_ref, both_ref, half_ref, side_ref, state_ref, next_ref, up_ref, down_ref):
+            half_ref[2 * i + pair] = jnp.where(low, first, pltpu.roll(second, 4, 0))
+    for i, layer in enumerate(narrow_layers(core)):
+        tile = own_ref[layer, 0]
+        for x in range(1, 4):
+            here = lax.rem(at + 8 - 2 * x + 2 * core, 8) < 2
+            tile = jnp.where(here, pltpu.roll(own_ref[layer, x], 2 * x, 0), tile)
+        half_ref[2 * SPAN_WIDE + i] = tile
+
+
+def inner_kernel(
+    own_ref, both_ref, half_ref, side_ref, state_ref, next_ref, odd_ref, even_ref, message_ref
+):
     core = lax.rem(lax.axis_index("span"), 2)
-    for layer in range(21):
-        for pair in range(2):
-            came = half_ref[layer, pair]
-            low = (sublane(came) < 4) == (core == 0)
-            for x, tile in ((2 * pair, came), (2 * pair + 1, pltpu.roll(came, 4, 0))):
-                side_ref[layer, x] = jnp.where(low, both_ref[1 - core, layer, x], tile)
+    odd = lax.rem(lax.axis_index("stream"), 2)
+    low = (sublane(half_ref[0]) < 4) == (core == 0)
+    for i, layer in enumerate(wide_layers(1 - core)):
+        for x in range(4):
+            tile = half_ref[2 * i + x // 2]
+            tile = pltpu.roll(tile, 4, 0) if x % 2 else tile
+            side_ref[layer, x] = jnp.where(low, both_ref[1 - core, layer, x], tile)
+    for i, layer in enumerate(narrow_layers(1 - core)):
+        for x in range(4):
+            tile = half_ref[2 * SPAN_WIDE + i]
+            tile = pltpu.roll(tile, 8 - 2 * x, 0) if x else tile
+            side_ref[layer, x] = jnp.where(low, both_ref[1 - core, layer, x], tile)
 
     def c0(p, x):
         return (own_ref[p, x], side_ref[p, x])
@@ -285,10 +314,7 @@
     def c1(p, x):
         return (next_ref[p, x - 1, 0], next_ref[p, x - 1, 1])
 
-    for ref, near, far, inward, outward in (
-        (up_ref, 3, 2, UP, DOWN),
-        (down_ref, 0, 1, DOWN, UP),
-    ):
+    for side, near, far, inward, outward in ((0, 3, 2, UP, DOWN), (1, 0, 1, DOWN, UP)):
         step = far - near
         enter = [moved(p, c0(p, near)) for p in inward]
         known = {p: moved(p, c0(p, near if p in FLAT else far)) for p in inward + FLAT}
@@ -319,19 +345,30 @@
         layers[SUM_OWN : SUM_OWN + 3] = list(zip(*halves))
         layers[WEIGHT_FAR] = c0(WEIGHT, far)
         layers[WEIGHT_NEAR] = c0(WEIGHT, near)
-        put_message(ref, layers)
+        put_message(message_ref.at[side], layers)
+    for i in range(TILES):
+        odd_ref[i] = message_ref[1 - odd, i]
+        even_ref[i] = message_ref[odd, i]
 
 
 def last_kernel(
-    f_ref, solid_ref, surface_ref, own_ref, side_ref, state_ref, next_ref, low_ref, high_ref,
+    f_ref, solid_ref, surface_ref, own_ref, side_ref, state_ref, next_ref, odd_ref, even_ref,
     adjoint_ref, sensitivity_ref, s1_ref, c1_ref, sum_ref, flow_ref, a1_ref, field_ref,
 ):
     place = lax.axis_index("stream")
     at_start = place == 0
     at_end = place == lax.axis_size("stream") - 1
+    odd = lax.rem(place, 2)
+
+    def low(i):
+        return jnp.where(odd == 1, even_ref[1 - odd, i], odd_ref[i])
+
+    def high(i):
+        return jnp.where(odd == 1, odd_ref[i], even_ref[1 - odd, i])
+
     ends = (
-        (low_ref, at_start, 0, -1, UP, DOWN),
-        (high_ref, at_end, 3, 1, DOWN, UP),
+        (low, at_start, 0, -1, UP, DOWN),
+        (high, at_end, 3, 1, DOWN, UP),
     )
 
     def moved(p, pair, fill=None):
@@ -345,11 +382,11 @@
             for t in range(2):
                 s1_ref[p, x, t] = state_ref[p, x - 1, t]
                 c1_ref[p, x, t] = next_ref[p, x - 1, t]
-    for ref, end, x, out, inward, outward in ends:
+    for read, end, x, out, inward, outward in ends:
         f = {p: moved(p, c0(p, x if p in FLAT else x - out)) for p in FLAT + outward}
         for i, p in enumerate(inward):
             f[p] = tuple(
-                jnp.where(end, GHOST[p], part) for part in get_message(ref, STATE + i)
+                jnp.where(end, GHOST[p], part) for part in get_message(read, STATE + i)
             )
         blend = c0(BLEND, x)
         for t in range(2):
@@ -370,8 +407,8 @@
             value = weight * value
             field_ref[i, x + 2, t] = value if end is None else jnp.where(end, 0.0, value)
 
-    for side, (ref, end, x, out, inward, outward) in enumerate(ends):
-        sent = [get_message(ref, i) for i in range(LAYERS)]
+    for side, (read, end, x, out, inward, outward) in enumerate(ends):
+        sent = [get_message(read, i) for i in range(LAYERS)]
         blend = sent[NEAR_BLEND]
         leaving = {p: moved(p, c0(p, x)) for p in outward}
         to_far, to_near, to_own = {}, {}, {}
@@ -469,9 +506,9 @@
                 a1_ref[p, x + 1, t] = value
             if part is not None:
                 sensitivity_ref[x] = part
-    for side, (ref, end, x, out, inward, outward) in enumerate(ends):
+    for side, (read, end, x, out, inward, outward) in enumerate(ends):
         h = [cotangent(p, x + out) for p in range(19)]
-        blend = get_message(ref, NEAR_BLEND)
+        blend = get_message(read, NEAR_BLEND)
         for t in range(2):
             u = [flow_ref[side, i, t] for i in range(3)]
             wanted = [p for p in outward if t == 0 or VEL[p][1] != 0]
@@ -512,7 +549,7 @@
 def shards(checkpoint, porosity, deposit_weight, solid_mask, surface_mask):
     stream, span = lax.axis_size("stream"), lax.axis_size("span")
     tile = (8, 128)
-    block, half = (21, 4) + tile, (21, 2) + tile
+    block, half = (21, 4) + tile, (SPAN_TILES,) + tile
     inputs = tuple(
         pltpu.with_memory_space_constraint(value, pltpu.HBM)
         for value in (checkpoint, porosity, deposit_weight, solid_mask, surface_mask)
@@ -531,15 +568,22 @@
     both = lax.all_gather(own, "span", axis_index_groups=cores)
     rows = (19, 2, 2) + tile
     message = (TILES,) + tile
-    side, state, following, up, down = call(
-        inner_kernel, (own, both, came), [block, rows, rows, message, message]
-    )
-    low = lax.ppermute(up, "stream", [(i, i + 1) for i in range(stream - 1)])
-    high = lax.ppermute(down, "stream", [(i + 1, i) for i in range(stream - 1)])
+    side, state, following, first, second = call(
+        inner_kernel,
+        (own, both, came),
+        [block, rows, rows, message, message],
+        [pltpu.VMEM((2,) + message, jnp.float32)],
+    )
+
+    pairs = [(i, i + 1) for i in range(1, stream - 1, 2)]
+    odd = lax.ppermute(first, "stream", pairs + [(b, a) for a, b in pairs])
+    even = lax.all_gather(
+        second, "stream", axis_index_groups=[[i, i + 1] for i in range(0, stream, 2)]
+    )
     scratch = [(19, 4, 2), (19, 4, 2), (2, 4, 2), (2, 4, 2), (19, 6, 2), (4, 8, 2)]
     adjoint, sensitivity = call(
         last_kernel,
-        (checkpoint, solid_mask, surface_mask, own, side, state, following, low, high),
+        (checkpoint, solid_mask, surface_mask, own, side, state, following, odd, even),
         [(19, 4) + tile, (4,) + tile],
         [pltpu.VMEM(shape + tile, jnp.float32) for shape in scratch],
     )

time: 30.7 us -> 28.5 us (0.928)
  the two profiles are of different devices: /device:TPU:238 before, /device:TPU:395 now
where the time goes in v4:
time: 28.5 us; the launch traced here: 28.2 us
  blocking collectives  12.1 us (42%)
  starting transfers between devices  9.27 us (33%)
  Pallas kernels  3.4 us (12%)
  waiting for transfers between devices  2.8 us (10%)
  between operations  0.69 us (2%)
    all_gather x1, blocking collectives, shards(): lax.all_gather(second, 'stream', axis_index_groups=[[i, i + 1] for i in r...  9.75 us
    ppermute x1, starting transfers between devices, shards(): odd = lax.ppermute(first, 'stream', pairs + [(b, a) for a, b in pairs])  5.54 us
    ppermute x1, starting transfers between devices, shards(): came = lax.ppermute(mine, 'span', chips + [(b, a) for a, b in chips])  3.74 us
    pallas_call x3, Pallas kernels, call(): pl.pallas_call(kernel, out_shape=[jax.ShapeDtypeStruct(shape, jnp.float32...  3.4 us
    ppermute x1, waiting for transfers between devices, shards(): came = lax.ppermute(mine, 'span', chips + [(b, a) for a, b in chips])  2.79 us
    all_gather x1, blocking collectives, shards(): both = lax.all_gather(own, 'span', axis_index_groups=cores)  2.3 us
  transfers between devices with their start and end apart: 2, of which 1 were waited for; matrix products, arithmetic and copies ran while one was open for 0% of the time, Pallas kernels for 0%

profile of v4, /device:TPU:395, one launch (start us, length us, event | category | flops | bytes accessed | tf_op | source)
XLA Modules:
  0.0 28.2 jit_solution(13661270344696732887)
XLA Ops:
  0.6 1.2 %shard_map.68 = (f32[21,4,8,128]{3,2,1,0:T(8,128)S(1)}, f32[36,8,128]{2,1,0:T(8,128)S(1)}) custom-call(f32[19,4,8,128]{3,2,1,0:T(8,128)} %f_ref.1, f32[4,8,128]{2,1,0:T(8,128)} %porosity_hbm.1, f32[4,8,128]{2,1,0:T(8,128)} %weight_hbm.1, s32[4,8,128]{2,1,0:T(8,128)} %solid_ref.1, s32[4,8,128]{2,1,0:T(8,128)} %surface_ref.1), custom_call_target="tpu_custom_call" | custom-call | tf_op jit(solution)/shard_map/pallas_call | solution.py:539
  1.9 3.7 %collective-permute-start = (f32[36,8,128]{2,1,0:T(8,128)S(1)}, f32[36,8,128]{2,1,0:T(8,128)S(1)}, u32[]{:S(2)}, u32[]{:S(2)}) collective-permute-start(f32[36,8,128]{2,1,0:T(8,128)S(1)} %get-tuple-element.10), channel_id=1, source_target_pairs={{1,2},{3,4},{5,6},{7,8},{9,10},{11,12},{13,14},{15,0},{2,1},{4,3},... | collective-permute-start | bytes 442376 | tf_op jit(solution)/shard_map/ppermute | solution.py:567
  5.6 2.3 %all-gather = f32[42,4,8,128]{3,2,1,0:T(8,128)S(1)} all-gather(f32[21,4,8,128]{3,2,1,0:T(8,128)S(1)} %get-tuple-element.9.own_ref), channel_id=2, replica_groups={{0,1},{2,3},{4,5},{6,7},{8,9},{10,11},{12,13},{14,15},{16,17},{18,19},{..., dimensions={0}, use_global_device_ids=true | all-gather | bytes 1032192 | tf_op jit(solution)/shard_map/all_gather | solution.py:568
  7.9 2.8 %collective-permute-done.half_ref = f32[36,8,128]{2,1,0:T(8,128)S(1)} collective-permute-done((f32[36,8,128]{2,1,0:T(8,128)S(1)}, f32[36,8,128]{2,1,0:T(8,128)S(1)}, u32[]{:S(2)}, u32[]{:S(2)}) %collective-permute-start) | collective-permute-done | bytes 147488 | tf_op jit(solution)/shard_map/ppermute | solution.py:567
  10.7 0.4 %shard_map.69 = (f32[21,4,8,128]{3,2,1,0:T(8,128)S(1)}, f32[19,2,2,8,128]{4,3,2,1,0:T(8,128)S(1)}, f32[19,2,2,8,128]{4,3,2,1,0:T(8,128)S(1)}, f32[40,8,128]{2,1,0:T(8,128)S(1)}, f32[40,8,128]{2,1,0:T(8,128)S(1)}) custom-call(f32[21,4,8,128]{3,2,1,0:T(8,128)S(1)} %get-tuple-element.9.own_ref, f32[2,21,4,8,128]{4,3,2,1,0:T(8,128)S(1)} %bitcast.2, ...), custom_call_target="tpu_custom_call" | custom-call | tf_op jit(solution)/shard_map/pallas_call | solution.py:539
  11.1 0.0 copy-start
  11.1 5.5 %collective-permute-start.1 = (f32[40,8,128]{2,1,0:T(8,128)S(1)}, f32[40,8,128]{2,1,0:T(8,128)S(1)}, u32[]{:S(2)}, u32[]{:S(2)}) collective-permute-start(f32[40,8,128]{2,1,0:T(8,128)S(1)} %get-tuple-element.14), channel_id=1, source_target_pairs={{16,32},{48,64},{80,96},{112,128},{144,160},{176,192},{208,224},{2... | collective-permute-start | bytes 491528 | tf_op jit(solution)/shard_map/ppermute | solution.py:579
  16.7 0.0 copy-start.1
  16.7 0.0 copy-start.2
  16.7 9.8 %all-gather.1 = f32[80,8,128]{2,1,0:T(8,128)S(1)} all-gather(f32[40,8,128]{2,1,0:T(8,128)S(1)} %get-tuple-element.15), channel_id=3, replica_groups={{0,16},{32,48},{64,80},{96,112},{128,144},{160,176},{192,208},{224,240}..., dimensions={0}, use_global_device_ids=true | all-gather | bytes 491520 | tf_op jit(solution)/shard_map/all_gather | solution.py:580
  26.5 0.0 collective-permute-done.1.odd_ref
  26.5 0.0 copy-done
  26.5 0.0 copy-done.1
  26.5 0.0 copy-done.2
  26.5 1.8 %shard_map.70 = (f32[19,4,8,128]{3,2,1,0:T(8,128)}, f32[4,8,128]{2,1,0:T(8,128)}) custom-call(f32[19,4,8,128]{3,2,1,0:T(8,128)S(1)} %copy-done, s32[4,8,128]{2,1,0:T(8,128)S(1)} %copy-done.1, s32[4,8,128]{2,1,0:T(8,128)S(1)} %copy-done.2, f32[21,4,8,128]{3,2,1,0:T(8,128)S(1)} %get-tuple-element.9.own_ref, f32[21,4,8,128]{3,2,1,0:T(8,128)S(1)} %get-tuple-element.11.side_ref, ...), custom_call_target="tpu_custom_call" | custom-call | tf_op jit(solution)/shard_map/pallas_call | solution.py:539
Async XLA Ops:
  1.9 8.8 %collective-permute-start = (f32[36,8,128]{2,1,0:T(8,128)S(1)}, f32[36,8,128]{2,1,0:T(8,128)S(1)}, u32[]{:S(2)}, u32[]{:S(2)}) collective-permute-start(f32[36,8,128]{2,1,0:T(8,128)S(1)} %get-tuple-element.10), channel_id=1, source_target_pairs={{1,2},{3,4},{5,6},{7,8},{9,10},{11,12},{13,14},{15,0},{2,1},{4,3},... | collective-permute-start | bytes 442376 | tf_op jit(solution)/shard_map/ppermute | solution.py:567
  11.1 15.3 %copy-start = (f32[19,4,8,128]{3,2,1,0:T(8,128)S(1)}, f32[19,4,8,128]{3,2,1,0:T(8,128)}, u32[]{:S(2)}) copy-start(f32[19,4,8,128]{3,2,1,0:T(8,128)} %f_ref.1) | copy-start | bytes 933892
  11.1 15.3 %collective-permute-start.1 = (f32[40,8,128]{2,1,0:T(8,128)S(1)}, f32[40,8,128]{2,1,0:T(8,128)S(1)}, u32[]{:S(2)}, u32[]{:S(2)}) collective-permute-start(f32[40,8,128]{2,1,0:T(8,128)S(1)} %get-tuple-element.14), channel_id=1, source_target_pairs={{16,32},{48,64},{80,96},{112,128},{144,160},{176,192},{208,224},{2... | collective-permute-start | bytes 491528 | tf_op jit(solution)/shard_map/ppermute | solution.py:579
  16.7 9.8 %copy-start.1 = (s32[4,8,128]{2,1,0:T(8,128)S(1)}, s32[4,8,128]{2,1,0:T(8,128)}, u32[]{:S(2)}) copy-start(s32[4,8,128]{2,1,0:T(8,128)} %solid_ref.1) | copy-start | bytes 49156
  16.7 9.8 %copy-start.2 = (s32[4,8,128]{2,1,0:T(8,128)S(1)}, s32[4,8,128]{2,1,0:T(8,128)}, u32[]{:S(2)}) copy-start(s32[4,8,128]{2,1,0:T(8,128)} %surface_ref.1) | copy-start | bytes 49156

commit v5 on v4

--- a/solution.py
+++ b/solution.py
@@ -59,7 +59,8 @@
 SPAN_TILES = 2 * SPAN_WIDE + 6
 STATE, MOMENTS, NEAR_BLEND, WIDE = 0, 5, 9, 10
 SUM_FAR, SUM_NEAR, SUM_OWN, WEIGHT_FAR, WEIGHT_NEAR, LAYERS = 10, 14, 18, 21, 22, 23
-TILES = LAYERS + WIDE + (LAYERS - WIDE + 1) // 2
+INSET = WIDE // 2
+TILES = LAYERS + WIDE + (LAYERS - WIDE - INSET + 1) // 2
 
 
 def sublane(tile):
@@ -207,21 +208,29 @@
 def put_message(ref, layers):
     for i, pair in enumerate(layers):
         ref[i] = pair[0]
+    at = sublane(layers[0][1])
     for i in range(WIDE):
-        ref[LAYERS + i] = layers[i][1]
-    for i in range(WIDE, LAYERS, 2):
+        tile = layers[i][1]
+        if i // 2 < INSET:
+            inset = pltpu.roll(layers[WIDE + i // 2][1], 5 if i % 2 else 3, 0)
+            tile = jnp.where((at == 3) | (at == 4), inset, tile)
+        ref[LAYERS + i] = tile
+    for i in range(WIDE + INSET, LAYERS, 2):
         tile = layers[i][1]
         if i + 1 < LAYERS:
-            at = sublane(tile)
             tile = jnp.where((at < 2) | (at > 5), tile, pltpu.roll(layers[i + 1][1], 4, 0))
-        ref[LAYERS + WIDE + (i - WIDE) // 2] = tile
+        ref[LAYERS + WIDE + (i - WIDE - INSET) // 2] = tile
 
 
 def get_message(read, i):
     if i < WIDE:
         return (read(i), read(LAYERS + i))
-    tile = read(LAYERS + WIDE + (i - WIDE) // 2)
-    return (read(i), pltpu.roll(tile, 4, 0) if (i - WIDE) % 2 else tile)
+    if i < WIDE + INSET:
+        first, second = (read(LAYERS + 2 * (i - WIDE) + k) for k in range(2))
+        first, second = pltpu.roll(first, 5, 0), pltpu.roll(second, 3, 0)
+        return (read(i), jnp.where(sublane(first) < 4, first, second))
+    tile = read(LAYERS + WIDE + (i - WIDE - INSET) // 2)
+    return (read(i), pltpu.roll(tile, 4, 0) if (i - WIDE - INSET) % 2 else tile)
 
 
 def wide_layers(core):
@@ -237,7 +246,7 @@
     f_hbm, porosity_hbm, weight_hbm, solid_hbm, surface_hbm, own_ref, half_ref,
     f_ref, porosity_ref, weight_ref, solid_ref, surface_ref, sems,
 ):
-    copies = [
+    small = [
         pltpu.make_async_copy(source, target, sems.at[i])
         for i, (source, target) in enumerate(
             (
@@ -245,31 +254,34 @@
                 (surface_hbm, surface_ref),
                 (porosity_hbm, porosity_ref),
                 (weight_hbm, weight_ref),
-                (f_hbm, f_ref),
             )
         )
     ]
-    for copy in copies:
+    rows = [
+        pltpu.make_async_copy(f_hbm.at[:, x], f_ref.at[:, x], sems.at[4 + x]) for x in range(4)
+    ]
+    for copy in rows[:1] + small + rows[1:]:
         copy.start()
-    for copy in copies:
+    core = lax.rem(lax.axis_index("span"), 2)
+    at = lax.broadcasted_iota(jnp.int32, (8, 128), 0)
+    low = (at < 4) == (core == 0)
+    for copy in small:
         copy.wait()
-    core = lax.rem(lax.axis_index("span"), 2)
     for x in range(4):
         porosity = porosity_ref[x]
         blend = jnp.where(
             solid_ref[x] == 1, 1.0, jnp.where(surface_ref[x] == 1, porosity, 0.0)
         )
+        rows[x].wait()
         out = collide([f_ref[p, x] for p in range(19)], blend)
         for p in range(19):
             own_ref[p, x] = out[p]
         own_ref[BLEND, x] = blend
         own_ref[WEIGHT, x] = weight_ref[x]
-    at = sublane(own_ref[0, 0])
-    low = (at < 4) == (core == 0)
-    for i, layer in enumerate(wide_layers(core)):
-        for pair in range(2):
-            first, second = own_ref[layer, 2 * pair], own_ref[layer, 2 * pair + 1]
-            half_ref[2 * i + pair] = jnp.where(low, first, pltpu.roll(second, 4, 0))
+        if x % 2:
+            for i, layer in enumerate(wide_layers(core)):
+                first, second = own_ref[layer, x - 1], own_ref[layer, x]
+                half_ref[2 * i + x // 2] = jnp.where(low, first, pltpu.roll(second, 4, 0))
     for i, layer in enumerate(narrow_layers(core)):
         tile = own_ref[layer, 0]
         for x in range(1, 4):
@@ -353,7 +365,8 @@
 
 def last_kernel(
     f_ref, solid_ref, surface_ref, own_ref, side_ref, state_ref, next_ref, odd_ref, even_ref,
-    adjoint_ref, sensitivity_ref, s1_ref, c1_ref, sum_ref, flow_ref, a1_ref, field_ref,
+    adjoint_hbm, sensitivity_hbm, adjoint_ref, sensitivity_ref,
+    s1_ref, c1_ref, sum_ref, flow_ref, a1_ref, field_ref, sems,
 ):
     place = lax.axis_index("stream")
     at_start = place == 0
@@ -377,11 +390,6 @@
     def c0(p, x):
         return (own_ref[p, x], side_ref[p, x])
 
-    for x in (1, 2):
-        for p in range(19):
-            for t in range(2):
-                s1_ref[p, x, t] = state_ref[p, x - 1, t]
-                c1_ref[p, x, t] = next_ref[p, x - 1, t]
     for read, end, x, out, inward, outward in ends:
         f = {p: moved(p, c0(p, x if p in FLAT else x - out)) for p in FLAT + outward}
         for i, p in enumerate(inward):
@@ -393,11 +401,15 @@
             tiles = [f[p][t] for p in range(19)]
             after = collide(tiles, blend[t])
             for p in range(19):
-                s1_ref[p, x, t] = tiles[p]
-                c1_ref[p, x, t] = after[p]
+                s1_ref[p, x // 3, t] = tiles[p]
+                c1_ref[p, x // 3, t] = after[p]
+
+    def s1(p, x, t):
+        return state_ref[p, x - 1, t] if x in (1, 2) else s1_ref[p, x // 3, t]
 
     def c1(p, x):
-        return (c1_ref[p, x, 0], c1_ref[p, x, 1])
+        ref, at = (next_ref, x - 1) if x in (1, 2) else (c1_ref, x // 3)
+        return (ref[p, at, 0], ref[p, at, 1])
 
     def save_field(x, t, total, weight, end=None):
         inverse = 1.0 / total[0]
@@ -496,7 +508,7 @@
         for t in range(2):
             wanted = [p for p in range(19) if t == 0 or VEL[p][1] != 0]
             out, part = adjoint_collide(
-                [s1_ref[p, x, t] for p in range(19)],
+                [s1(p, x, t) for p in range(19)],
                 blend[t],
                 [h[p][t] for p in range(19)],
                 wanted,
@@ -518,6 +530,7 @@
             for p, value in got.items():
                 a1_ref[p, x + out + 1, t] = jnp.where(end, 0.0, value)
 
+    sent = []
     for x in range(4):
         h = []
         for p in range(19):
@@ -531,16 +544,24 @@
         )
         for p in range(19):
             adjoint_ref[p, x] = out[p]
+        sent.append(
+            pltpu.make_async_copy(adjoint_ref.at[:, x], adjoint_hbm.at[:, x], sems.at[x])
+        )
+        sent[x].start()
         design = (solid_ref[x] == 0) & (surface_ref[x] == 1)
         sensitivity_ref[x] = jnp.where(design, sensitivity_ref[x] + part, 0.0)
-
-
-def call(kernel, inputs, shapes, scratch=(), space=pltpu.VMEM):
+    sent.append(pltpu.make_async_copy(sensitivity_ref, sensitivity_hbm, sems.at[4]))
+    sent[4].start()
+    for copy in sent:
+        copy.wait()
+
+
+def call(kernel, inputs, shapes, scratch=(), space=pltpu.VMEM, result=pltpu.VMEM):
     return pl.pallas_call(
         kernel,
         out_shape=[jax.ShapeDtypeStruct(shape, jnp.float32) for shape in shapes],
         in_specs=[pl.BlockSpec(memory_space=space)] * len(inputs),
-        out_specs=[pl.BlockSpec(memory_space=pltpu.VMEM)] * len(shapes),
+        out_specs=[pl.BlockSpec(memory_space=result)] * len(shapes),
         scratch_shapes=scratch,
         compiler_params=pltpu.CompilerParams(vmem_limit_bytes=24 * 1024 * 1024),
     )(*inputs)
@@ -559,7 +580,7 @@
         inputs,
         [block, half],
         [pltpu.VMEM(value.shape, value.dtype) for value in inputs]
-        + [pltpu.SemaphoreType.DMA((5,))],
+        + [pltpu.SemaphoreType.DMA((8,))],
         pltpu.HBM,
     )
     cores = [[i, i + 1] for i in range(0, span, 2)]
@@ -580,12 +601,16 @@
     even = lax.all_gather(
         second, "stream", axis_index_groups=[[i, i + 1] for i in range(0, stream, 2)]
     )
-    scratch = [(19, 4, 2), (19, 4, 2), (2, 4, 2), (2, 4, 2), (19, 6, 2), (4, 8, 2)]
+    scratch = [
+        (19, 4), (4,), (19, 2, 2), (19, 2, 2), (2, 4, 2), (2, 4, 2), (19, 6, 2), (4, 8, 2),
+    ]
     adjoint, sensitivity = call(
         last_kernel,
         (checkpoint, solid_mask, surface_mask, own, side, state, following, odd, even),
         [(19, 4) + tile, (4,) + tile],
-        [pltpu.VMEM(shape + tile, jnp.float32) for shape in scratch],
+        [pltpu.VMEM(shape + tile, jnp.float32) for shape in scratch]
+        + [pltpu.SemaphoreType.DMA((5,))],
+        result=pl.ANY,
     )
     return (adjoint, sensitivity)
 

time: 28.5 us -> 28.3 us (level)
  the two profiles are of different devices: /device:TPU:395 before, /device:TPU:384 now
where the time goes in v5:
time: 28.3 us; the launch traced here: 28.1 us
  starting transfers between devices  12 us (42%)
  blocking collectives  9.67 us (34%)
  Pallas kernels  3.39 us (12%)
  waiting for transfers between devices  2.25 us (8%)
  between operations  0.69 us (2%)
    all_gather x1, blocking collectives, shards(): lax.all_gather(second, 'stream', axis_index_groups=[[i, i + 1] for i in r...  7.37 us
    ppermute x1, starting transfers between devices, shards(): odd = lax.ppermute(first, 'stream', pairs + [(b, a) for a, b in pairs])  6.76 us
    ppermute x1, starting transfers between devices, shards(): came = lax.ppermute(mine, 'span', chips + [(b, a) for a, b in chips])  5.29 us
    pallas_call x3, Pallas kernels, call(): pl.pallas_call(kernel, out_shape=[jax.ShapeDtypeStruct(shape, jnp.float32...  3.39 us
    all_gather x1, blocking collectives, shards(): both = lax.all_gather(own, 'span', axis_index_groups=cores)  2.3 us
    ppermute x1, waiting for transfers between devices, shards(): came = lax.ppermute(mine, 'span', chips + [(b, a) for a, b in chips])  2.25 us
  transfers between devices with their start and end apart: 2, of which 1 were waited for; matrix products, arithmetic and copies ran while one was open for 0% of the time, Pallas kernels for 0%

profile of v5, /device:TPU:384, one launch (start us, length us, event | category | flops | bytes accessed | tf_op | source)
XLA Modules:
  0.0 28.1 jit_solution(14617363793108591971)
XLA Ops:
  0.6 1.2 %shard_map.68 = (f32[21,4,8,128]{3,2,1,0:T(8,128)S(1)}, f32[36,8,128]{2,1,0:T(8,128)S(1)}) custom-call(f32[19,4,8,128]{3,2,1,0:T(8,128)} %f_ref.1, f32[4,8,128]{2,1,0:T(8,128)} %porosity_hbm.1, f32[4,8,128]{2,1,0:T(8,128)} %weight_hbm.1, s32[4,8,128]{2,1,0:T(8,128)} %solid_ref.1, s32[4,8,128]{2,1,0:T(8,128)} %surface_ref.1), custom_call_target="tpu_custom_call" | custom-call | tf_op jit(solution)/shard_map/pallas_call | solution.py:560
  1.8 5.3 %collective-permute-start = (f32[36,8,128]{2,1,0:T(8,128)S(1)}, f32[36,8,128]{2,1,0:T(8,128)S(1)}, u32[]{:S(2)}, u32[]{:S(2)}) collective-permute-start(f32[36,8,128]{2,1,0:T(8,128)S(1)} %get-tuple-element.10), channel_id=1, source_target_pairs={{1,2},{3,4},{5,6},{7,8},{9,10},{11,12},{13,14},{15,0},{2,1},{4,3},... | collective-permute-start | bytes 442376 | tf_op jit(solution)/shard_map/ppermute | solution.py:588
  7.1 2.3 %all-gather = f32[42,4,8,128]{3,2,1,0:T(8,128)S(1)} all-gather(f32[21,4,8,128]{3,2,1,0:T(8,128)S(1)} %get-tuple-element.9.own_ref), channel_id=2, replica_groups={{0,1},{2,3},{4,5},{6,7},{8,9},{10,11},{12,13},{14,15},{16,17},{18,19},{..., dimensions={0}, use_global_device_ids=true | all-gather | bytes 1032192 | tf_op jit(solution)/shard_map/all_gather | solution.py:589
  9.4 2.2 %collective-permute-done.half_ref = f32[36,8,128]{2,1,0:T(8,128)S(1)} collective-permute-done((f32[36,8,128]{2,1,0:T(8,128)S(1)}, f32[36,8,128]{2,1,0:T(8,128)S(1)}, u32[]{:S(2)}, u32[]{:S(2)}) %collective-permute-start) | collective-permute-done | bytes 147488 | tf_op jit(solution)/shard_map/ppermute | solution.py:588
  11.7 0.4 %shard_map.69 = (f32[21,4,8,128]{3,2,1,0:T(8,128)S(1)}, f32[19,2,2,8,128]{4,3,2,1,0:T(8,128)S(1)}, f32[19,2,2,8,128]{4,3,2,1,0:T(8,128)S(1)}, f32[37,8,128]{2,1,0:T(8,128)S(1)}, f32[37,8,128]{2,1,0:T(8,128)S(1)}) custom-call(f32[21,4,8,128]{3,2,1,0:T(8,128)S(1)} %get-tuple-element.9.own_ref, f32[2,21,4,8,128]{4,3,2,1,0:T(8,128)S(1)} %bitcast.2, ...), custom_call_target="tpu_custom_call" | custom-call | tf_op jit(solution)/shard_map/pallas_call | solution.py:560
  12.1 0.0 copy-start
  12.2 6.8 %collective-permute-start.1 = (f32[37,8,128]{2,1,0:T(8,128)S(1)}, f32[37,8,128]{2,1,0:T(8,128)S(1)}, u32[]{:S(2)}, u32[]{:S(2)}) collective-permute-start(f32[37,8,128]{2,1,0:T(8,128)S(1)} %get-tuple-element.14), channel_id=1, source_target_pairs={{16,32},{48,64},{80,96},{112,128},{144,160},{176,192},{208,224},{2... | collective-permute-start | bytes 454664 | tf_op jit(solution)/shard_map/ppermute | solution.py:600
  18.9 0.0 copy-start.1
  18.9 0.0 copy-start.2
  18.9 7.4 %all-gather.1 = f32[74,8,128]{2,1,0:T(8,128)S(1)} all-gather(f32[37,8,128]{2,1,0:T(8,128)S(1)} %get-tuple-element.15), channel_id=3, replica_groups={{0,16},{32,48},{64,80},{96,112},{128,144},{160,176},{192,208},{224,240}..., dimensions={0}, use_global_device_ids=true | all-gather | bytes 454656 | tf_op jit(solution)/shard_map/all_gather | solution.py:601
  26.3 0.0 collective-permute-done.1.odd_ref
  26.3 0.0 copy-done
  26.3 0.0 copy-done.1
  26.3 0.0 copy-done.2
  26.3 1.7 %shard_map.70 = (f32[19,4,8,128]{3,2,1,0:T(8,128)}, f32[4,8,128]{2,1,0:T(8,128)}) custom-call(f32[19,4,8,128]{3,2,1,0:T(8,128)S(1)} %copy-done, s32[4,8,128]{2,1,0:T(8,128)S(1)} %copy-done.1, s32[4,8,128]{2,1,0:T(8,128)S(1)} %copy-done.2, f32[21,4,8,128]{3,2,1,0:T(8,128)S(1)} %get-tuple-element.9.own_ref, f32[21,4,8,128]{3,2,1,0:T(8,128)S(1)} %get-tuple-element.11.side_ref, ...), custom_call_target="tpu_custom_call" | custom-call | tf_op jit(solution)/shard_map/pallas_call | solution.py:560
Async XLA Ops:
  1.8 9.8 %collective-permute-start = (f32[36,8,128]{2,1,0:T(8,128)S(1)}, f32[36,8,128]{2,1,0:T(8,128)S(1)}, u32[]{:S(2)}, u32[]{:S(2)}) collective-permute-start(f32[36,8,128]{2,1,0:T(8,128)S(1)} %get-tuple-element.10), channel_id=1, source_target_pairs={{1,2},{3,4},{5,6},{7,8},{9,10},{11,12},{13,14},{15,0},{2,1},{4,3},... | collective-permute-start | bytes 442376 | tf_op jit(solution)/shard_map/ppermute | solution.py:588
  12.1 14.2 %copy-start = (f32[19,4,8,128]{3,2,1,0:T(8,128)S(1)}, f32[19,4,8,128]{3,2,1,0:T(8,128)}, u32[]{:S(2)}) copy-start(f32[19,4,8,128]{3,2,1,0:T(8,128)} %f_ref.1) | copy-start | bytes 933892
  12.2 14.2 %collective-permute-start.1 = (f32[37,8,128]{2,1,0:T(8,128)S(1)}, f32[37,8,128]{2,1,0:T(8,128)S(1)}, u32[]{:S(2)}, u32[]{:S(2)}) collective-permute-start(f32[37,8,128]{2,1,0:T(8,128)S(1)} %get-tuple-element.14), channel_id=1, source_target_pairs={{16,32},{48,64},{80,96},{112,128},{144,160},{176,192},{208,224},{2... | collective-permute-start | bytes 454664 | tf_op jit(solution)/shard_map/ppermute | solution.py:600
  18.9 7.4 %copy-start.1 = (s32[4,8,128]{2,1,0:T(8,128)S(1)}, s32[4,8,128]{2,1,0:T(8,128)}, u32[]{:S(2)}) copy-start(s32[4,8,128]{2,1,0:T(8,128)} %solid_ref.1) | copy-start | bytes 49156
  18.9 7.4 %copy-start.2 = (s32[4,8,128]{2,1,0:T(8,128)S(1)}, s32[4,8,128]{2,1,0:T(8,128)}, u32[]{:S(2)}) copy-start(s32[4,8,128]{2,1,0:T(8,128)} %surface_ref.1) | copy-start | bytes 49156

commit v6 on v5

--- a/solution.py
+++ b/solution.py
@@ -231,6 +231,10 @@
         return (read(i), jnp.where(sublane(first) < 4, first, second))
     tile = read(LAYERS + WIDE + (i - WIDE - INSET) // 2)
     return (read(i), pltpu.roll(tile, 4, 0) if (i - WIDE - INSET) % 2 else tile)
+
+
+def turn_of(column):
+    return min(column // 2, 1) if isinstance(column, int) else jnp.minimum(column // 2, 1)
 
 
 def wide_layers(core):
@@ -291,7 +295,7 @@
 
 
 def inner_kernel(
-    own_ref, both_ref, half_ref, side_ref, state_ref, next_ref, odd_ref, even_ref, message_ref
+    own_ref, both_ref, half_ref, side_ref, state_ref, next_ref, first_ref, second_ref, message_ref
 ):
     core = lax.rem(lax.axis_index("span"), 2)
     odd = lax.rem(lax.axis_index("stream"), 2)
@@ -358,26 +362,27 @@
         layers[WEIGHT_FAR] = c0(WEIGHT, far)
         layers[WEIGHT_NEAR] = c0(WEIGHT, near)
         put_message(message_ref.at[side], layers)
+    towards = lax.rem(1 - odd + turn_of(lax.axis_index("span")), 2)
     for i in range(TILES):
-        odd_ref[i] = message_ref[1 - odd, i]
-        even_ref[i] = message_ref[odd, i]
+        first_ref[i] = message_ref[towards, i]
+        second_ref[i] = message_ref[1 - towards, i]
 
 
 def last_kernel(
-    f_ref, solid_ref, surface_ref, own_ref, side_ref, state_ref, next_ref, odd_ref, even_ref,
+    f_ref, solid_ref, surface_ref, own_ref, side_ref, state_ref, next_ref, one_ref, two_ref,
     adjoint_hbm, sensitivity_hbm, adjoint_ref, sensitivity_ref,
     s1_ref, c1_ref, sum_ref, flow_ref, a1_ref, field_ref, sems,
 ):
     place = lax.axis_index("stream")
     at_start = place == 0
     at_end = place == lax.axis_size("stream") - 1
-    odd = lax.rem(place, 2)
+    origin = lax.rem(1 - lax.rem(place, 2) + turn_of(lax.axis_index("span")), 2)
 
     def low(i):
-        return jnp.where(odd == 1, even_ref[1 - odd, i], odd_ref[i])
+        return jnp.where(origin == 1, one_ref[i], two_ref[origin, i])
 
     def high(i):
-        return jnp.where(odd == 1, odd_ref[i], even_ref[1 - odd, i])
+        return jnp.where(origin == 0, one_ref[i], two_ref[origin, i])
 
     ends = (
         (low, at_start, 0, -1, UP, DOWN),
@@ -596,17 +601,22 @@
         [pltpu.VMEM((2,) + message, jnp.float32)],
     )
 
-    pairs = [(i, i + 1) for i in range(1, stream - 1, 2)]
-    odd = lax.ppermute(first, "stream", pairs + [(b, a) for a, b in pairs])
-    even = lax.all_gather(
-        second, "stream", axis_index_groups=[[i, i + 1] for i in range(0, stream, 2)]
-    )
+    swaps, groups = [], []
+    for j in range(span):
+        turn = turn_of(j)
+        swaps += [(i * span + j, (i + 1) * span + j) for i in range(1 - turn, stream - 1, 2)]
+        groups += [[i * span + j, (i + 1) * span + j] for i in range(turn, stream - 1, 2)]
+        if turn and j % 2:
+            groups += [[i * span + j - 1, i * span + j] for i in (0, stream - 1)]
+    axes = ("stream", "span")
+    one = lax.ppermute(first, axes, swaps + [(b, a) for a, b in swaps])
+    two = lax.all_gather(second, axes, axis_index_groups=groups)
     scratch = [
         (19, 4), (4,), (19, 2, 2), (19, 2, 2), (2, 4, 2), (2, 4, 2), (19, 6, 2), (4, 8, 2),
     ]
     adjoint, sensitivity = call(
         last_kernel,
-        (checkpoint, solid_mask, surface_mask, own, side, state, following, odd, even),
+        (checkpoint, solid_mask, surface_mask, own, side, state, following, one, two),
         [(19, 4) + tile, (4,) + tile],
         [pltpu.VMEM(shape + tile, jnp.float32) for shape in scratch]
         + [pltpu.SemaphoreType.DMA((5,))],

time: 28.3 us -> 28.3 us (level)
  no operation moved by 1% of the time
where the time goes in v6:
time: 28.3 us; the launch traced here: 28.1 us
  starting transfers between devices  12 us (42%)
  blocking collectives  9.67 us (34%)
  Pallas kernels  3.4 us (12%)
  waiting for transfers between devices  2.25 us (8%)
  between operations  0.69 us (2%)
    all_gather x1, blocking collectives, shards(): two = lax.all_gather(second, axes, axis_index_groups=groups)  7.37 us
    ppermute x1, starting transfers between devices, shards(): one = lax.ppermute(first, axes, swaps + [(b, a) for a, b in swaps])  6.76 us
    ppermute x1, starting transfers between devices, shards(): came = lax.ppermute(mine, 'span', chips + [(b, a) for a, b in chips])  5.29 us
    pallas_call x3, Pallas kernels, call(): pl.pallas_call(kernel, out_shape=[jax.ShapeDtypeStruct(shape, jnp.float32...  3.4 us
    all_gather x1, blocking collectives, shards(): both = lax.all_gather(own, 'span', axis_index_groups=cores)  2.3 us
    ppermute x1, waiting for transfers between devices, shards(): came = lax.ppermute(mine, 'span', chips + [(b, a) for a, b in chips])  2.25 us
  transfers between devices with their start and end apart: 2, of which 1 were waited for; matrix products, arithmetic and copies ran while one was open for 0% of the time, Pallas kernels for 0%

profile of v6, /device:TPU:384, one launch (start us, length us, event | category | flops | bytes accessed | tf_op | source)
XLA Modules:
  0.0 28.1 jit_solution(5348008761728420330)
XLA Ops:
  0.6 1.2 %shard_map.68 = (f32[21,4,8,128]{3,2,1,0:T(8,128)S(1)}, f32[36,8,128]{2,1,0:T(8,128)S(1)}) custom-call(f32[19,4,8,128]{3,2,1,0:T(8,128)} %f_ref.1, f32[4,8,128]{2,1,0:T(8,128)} %porosity_hbm.1, f32[4,8,128]{2,1,0:T(8,128)} %weight_hbm.1, s32[4,8,128]{2,1,0:T(8,128)} %solid_ref.1, s32[4,8,128]{2,1,0:T(8,128)} %surface_ref.1), custom_call_target="tpu_custom_call" | custom-call | tf_op jit(solution)/shard_map/pallas_call | solution.py:565
  1.8 5.3 %collective-permute-start = (f32[36,8,128]{2,1,0:T(8,128)S(1)}, f32[36,8,128]{2,1,0:T(8,128)S(1)}, u32[]{:S(2)}, u32[]{:S(2)}) collective-permute-start(f32[36,8,128]{2,1,0:T(8,128)S(1)} %get-tuple-element.10), channel_id=1, source_target_pairs={{1,2},{3,4},{5,6},{7,8},{9,10},{11,12},{13,14},{15,0},{2,1},{4,3},... | collective-permute-start | bytes 442376 | tf_op jit(solution)/shard_map/ppermute | solution.py:593
  7.1 2.3 %all-gather = f32[42,4,8,128]{3,2,1,0:T(8,128)S(1)} all-gather(f32[21,4,8,128]{3,2,1,0:T(8,128)S(1)} %get-tuple-element.9.own_ref), channel_id=2, replica_groups={{0,1},{2,3},{4,5},{6,7},{8,9},{10,11},{12,13},{14,15},{16,17},{18,19},{..., dimensions={0}, use_global_device_ids=true | all-gather | bytes 1032192 | tf_op jit(solution)/shard_map/all_gather | solution.py:594
  9.4 2.2 %collective-permute-done.half_ref = f32[36,8,128]{2,1,0:T(8,128)S(1)} collective-permute-done((f32[36,8,128]{2,1,0:T(8,128)S(1)}, f32[36,8,128]{2,1,0:T(8,128)S(1)}, u32[]{:S(2)}, u32[]{:S(2)}) %collective-permute-start) | collective-permute-done | bytes 147488 | tf_op jit(solution)/shard_map/ppermute | solution.py:593
  11.7 0.4 %shard_map.69 = (f32[21,4,8,128]{3,2,1,0:T(8,128)S(1)}, f32[19,2,2,8,128]{4,3,2,1,0:T(8,128)S(1)}, f32[19,2,2,8,128]{4,3,2,1,0:T(8,128)S(1)}, f32[37,8,128]{2,1,0:T(8,128)S(1)}, f32[37,8,128]{2,1,0:T(8,128)S(1)}) custom-call(f32[21,4,8,128]{3,2,1,0:T(8,128)S(1)} %get-tuple-element.9.own_ref, f32[2,21,4,8,128]{4,3,2,1,0:T(8,128)S(1)} %bitcast.2, ...), custom_call_target="tpu_custom_call" | custom-call | tf_op jit(solution)/shard_map/pallas_call | solution.py:565
  12.1 0.0 copy-start
  12.2 6.8 %collective-permute-start.1 = (f32[37,8,128]{2,1,0:T(8,128)S(1)}, f32[37,8,128]{2,1,0:T(8,128)S(1)}, u32[]{:S(2)}, u32[]{:S(2)}) collective-permute-start(f32[37,8,128]{2,1,0:T(8,128)S(1)} %get-tuple-element.14), channel_id=1, source_target_pairs={{16,32},{48,64},{80,96},{112,128},{144,160},{176,192},{208,224},{2... | collective-permute-start | bytes 454664 | tf_op jit(solution)/shard_map/ppermute | solution.py:612
  18.9 0.0 copy-start.1
  18.9 0.0 copy-start.2
  18.9 7.4 %all-gather.1 = f32[74,8,128]{2,1,0:T(8,128)S(1)} all-gather(f32[37,8,128]{2,1,0:T(8,128)S(1)} %get-tuple-element.15), channel_id=3, replica_groups={{0,16},{32,48},{64,80},{96,112},{128,144},{160,176},{192,208},{224,240}..., dimensions={0}, use_global_device_ids=true | all-gather | bytes 454656 | tf_op jit(solution)/shard_map/all_gather | solution.py:613
  26.3 0.0 collective-permute-done.1.one_ref
  26.3 0.0 copy-done
  26.3 0.0 copy-done.1
  26.3 0.0 copy-done.2
  26.3 1.7 %shard_map.70 = (f32[19,4,8,128]{3,2,1,0:T(8,128)}, f32[4,8,128]{2,1,0:T(8,128)}) custom-call(f32[19,4,8,128]{3,2,1,0:T(8,128)S(1)} %copy-done, s32[4,8,128]{2,1,0:T(8,128)S(1)} %copy-done.1, s32[4,8,128]{2,1,0:T(8,128)S(1)} %copy-done.2, f32[21,4,8,128]{3,2,1,0:T(8,128)S(1)} %get-tuple-element.9.own_ref, f32[21,4,8,128]{3,2,1,0:T(8,128)S(1)} %get-tuple-element.11.side_ref, ...), custom_call_target="tpu_custom_call" | custom-call | tf_op jit(solution)/shard_map/pallas_call | solution.py:565
Async XLA Ops:
  1.8 9.8 %collective-permute-start = (f32[36,8,128]{2,1,0:T(8,128)S(1)}, f32[36,8,128]{2,1,0:T(8,128)S(1)}, u32[]{:S(2)}, u32[]{:S(2)}) collective-permute-start(f32[36,8,128]{2,1,0:T(8,128)S(1)} %get-tuple-element.10), channel_id=1, source_target_pairs={{1,2},{3,4},{5,6},{7,8},{9,10},{11,12},{13,14},{15,0},{2,1},{4,3},... | collective-permute-start | bytes 442376 | tf_op jit(solution)/shard_map/ppermute | solution.py:593
  12.1 14.2 %copy-start = (f32[19,4,8,128]{3,2,1,0:T(8,128)S(1)}, f32[19,4,8,128]{3,2,1,0:T(8,128)}, u32[]{:S(2)}) copy-start(f32[19,4,8,128]{3,2,1,0:T(8,128)} %f_ref.1) | copy-start | bytes 933892
  12.2 14.2 %collective-permute-start.1 = (f32[37,8,128]{2,1,0:T(8,128)S(1)}, f32[37,8,128]{2,1,0:T(8,128)S(1)}, u32[]{:S(2)}, u32[]{:S(2)}) collective-permute-start(f32[37,8,128]{2,1,0:T(8,128)S(1)} %get-tuple-element.14), channel_id=1, source_target_pairs={{16,32},{48,64},{80,96},{112,128},{144,160},{176,192},{208,224},{2... | collective-permute-start | bytes 454664 | tf_op jit(solution)/shard_map/ppermute | solution.py:612
  18.9 7.4 %copy-start.1 = (s32[4,8,128]{2,1,0:T(8,128)S(1)}, s32[4,8,128]{2,1,0:T(8,128)}, u32[]{:S(2)}) copy-start(s32[4,8,128]{2,1,0:T(8,128)} %solid_ref.1) | copy-start | bytes 49156
  18.9 7.4 %copy-start.2 = (s32[4,8,128]{2,1,0:T(8,128)S(1)}, s32[4,8,128]{2,1,0:T(8,128)}, u32[]{:S(2)}) copy-start(s32[4,8,128]{2,1,0:T(8,128)} %surface_ref.1) | copy-start | bytes 49156

commit v7 on v6

--- a/solution.py
+++ b/solution.py
@@ -55,8 +55,8 @@
 ALONG = [p for p in range(19) if VEL[p][1] == 0]
 OPP = [0] + [p + 1 if p % 2 else p - 1 for p in range(1, 19)]
 BLEND, WEIGHT = 19, 20
-SPAN_WIDE = 15
-SPAN_TILES = 2 * SPAN_WIDE + 6
+SPAN_WIDE, SPAN_FREE = 15, 5
+SPAN_TILES = 2 * SPAN_WIDE + 1
 STATE, MOMENTS, NEAR_BLEND, WIDE = 0, 5, 9, 10
 SUM_FAR, SUM_NEAR, SUM_OWN, WEIGHT_FAR, WEIGHT_NEAR, LAYERS = 10, 14, 18, 21, 22, 23
 INSET = WIDE // 2
@@ -69,6 +69,10 @@
 
 def lane(tile):
     return lax.broadcasted_iota(jnp.int32, tile.shape, len(tile.shape) - 1)
+
+
+def spin(tile, rows):
+    return pltpu.roll(tile, rows % 8, 0) if rows % 8 else tile
 
 
 def shift_z(tile, step, fill):
@@ -291,7 +295,14 @@
         for x in range(1, 4):
             here = lax.rem(at + 8 - 2 * x + 2 * core, 8) < 2
             tile = jnp.where(here, pltpu.roll(own_ref[layer, x], 2 * x, 0), tile)
-        half_ref[2 * SPAN_WIDE + i] = tile
+        if i == 5:
+            half_ref[2 * SPAN_WIDE] = tile
+            continue
+        for k in range(4):
+            slot = 2 * SPAN_FREE + 4 * i + k
+            piece = jnp.where(core == 0, spin(tile, 3 - k), spin(tile, -k))
+            free = lax.rem(at, 4) == 3 * (1 - core)
+            half_ref[slot] = jnp.where(free, piece, half_ref[slot])
 
 
 def inner_kernel(
@@ -299,17 +310,21 @@
 ):
     core = lax.rem(lax.axis_index("span"), 2)
     odd = lax.rem(lax.axis_index("stream"), 2)
-    low = (sublane(half_ref[0]) < 4) == (core == 0)
+    at = lax.broadcasted_iota(jnp.int32, (8, 128), 0)
+    low = (at < 4) == (core == 0)
     for i, layer in enumerate(wide_layers(1 - core)):
         for x in range(4):
             tile = half_ref[2 * i + x // 2]
             tile = pltpu.roll(tile, 4, 0) if x % 2 else tile
             side_ref[layer, x] = jnp.where(low, both_ref[1 - core, layer, x], tile)
     for i, layer in enumerate(narrow_layers(1 - core)):
+        rows = half_ref[2 * SPAN_WIDE]
+        for k in range(4 if i < 5 else 0):
+            piece = half_ref[2 * SPAN_FREE + 4 * i + k]
+            piece = jnp.where(core == 1, spin(piece, k - 3), spin(piece, k))
+            rows = jnp.where(lax.rem(at, 4) == k, piece, rows) if k else piece
         for x in range(4):
-            tile = half_ref[2 * SPAN_WIDE + i]
-            tile = pltpu.roll(tile, 8 - 2 * x, 0) if x else tile
-            side_ref[layer, x] = jnp.where(low, both_ref[1 - core, layer, x], tile)
+            side_ref[layer, x] = jnp.where(low, both_ref[1 - core, layer, x], spin(rows, -2 * x))
 
     def c0(p, x):
         return (own_ref[p, x], side_ref[p, x])

time: 28.3 us -> 27.9 us (0.986)
  waiting for transfers between devices: 2.25 us -> 1.81 us
    ppermute x1, waiting for transfers between devices: 2.25 us -> 1.81 us  [shards(): came = lax.ppermute(mine, 'span', chips + [(b, a) for a, b in chips])]
where the time goes in v7:
time: 27.9 us; the launch traced here: 27.6 us
  starting transfers between devices  12.1 us (43%)
  blocking collectives  9.67 us (35%)
  Pallas kernels  3.39 us (12%)
  waiting for transfers between devices  1.81 us (6%)
  between operations  0.69 us (2%)
    all_gather x1, blocking collectives, shards(): two = lax.all_gather(second, axes, axis_index_groups=groups)  7.37 us
    ppermute x1, starting transfers between devices, shards(): one = lax.ppermute(first, axes, swaps + [(b, a) for a, b in swaps])  6.76 us
    ppermute x1, starting transfers between devices, shards(): came = lax.ppermute(mine, 'span', chips + [(b, a) for a, b in chips])  5.29 us
    pallas_call x3, Pallas kernels, call(): pl.pallas_call(kernel, out_shape=[jax.ShapeDtypeStruct(shape, jnp.float32...  3.39 us
    all_gather x1, blocking collectives, shards(): both = lax.all_gather(own, 'span', axis_index_groups=cores)  2.3 us
    ppermute x1, waiting for transfers between devices, shards(): came = lax.ppermute(mine, 'span', chips + [(b, a) for a, b in chips])  1.81 us
  transfers between devices with their start and end apart: 2, of which 1 were waited for; matrix products, arithmetic and copies ran while one was open for 0% of the time, Pallas kernels for 0%

profile of v7, /device:TPU:384, one launch (start us, length us, event | category | flops | bytes accessed | tf_op | source)
XLA Modules:
  0.0 27.6 jit_solution(17974547239182991460)
XLA Ops:
  0.6 1.2 %shard_map.68 = (f32[21,4,8,128]{3,2,1,0:T(8,128)S(1)}, f32[31,8,128]{2,1,0:T(8,128)S(1)}) custom-call(f32[19,4,8,128]{3,2,1,0:T(8,128)} %f_ref.1, f32[4,8,128]{2,1,0:T(8,128)} %porosity_hbm.1, f32[4,8,128]{2,1,0:T(8,128)} %weight_hbm.1, s32[4,8,128]{2,1,0:T(8,128)} %solid_ref.1, s32[4,8,128]{2,1,0:T(8,128)} %surface_ref.1), custom_call_target="tpu_custom_call" | custom-call | tf_op jit(solution)/shard_map/pallas_call | solution.py:580
  1.9 5.3 %collective-permute-start = (f32[31,8,128]{2,1,0:T(8,128)S(1)}, f32[31,8,128]{2,1,0:T(8,128)S(1)}, u32[]{:S(2)}, u32[]{:S(2)}) collective-permute-start(f32[31,8,128]{2,1,0:T(8,128)S(1)} %get-tuple-element.10), channel_id=1, source_target_pairs={{1,2},{3,4},{5,6},{7,8},{9,10},{11,12},{13,14},{15,0},{2,1},{4,3},... | collective-permute-start | bytes 380936 | tf_op jit(solution)/shard_map/ppermute | solution.py:608
  7.2 2.3 %all-gather = f32[42,4,8,128]{3,2,1,0:T(8,128)S(1)} all-gather(f32[21,4,8,128]{3,2,1,0:T(8,128)S(1)} %get-tuple-element.9.own_ref), channel_id=2, replica_groups={{0,1},{2,3},{4,5},{6,7},{8,9},{10,11},{12,13},{14,15},{16,17},{18,19},{..., dimensions={0}, use_global_device_ids=true | all-gather | bytes 1032192 | tf_op jit(solution)/shard_map/all_gather | solution.py:609
  9.5 1.8 %collective-permute-done.half_ref = f32[31,8,128]{2,1,0:T(8,128)S(1)} collective-permute-done((f32[31,8,128]{2,1,0:T(8,128)S(1)}, f32[31,8,128]{2,1,0:T(8,128)S(1)}, u32[]{:S(2)}, u32[]{:S(2)}) %collective-permute-start) | collective-permute-done | bytes 127008 | tf_op jit(solution)/shard_map/ppermute | solution.py:608
  11.3 0.4 %shard_map.69 = (f32[21,4,8,128]{3,2,1,0:T(8,128)S(1)}, f32[19,2,2,8,128]{4,3,2,1,0:T(8,128)S(1)}, f32[19,2,2,8,128]{4,3,2,1,0:T(8,128)S(1)}, f32[37,8,128]{2,1,0:T(8,128)S(1)}, f32[37,8,128]{2,1,0:T(8,128)S(1)}) custom-call(f32[21,4,8,128]{3,2,1,0:T(8,128)S(1)} %get-tuple-element.9.own_ref, f32[2,21,4,8,128]{4,3,2,1,0:T(8,128)S(1)} %bitcast.2, ...), custom_call_target="tpu_custom_call" | custom-call | tf_op jit(solution)/shard_map/pallas_call | solution.py:580
  11.7 0.0 copy-start
  11.7 6.8 %collective-permute-start.1 = (f32[37,8,128]{2,1,0:T(8,128)S(1)}, f32[37,8,128]{2,1,0:T(8,128)S(1)}, u32[]{:S(2)}, u32[]{:S(2)}) collective-permute-start(f32[37,8,128]{2,1,0:T(8,128)S(1)} %get-tuple-element.14), channel_id=1, source_target_pairs={{16,32},{48,64},{80,96},{112,128},{144,160},{176,192},{208,224},{2... | collective-permute-start | bytes 454664 | tf_op jit(solution)/shard_map/ppermute | solution.py:627
  18.5 0.0 copy-start.1
  18.5 0.0 copy-start.2
  18.5 7.4 %all-gather.1 = f32[74,8,128]{2,1,0:T(8,128)S(1)} all-gather(f32[37,8,128]{2,1,0:T(8,128)S(1)} %get-tuple-element.15), channel_id=3, replica_groups={{0,16},{32,48},{64,80},{96,112},{128,144},{160,176},{192,208},{224,240}..., dimensions={0}, use_global_device_ids=true | all-gather | bytes 454656 | tf_op jit(solution)/shard_map/all_gather | solution.py:628
  25.9 0.0 collective-permute-done.1.one_ref
  25.9 0.0 copy-done
  25.9 0.0 copy-done.1
  25.9 0.0 copy-done.2
  25.9 1.7 %shard_map.70 = (f32[19,4,8,128]{3,2,1,0:T(8,128)}, f32[4,8,128]{2,1,0:T(8,128)}) custom-call(f32[19,4,8,128]{3,2,1,0:T(8,128)S(1)} %copy-done, s32[4,8,128]{2,1,0:T(8,128)S(1)} %copy-done.1, s32[4,8,128]{2,1,0:T(8,128)S(1)} %copy-done.2, f32[21,4,8,128]{3,2,1,0:T(8,128)S(1)} %get-tuple-element.9.own_ref, f32[21,4,8,128]{3,2,1,0:T(8,128)S(1)} %get-tuple-element.11.side_ref, ...), custom_call_target="tpu_custom_call" | custom-call | tf_op jit(solution)/shard_map/pallas_call | solution.py:580
Async XLA Ops:
  1.9 9.4 %collective-permute-start = (f32[31,8,128]{2,1,0:T(8,128)S(1)}, f32[31,8,128]{2,1,0:T(8,128)S(1)}, u32[]{:S(2)}, u32[]{:S(2)}) collective-permute-start(f32[31,8,128]{2,1,0:T(8,128)S(1)} %get-tuple-element.10), channel_id=1, source_target_pairs={{1,2},{3,4},{5,6},{7,8},{9,10},{11,12},{13,14},{15,0},{2,1},{4,3},... | collective-permute-start | bytes 380936 | tf_op jit(solution)/shard_map/ppermute | solution.py:608
  11.7 14.2 %copy-start = (f32[19,4,8,128]{3,2,1,0:T(8,128)S(1)}, f32[19,4,8,128]{3,2,1,0:T(8,128)}, u32[]{:S(2)}) copy-start(f32[19,4,8,128]{3,2,1,0:T(8,128)} %f_ref.1) | copy-start | bytes 933892
  11.7 14.2 %collective-permute-start.1 = (f32[37,8,128]{2,1,0:T(8,128)S(1)}, f32[37,8,128]{2,1,0:T(8,128)S(1)}, u32[]{:S(2)}, u32[]{:S(2)}) collective-permute-start(f32[37,8,128]{2,1,0:T(8,128)S(1)} %get-tuple-element.14), channel_id=1, source_target_pairs={{16,32},{48,64},{80,96},{112,128},{144,160},{176,192},{208,224},{2... | collective-permute-start | bytes 454664 | tf_op jit(solution)/shard_map/ppermute | solution.py:627
  18.5 7.4 %copy-start.1 = (s32[4,8,128]{2,1,0:T(8,128)S(1)}, s32[4,8,128]{2,1,0:T(8,128)}, u32[]{:S(2)}) copy-start(s32[4,8,128]{2,1,0:T(8,128)} %solid_ref.1) | copy-start | bytes 49156
  18.5 7.4 %copy-start.2 = (s32[4,8,128]{2,1,0:T(8,128)S(1)}, s32[4,8,128]{2,1,0:T(8,128)}, u32[]{:S(2)}) copy-start(s32[4,8,128]{2,1,0:T(8,128)} %surface_ref.1) | copy-start | bytes 49156

commit v8 on v7

--- a/solution.py
+++ b/solution.py
@@ -238,7 +238,8 @@
 
 
 def turn_of(column):
-    return min(column // 2, 1) if isinstance(column, int) else jnp.minimum(column // 2, 1)
+    least = min if isinstance(column, int) else jnp.minimum
+    return least(column % 4 // 2 + column // 8, 1)
 
 
 def wide_layers(core):

time: 27.9 us -> 27.9 us (level)
  no operation moved by 1% of the time
where the time goes in v8:
time: 27.9 us; the launch traced here: 27.6 us
  starting transfers between devices  12.1 us (43%)
  blocking collectives  9.67 us (35%)
  Pallas kernels  3.39 us (12%)
  waiting for transfers between devices  1.81 us (6%)
  between operations  0.69 us (2%)
    all_gather x1, blocking collectives, shards(): two = lax.all_gather(second, axes, axis_index_groups=groups)  7.37 us
    ppermute x1, starting transfers between devices, shards(): one = lax.ppermute(first, axes, swaps + [(b, a) for a, b in swaps])  6.76 us
    ppermute x1, starting transfers between devices, shards(): came = lax.ppermute(mine, 'span', chips + [(b, a) for a, b in chips])  5.29 us
    pallas_call x3, Pallas kernels, call(): pl.pallas_call(kernel, out_shape=[jax.ShapeDtypeStruct(shape, jnp.float32...  3.39 us
    all_gather x1, blocking collectives, shards(): both = lax.all_gather(own, 'span', axis_index_groups=cores)  2.3 us
    ppermute x1, waiting for transfers between devices, shards(): came = lax.ppermute(mine, 'span', chips + [(b, a) for a, b in chips])  1.81 us
  transfers between devices with their start and end apart: 2, of which 1 were waited for; matrix products, arithmetic and copies ran while one was open for 0% of the time, Pallas kernels for 0%

profile of v8, /device:TPU:384, one launch (start us, length us, event | category | flops | bytes accessed | tf_op | source)
XLA Modules:
  0.0 27.6 jit_solution(2368485831354346963)
XLA Ops:
  0.6 1.2 %shard_map.68 = (f32[21,4,8,128]{3,2,1,0:T(8,128)S(1)}, f32[31,8,128]{2,1,0:T(8,128)S(1)}) custom-call(f32[19,4,8,128]{3,2,1,0:T(8,128)} %f_ref.1, f32[4,8,128]{2,1,0:T(8,128)} %porosity_hbm.1, f32[4,8,128]{2,1,0:T(8,128)} %weight_hbm.1, s32[4,8,128]{2,1,0:T(8,128)} %solid_ref.1, s32[4,8,128]{2,1,0:T(8,128)} %surface_ref.1), custom_call_target="tpu_custom_call" | custom-call | tf_op jit(solution)/shard_map/pallas_call | solution.py:581
  1.9 5.3 %collective-permute-start = (f32[31,8,128]{2,1,0:T(8,128)S(1)}, f32[31,8,128]{2,1,0:T(8,128)S(1)}, u32[]{:S(2)}, u32[]{:S(2)}) collective-permute-start(f32[31,8,128]{2,1,0:T(8,128)S(1)} %get-tuple-element.10), channel_id=1, source_target_pairs={{1,2},{3,4},{5,6},{7,8},{9,10},{11,12},{13,14},{15,0},{2,1},{4,3},... | collective-permute-start | bytes 380936 | tf_op jit(solution)/shard_map/ppermute | solution.py:609
  7.2 2.3 %all-gather = f32[42,4,8,128]{3,2,1,0:T(8,128)S(1)} all-gather(f32[21,4,8,128]{3,2,1,0:T(8,128)S(1)} %get-tuple-element.9.own_ref), channel_id=2, replica_groups={{0,1},{2,3},{4,5},{6,7},{8,9},{10,11},{12,13},{14,15},{16,17},{18,19},{..., dimensions={0}, use_global_device_ids=true | all-gather | bytes 1032192 | tf_op jit(solution)/shard_map/all_gather | solution.py:610
  9.5 1.8 %collective-permute-done.half_ref = f32[31,8,128]{2,1,0:T(8,128)S(1)} collective-permute-done((f32[31,8,128]{2,1,0:T(8,128)S(1)}, f32[31,8,128]{2,1,0:T(8,128)S(1)}, u32[]{:S(2)}, u32[]{:S(2)}) %collective-permute-start) | collective-permute-done | bytes 127008 | tf_op jit(solution)/shard_map/ppermute | solution.py:609
  11.3 0.4 %shard_map.69 = (f32[21,4,8,128]{3,2,1,0:T(8,128)S(1)}, f32[19,2,2,8,128]{4,3,2,1,0:T(8,128)S(1)}, f32[19,2,2,8,128]{4,3,2,1,0:T(8,128)S(1)}, f32[37,8,128]{2,1,0:T(8,128)S(1)}, f32[37,8,128]{2,1,0:T(8,128)S(1)}) custom-call(f32[21,4,8,128]{3,2,1,0:T(8,128)S(1)} %get-tuple-element.9.own_ref, f32[2,21,4,8,128]{4,3,2,1,0:T(8,128)S(1)} %bitcast.2, ...), custom_call_target="tpu_custom_call" | custom-call | tf_op jit(solution)/shard_map/pallas_call | solution.py:581
  11.7 0.0 copy-start
  11.7 6.8 %collective-permute-start.1 = (f32[37,8,128]{2,1,0:T(8,128)S(1)}, f32[37,8,128]{2,1,0:T(8,128)S(1)}, u32[]{:S(2)}, u32[]{:S(2)}) collective-permute-start(f32[37,8,128]{2,1,0:T(8,128)S(1)} %get-tuple-element.14), channel_id=1, source_target_pairs={{16,32},{48,64},{80,96},{112,128},{144,160},{176,192},{208,224},{2... | collective-permute-start | bytes 454664 | tf_op jit(solution)/shard_map/ppermute | solution.py:628
  18.5 0.0 copy-start.1
  18.5 0.0 copy-start.2
  18.5 7.4 %all-gather.1 = f32[74,8,128]{2,1,0:T(8,128)S(1)} all-gather(f32[37,8,128]{2,1,0:T(8,128)S(1)} %get-tuple-element.15), channel_id=3, replica_groups={{0,16},{32,48},{64,80},{96,112},{128,144},{160,176},{192,208},{224,240}..., dimensions={0}, use_global_device_ids=true | all-gather | bytes 454656 | tf_op jit(solution)/shard_map/all_gather | solution.py:629
  25.9 0.0 collective-permute-done.1.one_ref
  25.9 0.0 copy-done
  25.9 0.0 copy-done.1
  25.9 0.0 copy-done.2
  25.9 1.7 %shard_map.70 = (f32[19,4,8,128]{3,2,1,0:T(8,128)}, f32[4,8,128]{2,1,0:T(8,128)}) custom-call(f32[19,4,8,128]{3,2,1,0:T(8,128)S(1)} %copy-done, s32[4,8,128]{2,1,0:T(8,128)S(1)} %copy-done.1, s32[4,8,128]{2,1,0:T(8,128)S(1)} %copy-done.2, f32[21,4,8,128]{3,2,1,0:T(8,128)S(1)} %get-tuple-element.9.own_ref, f32[21,4,8,128]{3,2,1,0:T(8,128)S(1)} %get-tuple-element.11.side_ref, ...), custom_call_target="tpu_custom_call" | custom-call | tf_op jit(solution)/shard_map/pallas_call | solution.py:581
Async XLA Ops:
  1.9 9.4 %collective-permute-start = (f32[31,8,128]{2,1,0:T(8,128)S(1)}, f32[31,8,128]{2,1,0:T(8,128)S(1)}, u32[]{:S(2)}, u32[]{:S(2)}) collective-permute-start(f32[31,8,128]{2,1,0:T(8,128)S(1)} %get-tuple-element.10), channel_id=1, source_target_pairs={{1,2},{3,4},{5,6},{7,8},{9,10},{11,12},{13,14},{15,0},{2,1},{4,3},... | collective-permute-start | bytes 380936 | tf_op jit(solution)/shard_map/ppermute | solution.py:609
  11.7 14.2 %copy-start = (f32[19,4,8,128]{3,2,1,0:T(8,128)S(1)}, f32[19,4,8,128]{3,2,1,0:T(8,128)}, u32[]{:S(2)}) copy-start(f32[19,4,8,128]{3,2,1,0:T(8,128)} %f_ref.1) | copy-start | bytes 933892
  11.7 14.2 %collective-permute-start.1 = (f32[37,8,128]{2,1,0:T(8,128)S(1)}, f32[37,8,128]{2,1,0:T(8,128)S(1)}, u32[]{:S(2)}, u32[]{:S(2)}) collective-permute-start(f32[37,8,128]{2,1,0:T(8,128)S(1)} %get-tuple-element.14), channel_id=1, source_target_pairs={{16,32},{48,64},{80,96},{112,128},{144,160},{176,192},{208,224},{2... | collective-permute-start | bytes 454664 | tf_op jit(solution)/shard_map/ppermute | solution.py:628
  18.5 7.4 %copy-start.1 = (s32[4,8,128]{2,1,0:T(8,128)S(1)}, s32[4,8,128]{2,1,0:T(8,128)}, u32[]{:S(2)}) copy-start(s32[4,8,128]{2,1,0:T(8,128)} %solid_ref.1) | copy-start | bytes 49156
  18.5 7.4 %copy-start.2 = (s32[4,8,128]{2,1,0:T(8,128)S(1)}, s32[4,8,128]{2,1,0:T(8,128)}, u32[]{:S(2)}) copy-start(s32[4,8,128]{2,1,0:T(8,128)} %surface_ref.1) | copy-start | bytes 49156

commit v9 on v7

--- a/solution.py
+++ b/solution.py
@@ -386,18 +386,22 @@
 def last_kernel(
     f_ref, solid_ref, surface_ref, own_ref, side_ref, state_ref, next_ref, one_ref, two_ref,
     adjoint_hbm, sensitivity_hbm, adjoint_ref, sensitivity_ref,
-    s1_ref, c1_ref, sum_ref, flow_ref, a1_ref, field_ref, sems,
+    s1_ref, c1_ref, sum_ref, flow_ref, a1_ref, field_ref, came_ref, sems,
 ):
     place = lax.axis_index("stream")
     at_start = place == 0
     at_end = place == lax.axis_size("stream") - 1
     origin = lax.rem(1 - lax.rem(place, 2) + turn_of(lax.axis_index("span")), 2)
 
+    for i in range(TILES):
+        came_ref[1 - origin, i] = one_ref[i]
+        came_ref[origin, i] = two_ref[origin, i]
+
     def low(i):
-        return jnp.where(origin == 1, one_ref[i], two_ref[origin, i])
+        return came_ref[0, i]
 
     def high(i):
-        return jnp.where(origin == 0, one_ref[i], two_ref[origin, i])
+        return came_ref[1, i]
 
     ends = (
         (low, at_start, 0, -1, UP, DOWN),
@@ -628,6 +632,7 @@
     two = lax.all_gather(second, axes, axis_index_groups=groups)
     scratch = [
         (19, 4), (4,), (19, 2, 2), (19, 2, 2), (2, 4, 2), (2, 4, 2), (19, 6, 2), (4, 8, 2),
+        (2, TILES),
     ]
     adjoint, sensitivity = call(
         last_kernel,

time: 27.9 us -> 27.9 us (level)
  no operation moved by 1% of the time
where the time goes in v9:
time: 27.9 us; the launch traced here: 27.6 us
  starting transfers between devices  12.1 us (43%)
  blocking collectives  9.67 us (35%)
  Pallas kernels  3.39 us (12%)
  waiting for transfers between devices  1.81 us (6%)
  between operations  0.69 us (2%)
    all_gather x1, blocking collectives, shards(): two = lax.all_gather(second, axes, axis_index_groups=groups)  7.37 us
    ppermute x1, starting transfers between devices, shards(): one = lax.ppermute(first, axes, swaps + [(b, a) for a, b in swaps])  6.76 us
    ppermute x1, starting transfers between devices, shards(): came = lax.ppermute(mine, 'span', chips + [(b, a) for a, b in chips])  5.29 us
    pallas_call x3, Pallas kernels, call(): pl.pallas_call(kernel, out_shape=[jax.ShapeDtypeStruct(shape, jnp.float32...  3.39 us
    all_gather x1, blocking collectives, shards(): both = lax.all_gather(own, 'span', axis_index_groups=cores)  2.3 us
    ppermute x1, waiting for transfers between devices, shards(): came = lax.ppermute(mine, 'span', chips + [(b, a) for a, b in chips])  1.81 us
  transfers between devices with their start and end apart: 2, of which 1 were waited for; matrix products, arithmetic and copies ran while one was open for 0% of the time, Pallas kernels for 0%

profile of v9, /device:TPU:384, one launch (start us, length us, event | category | flops | bytes accessed | tf_op | source)
XLA Modules:
  0.0 27.6 jit_solution(10318737767198465447)
XLA Ops:
  0.6 1.2 %shard_map.68 = (f32[21,4,8,128]{3,2,1,0:T(8,128)S(1)}, f32[31,8,128]{2,1,0:T(8,128)S(1)}) custom-call(f32[19,4,8,128]{3,2,1,0:T(8,128)} %f_ref.1, f32[4,8,128]{2,1,0:T(8,128)} %porosity_hbm.1, f32[4,8,128]{2,1,0:T(8,128)} %weight_hbm.1, s32[4,8,128]{2,1,0:T(8,128)} %solid_ref.1, s32[4,8,128]{2,1,0:T(8,128)} %surface_ref.1), custom_call_target="tpu_custom_call" | custom-call | tf_op jit(solution)/shard_map/pallas_call | solution.py:584
  1.9 5.3 %collective-permute-start = (f32[31,8,128]{2,1,0:T(8,128)S(1)}, f32[31,8,128]{2,1,0:T(8,128)S(1)}, u32[]{:S(2)}, u32[]{:S(2)}) collective-permute-start(f32[31,8,128]{2,1,0:T(8,128)S(1)} %get-tuple-element.10), channel_id=1, source_target_pairs={{1,2},{3,4},{5,6},{7,8},{9,10},{11,12},{13,14},{15,0},{2,1},{4,3},... | collective-permute-start | bytes 380936 | tf_op jit(solution)/shard_map/ppermute | solution.py:612
  7.2 2.3 %all-gather = f32[42,4,8,128]{3,2,1,0:T(8,128)S(1)} all-gather(f32[21,4,8,128]{3,2,1,0:T(8,128)S(1)} %get-tuple-element.9.own_ref), channel_id=2, replica_groups={{0,1},{2,3},{4,5},{6,7},{8,9},{10,11},{12,13},{14,15},{16,17},{18,19},{..., dimensions={0}, use_global_device_ids=true | all-gather | bytes 1032192 | tf_op jit(solution)/shard_map/all_gather | solution.py:613
  9.5 1.8 %collective-permute-done.half_ref = f32[31,8,128]{2,1,0:T(8,128)S(1)} collective-permute-done((f32[31,8,128]{2,1,0:T(8,128)S(1)}, f32[31,8,128]{2,1,0:T(8,128)S(1)}, u32[]{:S(2)}, u32[]{:S(2)}) %collective-permute-start) | collective-permute-done | bytes 127008 | tf_op jit(solution)/shard_map/ppermute | solution.py:612
  11.3 0.4 %shard_map.69 = (f32[21,4,8,128]{3,2,1,0:T(8,128)S(1)}, f32[19,2,2,8,128]{4,3,2,1,0:T(8,128)S(1)}, f32[19,2,2,8,128]{4,3,2,1,0:T(8,128)S(1)}, f32[37,8,128]{2,1,0:T(8,128)S(1)}, f32[37,8,128]{2,1,0:T(8,128)S(1)}) custom-call(f32[21,4,8,128]{3,2,1,0:T(8,128)S(1)} %get-tuple-element.9.own_ref, f32[2,21,4,8,128]{4,3,2,1,0:T(8,128)S(1)} %bitcast.2, ...), custom_call_target="tpu_custom_call" | custom-call | tf_op jit(solution)/shard_map/pallas_call | solution.py:584
  11.7 0.0 copy-start
  11.7 6.8 %collective-permute-start.1 = (f32[37,8,128]{2,1,0:T(8,128)S(1)}, f32[37,8,128]{2,1,0:T(8,128)S(1)}, u32[]{:S(2)}, u32[]{:S(2)}) collective-permute-start(f32[37,8,128]{2,1,0:T(8,128)S(1)} %get-tuple-element.14), channel_id=1, source_target_pairs={{16,32},{48,64},{80,96},{112,128},{144,160},{176,192},{208,224},{2... | collective-permute-start | bytes 454664 | tf_op jit(solution)/shard_map/ppermute | solution.py:631
  18.5 0.0 copy-start.1
  18.5 0.0 copy-start.2
  18.5 7.4 %all-gather.1 = f32[74,8,128]{2,1,0:T(8,128)S(1)} all-gather(f32[37,8,128]{2,1,0:T(8,128)S(1)} %get-tuple-element.15), channel_id=3, replica_groups={{0,16},{32,48},{64,80},{96,112},{128,144},{160,176},{192,208},{224,240}..., dimensions={0}, use_global_device_ids=true | all-gather | bytes 454656 | tf_op jit(solution)/shard_map/all_gather | solution.py:632
  25.9 0.0 collective-permute-done.1.one_ref
  25.9 0.0 copy-done
  25.9 0.0 copy-done.1
  25.9 0.0 copy-done.2
  25.9 1.7 %shard_map.70 = (f32[19,4,8,128]{3,2,1,0:T(8,128)}, f32[4,8,128]{2,1,0:T(8,128)}) custom-call(f32[19,4,8,128]{3,2,1,0:T(8,128)S(1)} %copy-done, s32[4,8,128]{2,1,0:T(8,128)S(1)} %copy-done.1, s32[4,8,128]{2,1,0:T(8,128)S(1)} %copy-done.2, f32[21,4,8,128]{3,2,1,0:T(8,128)S(1)} %get-tuple-element.9.own_ref, f32[21,4,8,128]{3,2,1,0:T(8,128)S(1)} %get-tuple-element.11.side_ref, ...), custom_call_target="tpu_custom_call" | custom-call | tf_op jit(solution)/shard_map/pallas_call | solution.py:584
Async XLA Ops:
  1.9 9.4 %collective-permute-start = (f32[31,8,128]{2,1,0:T(8,128)S(1)}, f32[31,8,128]{2,1,0:T(8,128)S(1)}, u32[]{:S(2)}, u32[]{:S(2)}) collective-permute-start(f32[31,8,128]{2,1,0:T(8,128)S(1)} %get-tuple-element.10), channel_id=1, source_target_pairs={{1,2},{3,4},{5,6},{7,8},{9,10},{11,12},{13,14},{15,0},{2,1},{4,3},... | collective-permute-start | bytes 380936 | tf_op jit(solution)/shard_map/ppermute | solution.py:612
  11.7 14.2 %copy-start = (f32[19,4,8,128]{3,2,1,0:T(8,128)S(1)}, f32[19,4,8,128]{3,2,1,0:T(8,128)}, u32[]{:S(2)}) copy-start(f32[19,4,8,128]{3,2,1,0:T(8,128)} %f_ref.1) | copy-start | bytes 933892
  11.7 14.2 %collective-permute-start.1 = (f32[37,8,128]{2,1,0:T(8,128)S(1)}, f32[37,8,128]{2,1,0:T(8,128)S(1)}, u32[]{:S(2)}, u32[]{:S(2)}) collective-permute-start(f32[37,8,128]{2,1,0:T(8,128)S(1)} %get-tuple-element.14), channel_id=1, source_target_pairs={{16,32},{48,64},{80,96},{112,128},{144,160},{176,192},{208,224},{2... | collective-permute-start | bytes 454664 | tf_op jit(solution)/shard_map/ppermute | solution.py:631
  18.5 7.4 %copy-start.1 = (s32[4,8,128]{2,1,0:T(8,128)S(1)}, s32[4,8,128]{2,1,0:T(8,128)}, u32[]{:S(2)}) copy-start(s32[4,8,128]{2,1,0:T(8,128)} %solid_ref.1) | copy-start | bytes 49156
  18.5 7.4 %copy-start.2 = (s32[4,8,128]{2,1,0:T(8,128)S(1)}, s32[4,8,128]{2,1,0:T(8,128)}, u32[]{:S(2)}) copy-start(s32[4,8,128]{2,1,0:T(8,128)} %surface_ref.1) | copy-start | bytes 49156

commit v10 on v9

--- a/solution.py
+++ b/solution.py
@@ -268,7 +268,7 @@
     rows = [
         pltpu.make_async_copy(f_hbm.at[:, x], f_ref.at[:, x], sems.at[4 + x]) for x in range(4)
     ]
-    for copy in rows[:1] + small + rows[1:]:
+    for copy in rows + small:
         copy.start()
     core = lax.rem(lax.axis_index("span"), 2)
     at = lax.broadcasted_iota(jnp.int32, (8, 128), 0)

time: 27.9 us -> 27.9 us (level)
  no operation moved by 1% of the time
where the time goes in v10:
time: 27.9 us; the launch traced here: 27.6 us
  starting transfers between devices  12.1 us (43%)
  blocking collectives  9.67 us (35%)
  Pallas kernels  3.37 us (12%)
  waiting for transfers between devices  1.81 us (6%)
  between operations  0.69 us (2%)
    all_gather x1, blocking collectives, shards(): two = lax.all_gather(second, axes, axis_index_groups=groups)  7.37 us
    ppermute x1, starting transfers between devices, shards(): one = lax.ppermute(first, axes, swaps + [(b, a) for a, b in swaps])  6.76 us
    ppermute x1, starting transfers between devices, shards(): came = lax.ppermute(mine, 'span', chips + [(b, a) for a, b in chips])  5.29 us
    pallas_call x3, Pallas kernels, call(): pl.pallas_call(kernel, out_shape=[jax.ShapeDtypeStruct(shape, jnp.float32...  3.37 us
    all_gather x1, blocking collectives, shards(): both = lax.all_gather(own, 'span', axis_index_groups=cores)  2.3 us
    ppermute x1, waiting for transfers between devices, shards(): came = lax.ppermute(mine, 'span', chips + [(b, a) for a, b in chips])  1.81 us
  transfers between devices with their start and end apart: 2, of which 1 were waited for; matrix products, arithmetic and copies ran while one was open for 0% of the time, Pallas kernels for 0%

profile of v10, /device:TPU:384, one launch (start us, length us, event | category | flops | bytes accessed | tf_op | source)
XLA Modules:
  0.0 27.6 jit_solution(11931271574644962436)
XLA Ops:
  0.6 1.2 %shard_map.68 = (f32[21,4,8,128]{3,2,1,0:T(8,128)S(1)}, f32[31,8,128]{2,1,0:T(8,128)S(1)}) custom-call(f32[19,4,8,128]{3,2,1,0:T(8,128)} %f_ref.1, f32[4,8,128]{2,1,0:T(8,128)} %porosity_hbm.1, f32[4,8,128]{2,1,0:T(8,128)} %weight_hbm.1, s32[4,8,128]{2,1,0:T(8,128)} %solid_ref.1, s32[4,8,128]{2,1,0:T(8,128)} %surface_ref.1), custom_call_target="tpu_custom_call" | custom-call | tf_op jit(solution)/shard_map/pallas_call | solution.py:584
  1.8 5.3 %collective-permute-start = (f32[31,8,128]{2,1,0:T(8,128)S(1)}, f32[31,8,128]{2,1,0:T(8,128)S(1)}, u32[]{:S(2)}, u32[]{:S(2)}) collective-permute-start(f32[31,8,128]{2,1,0:T(8,128)S(1)} %get-tuple-element.10), channel_id=1, source_target_pairs={{1,2},{3,4},{5,6},{7,8},{9,10},{11,12},{13,14},{15,0},{2,1},{4,3},... | collective-permute-start | bytes 380936 | tf_op jit(solution)/shard_map/ppermute | solution.py:612
  7.1 2.3 %all-gather = f32[42,4,8,128]{3,2,1,0:T(8,128)S(1)} all-gather(f32[21,4,8,128]{3,2,1,0:T(8,128)S(1)} %get-tuple-element.9.own_ref), channel_id=2, replica_groups={{0,1},{2,3},{4,5},{6,7},{8,9},{10,11},{12,13},{14,15},{16,17},{18,19},{..., dimensions={0}, use_global_device_ids=true | all-gather | bytes 1032192 | tf_op jit(solution)/shard_map/all_gather | solution.py:613
  9.4 1.8 %collective-permute-done.half_ref = f32[31,8,128]{2,1,0:T(8,128)S(1)} collective-permute-done((f32[31,8,128]{2,1,0:T(8,128)S(1)}, f32[31,8,128]{2,1,0:T(8,128)S(1)}, u32[]{:S(2)}, u32[]{:S(2)}) %collective-permute-start) | collective-permute-done | bytes 127008 | tf_op jit(solution)/shard_map/ppermute | solution.py:612
  11.2 0.4 %shard_map.69 = (f32[21,4,8,128]{3,2,1,0:T(8,128)S(1)}, f32[19,2,2,8,128]{4,3,2,1,0:T(8,128)S(1)}, f32[19,2,2,8,128]{4,3,2,1,0:T(8,128)S(1)}, f32[37,8,128]{2,1,0:T(8,128)S(1)}, f32[37,8,128]{2,1,0:T(8,128)S(1)}) custom-call(f32[21,4,8,128]{3,2,1,0:T(8,128)S(1)} %get-tuple-element.9.own_ref, f32[2,21,4,8,128]{4,3,2,1,0:T(8,128)S(1)} %bitcast.2, ...), custom_call_target="tpu_custom_call" | custom-call | tf_op jit(solution)/shard_map/pallas_call | solution.py:584
  11.7 0.0 copy-start
  11.7 6.8 %collective-permute-start.1 = (f32[37,8,128]{2,1,0:T(8,128)S(1)}, f32[37,8,128]{2,1,0:T(8,128)S(1)}, u32[]{:S(2)}, u32[]{:S(2)}) collective-permute-start(f32[37,8,128]{2,1,0:T(8,128)S(1)} %get-tuple-element.14), channel_id=1, source_target_pairs={{16,32},{48,64},{80,96},{112,128},{144,160},{176,192},{208,224},{2... | collective-permute-start | bytes 454664 | tf_op jit(solution)/shard_map/ppermute | solution.py:631
  18.5 0.0 copy-start.1
  18.5 0.0 copy-start.2
  18.5 7.4 %all-gather.1 = f32[74,8,128]{2,1,0:T(8,128)S(1)} all-gather(f32[37,8,128]{2,1,0:T(8,128)S(1)} %get-tuple-element.15), channel_id=3, replica_groups={{0,16},{32,48},{64,80},{96,112},{128,144},{160,176},{192,208},{224,240}..., dimensions={0}, use_global_device_ids=true | all-gather | bytes 454656 | tf_op jit(solution)/shard_map/all_gather | solution.py:632
  25.8 0.0 collective-permute-done.1.one_ref
  25.8 0.0 copy-done
  25.9 0.0 copy-done.1
  25.9 0.0 copy-done.2
  25.9 1.7 %shard_map.70 = (f32[19,4,8,128]{3,2,1,0:T(8,128)}, f32[4,8,128]{2,1,0:T(8,128)}) custom-call(f32[19,4,8,128]{3,2,1,0:T(8,128)S(1)} %copy-done, s32[4,8,128]{2,1,0:T(8,128)S(1)} %copy-done.1, s32[4,8,128]{2,1,0:T(8,128)S(1)} %copy-done.2, f32[21,4,8,128]{3,2,1,0:T(8,128)S(1)} %get-tuple-element.9.own_ref, f32[21,4,8,128]{3,2,1,0:T(8,128)S(1)} %get-tuple-element.11.side_ref, ...), custom_call_target="tpu_custom_call" | custom-call | tf_op jit(solution)/shard_map/pallas_call | solution.py:584
Async XLA Ops:
  1.8 9.4 %collective-permute-start = (f32[31,8,128]{2,1,0:T(8,128)S(1)}, f32[31,8,128]{2,1,0:T(8,128)S(1)}, u32[]{:S(2)}, u32[]{:S(2)}) collective-permute-start(f32[31,8,128]{2,1,0:T(8,128)S(1)} %get-tuple-element.10), channel_id=1, source_target_pairs={{1,2},{3,4},{5,6},{7,8},{9,10},{11,12},{13,14},{15,0},{2,1},{4,3},... | collective-permute-start | bytes 380936 | tf_op jit(solution)/shard_map/ppermute | solution.py:612
  11.7 14.2 %copy-start = (f32[19,4,8,128]{3,2,1,0:T(8,128)S(1)}, f32[19,4,8,128]{3,2,1,0:T(8,128)}, u32[]{:S(2)}) copy-start(f32[19,4,8,128]{3,2,1,0:T(8,128)} %f_ref.1) | copy-start | bytes 933892
  11.7 14.2 %collective-permute-start.1 = (f32[37,8,128]{2,1,0:T(8,128)S(1)}, f32[37,8,128]{2,1,0:T(8,128)S(1)}, u32[]{:S(2)}, u32[]{:S(2)}) collective-permute-start(f32[37,8,128]{2,1,0:T(8,128)S(1)} %get-tuple-element.14), channel_id=1, source_target_pairs={{16,32},{48,64},{80,96},{112,128},{144,160},{176,192},{208,224},{2... | collective-permute-start | bytes 454664 | tf_op jit(solution)/shard_map/ppermute | solution.py:631
  18.5 7.4 %copy-start.1 = (s32[4,8,128]{2,1,0:T(8,128)S(1)}, s32[4,8,128]{2,1,0:T(8,128)}, u32[]{:S(2)}) copy-start(s32[4,8,128]{2,1,0:T(8,128)} %solid_ref.1) | copy-start | bytes 49156
  18.5 7.4 %copy-start.2 = (s32[4,8,128]{2,1,0:T(8,128)S(1)}, s32[4,8,128]{2,1,0:T(8,128)}, u32[]{:S(2)}) copy-start(s32[4,8,128]{2,1,0:T(8,128)} %surface_ref.1) | copy-start | bytes 49156
